TPU v7x, 32 devices: a whole 2x2x4 slice. The times are simulated.
32 devices in a mesh: box: 8 (over z, y), level: 4 (over x, core).
Axes of the slice: x: 2, y: 2, z: 4, core: 2. Of those that a mesh axis runs over, the one named last changes fastest.
Arguments:
- rhs_field: float32 [4, 128, 128], P(None, 'box'), may hold values from -6 to 6
- self_coef: float32 [128, 128], P('box'), may hold values from 2 to 4
- expand: bfloat16 [128, 256, 128], P('box'), may hold values from -0.5 to 0.5
- near_ops: bfloat16 [26, 128, 128], replicated, may hold values from -0.109375 to 0.109375
- class_ops: bfloat16 [8, 256, 256], P('box', 'level'), may hold values from -0.1875 to 0.1875
- near_src: int32 [128, 26], P('box'), may hold values from 0 to 47
- send_rows: int32 [8, 8, 2], P('box'), may hold values from 0 to 15
- list_slot: int32 [128, 4], P('box'), may hold values from 0 to 15
- list_class: int32 [128, 4], P('box'), may hold values from 0 to 7, all different within a row
Outputs:
- solution: float32 [4, 128, 128], P(None, 'box')
Inputs may be any that keep to these rules, and one draw needn't show every extreme that they name: `near_src`: the near-field neighbours of a box lie among the boxes of the index of box before it, its own and the one after it, counted in that order. `send_rows`: each entry is a box of the sending index. `list_slot`: entry q * 2 + j names the j-th row sent by index q of box. `list_class`: the classes of one box's list are distinct.
All inputs are finite; a program needn't handle non-finite values.
Results may differ from a plain program's by a relative error of at most 0.004.
Values may be sent and summed in bfloat16 or wider, within the bound.
No kernel may reach another device: no remote copies, remote signals or barrier semaphores. Data moves between devices by JAX's collectives and lax.ppermute only.
A program may use at most 64 MiB of HBM per device.

v0:
```python
import math

import jax
import jax.numpy as jnp
from jax import lax
from jax.sharding import PartitionSpec as P


def extended_2(block, sides, width):
    for axis, dim in sides:
        count = lax.axis_size(axis)
        forward = [(i, i + 1) for i in range(count - 1)]
        backward = [(target, source) for source, target in forward]
        low = lax.ppermute(
            lax.slice_in_dim(block, block.shape[dim] - width, None, axis=dim), axis, forward
        )
        high = lax.ppermute(lax.slice_in_dim(block, 0, width, axis=dim), axis, backward)
        block = jnp.concatenate([low, block, high], axis=dim)
    return block


def slot_table(list_slot, list_class, classes):
    labels = jnp.arange(classes, dtype=jnp.int32)
    matches = list_class[:, :, None] == labels[None, None, :]
    return jnp.sum(jnp.where(matches, list_slot[:, :, None] + 1, 0), axis=1) - 1


def apply_classes(totals, operators, offset, table, received):
    count = operators.shape[0]
    picked = lax.dynamic_slice_in_dim(table, offset, count, 1)
    sources = jnp.where(
        (picked >= 0)[:, :, None, None],
        received[jnp.maximum(picked, 0)],
        jnp.zeros((), received.dtype),
    )
    return totals + jnp.einsum(
        "cqp,tcrp->trq", operators, sources, preferred_element_type=jnp.float32
    )


def fold_classes(totals, pieces, offset, table, received):
    count = pieces.shape[0]
    stride = math.gcd(count, 16)
    if stride == count:
        return apply_classes(totals, pieces, offset, table, received)

    def step_once(number, current):
        operators = lax.dynamic_slice_in_dim(pieces, number * stride, stride, 0)
        return apply_classes(current, operators, offset + number * stride, table, received)

    return lax.fori_loop(0, count // stride, step_once, totals)


def inner(first, second):
    return jnp.sum(first * second, axis=(1, 2))


def spread(values, field):
    return values[:, None, None] * field


def per_device(
    rhs_field, self_coef, expand, near_ops, class_ops, near_src, send_rows, list_slot, list_class
):
    boxes = expand.shape[0]
    band = class_ops.shape[1]
    classes = class_ops.shape[0] * lax.axis_size("box")
    table = slot_table(list_slot, list_class, classes)
    level_index = lax.axis_index("level")
    cached = lax.all_gather(class_ops, "box", axis=0, tiled=True)

    def apply_matrix(field):
        field_half = field.astype(jnp.bfloat16)
        multipoles = jnp.einsum(
            "tpk,rtk->trp", expand, field_half, preferred_element_type=jnp.float32
        ).astype(jnp.bfloat16)
        outgoing = multipoles[send_rows[0]]
        received = lax.all_to_all(outgoing, "box", split_axis=0, concat_axis=0, tiled=True)
        received = received.reshape((-1,) + received.shape[2:])
        extended = extended_2(field_half, (("box", 1),), boxes)
        neighbours = extended[:, near_src]
        near_part = jnp.einsum(
            "kij,rtkj->rti", near_ops, neighbours, preferred_element_type=jnp.float32
        )
        empty = jnp.zeros((boxes, field.shape[0], band), jnp.float32)
        local_full = fold_classes(empty, cached, 0, table, received)
        local_half = local_full.astype(jnp.bfloat16)
        expand_rows = lax.dynamic_slice_in_dim(expand, level_index * band, band, 1)
        partial_field = jnp.einsum(
            "tqk,trq->rtk", expand_rows, local_half, preferred_element_type=jnp.float32
        )
        far_part = lax.psum(partial_field.astype(jnp.bfloat16), "level").astype(jnp.float32)
        return self_coef[None] * field + near_part + far_part

    def orthogonalize(basis, image):
        stacked = jnp.stack([inner(vector, image) for vector in basis])
        coeffs = lax.psum(stacked, "box")
        for position in range(len(basis)):
            image = image - spread(coeffs[position], basis[position])
        height = jnp.sqrt(lax.psum(inner(image, image), "box"))
        return (coeffs, height, image / height[:, None, None])

    beta = jnp.sqrt(lax.psum(inner(rhs_field, rhs_field), "box"))
    first = rhs_field / beta[:, None, None]
    coeffs_one, h_two_one, second = orthogonalize([first], apply_matrix(first))
    coeffs_two, h_three_two, unused_next = orthogonalize([first, second], apply_matrix(second))
    h_one_one = coeffs_one[0]
    h_one_two = coeffs_two[0]
    h_two_two = coeffs_two[1]
    gram_aa = h_one_one * h_one_one + h_two_one * h_two_one
    gram_ab = h_one_one * h_one_two + h_two_one * h_two_two
    gram_bb = h_one_two * h_one_two + h_two_two * h_two_two + h_three_two * h_three_two
    right_a = beta * h_one_one
    right_b = beta * h_one_two
    determinant = gram_aa * gram_bb - gram_ab * gram_ab
    coef_a = (gram_bb * right_a - gram_ab * right_b) / determinant
    coef_b = (gram_aa * right_b - gram_ab * right_a) / determinant
    return spread(coef_a, first) + spread(coef_b, second)


def solution(mesh):
    return jax.shard_map(
        per_device,
        mesh=mesh,
        in_specs=(
            P(None, "box", None),
            P("box", None),
            P("box", None, None),
            P(),
            P("box", "level", None),
            P("box", None),
            P("box", None, None),
            P("box", None),
            P("box", None),
        ),
        out_specs=P(None, "box", None),
        check_vma=False,
    )
```

profile of v0, /device:TPU:0, one launch (start us, length us, event | category | flops | bytes accessed | tf_op | source)
XLA Modules:
  0.0 188.9 jit_solution(552104534874354420)
XLA Ops:
  0.0 1.0 multiply_reduce_fusion.5
  1.0 23.1 %psum.49 = f32[4]{0:T(128)S(1)} all-reduce(f32[4]{0:T(128)S(1)} %multiply_reduce_fusion.5), channel_id=1, replica_groups=mesh['box'=8,'level'=4] {'box'}, use_global_device_ids=true, to_apply=%region_1.2 | all-reduce | flops 4 | bytes 32 | tf_op jit(solution)/shard_map/psum | solution.py:103
  24.2 1.3 collective-permute-start.1
  25.5 4.5 %collective-permute-start = (bf16[4,16,128]{2,1,0:T(8,128)(2,1)S(1)}, bf16[4,16,128]{2,1,0:T(8,128)(2,1)S(1)}, u32[]{:S(2)}, u32[]{:S(2)}) collective-permute-start(bf16[4,16,128]{2,1,0:T(8,128)(2,1)S(1)} %fusion.26), channel_id=1, source_target_pairs={{0,4},{4,8},{8,12},{12,16},{16,20},{20,24},{24,28},{1,5},{5,9},{9,... | collective-permute-start | bytes 49160 | tf_op jit(solution)/shard_map/ppermute | solution.py:14
  30.6 1.2 gather_fusion.1
  31.8 3.5 %all-to-all-start = ((bf16[8,2,4,256]{3,2,1,0:T(4,128)(2,1)}), bf16[8,2,4,256]{3,2,1,0:T(4,128)(2,1)S(1)}, u32[]{:S(2)}, u32[]{:S(2)}) async-start(bf16[8,2,4,256]{3,2,1,0:T(4,128)(2,1)} %bitcast.6), calls=%async_computation | async-start | bytes 65536 | tf_op jit(solution)/shard_map/all_to_all | solution.py:78
  35.3 0.7 copy-done.7
  36.0 31.2 %all_gather.3 = bf16[8,64,256]{2,1,0:T(8,128)(2,1)S(1)} all-gather(bf16[1,64,256]{2,1,0:T(8,128)(2,1)S(1)} %copy-done.4), channel_id=1, replica_groups=mesh['box'=8,'level'=4] {'box'}, dimensions={0}, use_global_device_ids=true | all-gather | bytes 294912 | tf_op jit(solution)/shard_map/all_gather | solution.py:70
  68.3 2.2 %gather_fusion = bf16[416,4,128]{2,1,0:T(4,128)(2,1)S(1)} fusion(bf16[4,48,128]{2,0,1:T(4,128)(2,1)S(1)} %copy.76, s32[1024]{0:T(1024)S(1)} %pad_clamp_fusion.2), kind=kCustom, calls=%fused_computation | custom fusion | bytes 853632 | tf_op jit(solution)/shard_map/gather | solution.py:81
  70.5 0.8 gather_fusion.2
  71.9 10.1 %psum.50 = bf16[4,16,128]{2,1,0:T(8,128)(2,1)S(1)} all-reduce(bf16[4,16,128]{2,1,0:T(8,128)(2,1)S(1)} %bitcast.94), channel_id=1, replica_groups=mesh['box'=8,'level'=4] {'level'}, use_global_device_ids=true, to_apply=%region_3.4 | all-reduce | flops 8192 | bytes 32768 | tf_op jit(solution)/shard_map/psum | solution.py:92
  82.5 21.4 %psum.51 = f32[4]{0:T(128)S(1)} all-reduce(f32[4]{0:T(128)S(1)} %get-tuple-element.13), channel_id=1, replica_groups=mesh['box'=8,'level'=4] {'box'}, use_global_device_ids=true, to_apply=%region_5.6 | all-reduce | flops 4 | bytes 32 | tf_op jit(solution)/shard_map/psum | solution.py:97
  104.1 17.1 %psum.52 = f32[4]{0:T(128)S(1)} all-reduce(f32[4]{0:T(128)S(1)} %multiply_reduce_fusion.3), channel_id=1, replica_groups=mesh['box'=8,'level'=4] {'box'}, use_global_device_ids=true, to_apply=%region_7.8 | all-reduce | flops 4 | bytes 32 | tf_op jit(solution)/shard_map/psum | solution.py:100
  121.4 1.3 collective-permute-start.3
  122.7 4.5 %collective-permute-start.2 = (bf16[4,16,128]{2,1,0:T(8,128)(2,1)S(1)}, bf16[4,16,128]{2,1,0:T(8,128)(2,1)S(1)}, u32[]{:S(2)}, u32[]{:S(2)}) collective-permute-start(bf16[4,16,128]{2,1,0:T(8,128)(2,1)S(1)} %get-tuple-element.7), channel_id=1, source_target_pairs={{0,4},{4,8},{8,12},{12,16},{16,20},{20,24},{24,28},{1,5},{5,9},{9,... | collective-permute-start | bytes 49160 | tf_op jit(solution)/shard_map/ppermute | solution.py:14
  127.6 1.2 gather_fusion.4
  128.8 4.2 %all-to-all-start.1 = ((bf16[8,2,4,256]{3,2,1,0:T(4,128)(2,1)}), bf16[8,2,4,256]{3,2,1,0:T(4,128)(2,1)S(1)}, u32[]{:S(2)}, u32[]{:S(2)}) async-start(bf16[8,2,4,256]{3,2,1,0:T(4,128)(2,1)} %bitcast.17), calls=%async_computation.1 | async-start | bytes 65536 | tf_op jit(solution)/shard_map/all_to_all | solution.py:78
  133.1 2.2 %gather_fusion.3 = bf16[416,4,128]{2,1,0:T(4,128)(2,1)S(1)} fusion(bf16[4,48,128]{2,0,1:T(4,128)(2,1)S(1)} %copy.86, s32[1024]{0:T(1024)S(1)} %pad_clamp_fusion.2), kind=kCustom, calls=%fused_computation.3 | custom fusion | bytes 853632 | tf_op jit(solution)/shard_map/gather | solution.py:81
  135.3 4.4 %all-to-all-done.1 = bf16[8,2,4,256]{3,2,1,0:T(4,128)(2,1)S(1)} async-done(((bf16[8,2,4,256]{3,2,1,0:T(4,128)(2,1)}), bf16[8,2,4,256]{3,2,1,0:T(4,128)(2,1)S(1)}, u32[]{:S(2)}, u32[]{:S(2)}) %all-to-all-start.1) | async-done | bytes 32800 | tf_op jit(solution)/shard_map/all_to_all | solution.py:78
  139.7 0.8 gather_fusion.5
  141.0 10.1 %psum.53 = bf16[4,16,128]{2,1,0:T(8,128)(2,1)S(1)} all-reduce(bf16[4,16,128]{2,1,0:T(8,128)(2,1)S(1)} %bitcast.95), channel_id=1, replica_groups=mesh['box'=8,'level'=4] {'level'}, use_global_device_ids=true, to_apply=%region_8.9 | all-reduce | flops 8192 | bytes 32768 | tf_op jit(solution)/shard_map/psum | solution.py:92
  151.7 17.8 %psum.54 = f32[2,4]{1,0:T(2,128)S(1)} all-reduce(f32[2,4]{1,0:T(2,128)S(1)} %pad_maximum_fusion.2), channel_id=1, replica_groups=mesh['box'=8,'level'=4] {'box'}, use_global_device_ids=true, to_apply=%region_11.12 | all-reduce | flops 8 | bytes 64 | tf_op jit(solution)/shard_map/psum | solution.py:97
  169.7 18.4 %psum.55 = f32[4]{0:T(128)S(1)} all-reduce(f32[4]{0:T(128)S(1)} %multiply_reduce_fusion), channel_id=1, replica_groups=mesh['box'=8,'level'=4] {'box'}, use_global_device_ids=true, to_apply=%region_13.14 | all-reduce | flops 4 | bytes 32 | tf_op jit(solution)/shard_map/psum | solution.py:100
  188.2 0.7 multiply_add_fusion
  (62 shorter events, 4.7 us)
Async XLA Ops:
  0.0 30.0 %copy-start = (bf16[16,256,128]{2,1,0:T(8,128)(2,1)S(1)}, bf16[16,256,128]{2,1,0:T(8,128)(2,1)}, u32[]{:S(2)}) copy-start(bf16[16,256,128]{2,1,0:T(8,128)(2,1)} %param.11) | copy-start | bytes 3145732
  0.0 24.1 %copy-start.2 = (f32[4,16,128]{2,1,0:T(8,128)S(1)}, f32[4,16,128]{2,1,0:T(8,128)}, u32[]{:S(2)}) copy-start(f32[4,16,128]{2,1,0:T(8,128)} %param.9) | copy-start | bytes 98308
  24.2 6.3 %copy-start.8 = (s32[1,8,2]{1,2,0:T(2,128)S(1)}, s32[1,8,2]{1,2,0:T(2,128)}, u32[]{:S(2)}) copy-start(s32[1,8,2]{1,2,0:T(2,128)} %param.15) | copy-start | bytes 196
  24.2 44.0 %collective-permute-start.1 = (bf16[4,16,128]{2,1,0:T(8,128)(2,1)S(1)}, bf16[4,16,128]{2,1,0:T(8,128)(2,1)S(1)}, u32[]{:S(2)}, u32[]{:S(2)}) collective-permute-start(bf16[4,16,128]{2,1,0:T(8,128)(2,1)S(1)} %fusion.26), channel_id=1, source_target_pairs={{4,0},{8,4},{12,8},{16,12},{20,16},{24,20},{28,24},{5,1},{9,5},{13... | collective-permute-start | bytes 49160 | tf_op jit(solution)/shard_map/ppermute | solution.py:17
  25.5 42.8 %collective-permute-start = (bf16[4,16,128]{2,1,0:T(8,128)(2,1)S(1)}, bf16[4,16,128]{2,1,0:T(8,128)(2,1)S(1)}, u32[]{:S(2)}, u32[]{:S(2)}) collective-permute-start(bf16[4,16,128]{2,1,0:T(8,128)(2,1)S(1)} %fusion.26), channel_id=1, source_target_pairs={{0,4},{4,8},{8,12},{12,16},{16,20},{20,24},{24,28},{1,5},{5,9},{9,... | collective-permute-start | bytes 49160 | tf_op jit(solution)/shard_map/ppermute | solution.py:14
  31.8 3.5 %copy-start.6 = (s32[16,4]{0,1:T(4,128)S(1)}, s32[16,4]{0,1:T(4,128)}, u32[]{:S(2)}) copy-start(s32[16,4]{0,1:T(4,128)} %param.16) | copy-start | bytes 772
  31.8 4.2 %copy-start.4 = (bf16[1,64,256]{2,1,0:T(8,128)(2,1)S(1)}, bf16[1,64,256]{2,1,0:T(8,128)(2,1)}, u32[]{:S(2)}) copy-start(bf16[1,64,256]{2,1,0:T(8,128)(2,1)} %param.13) | copy-start | bytes 98308
  31.8 38.7 %all-to-all-start = ((bf16[8,2,4,256]{3,2,1,0:T(4,128)(2,1)}), bf16[8,2,4,256]{3,2,1,0:T(4,128)(2,1)S(1)}, u32[]{:S(2)}, u32[]{:S(2)}) async-start(bf16[8,2,4,256]{3,2,1,0:T(4,128)(2,1)} %bitcast.6), calls=%async_computation | async-start | bytes 65536 | tf_op jit(solution)/shard_map/all_to_all | solution.py:78
  35.3 0.7 copy-start.7
  67.3 0.7 copy-start.5
  71.3 10.7 %copy-start.1 = (bf16[26,128,128]{2,1,0:T(8,128)(2,1)S(1)}, bf16[26,128,128]{2,1,0:T(8,128)(2,1)}, u32[]{:S(2)}) copy-start(bf16[26,128,128]{2,1,0:T(8,128)(2,1)} %param.12) | copy-start | bytes 2555908
  71.9 10.1 %copy-start.3 = (f32[16,128]{1,0:T(8,128)S(1)}, f32[16,128]{1,0:T(8,128)}, u32[]{:S(2)}) copy-start(f32[16,128]{1,0:T(8,128)} %param.10) | copy-start | bytes 24580
  121.4 11.6 %collective-permute-start.3 = (bf16[4,16,128]{2,1,0:T(8,128)(2,1)S(1)}, bf16[4,16,128]{2,1,0:T(8,128)(2,1)S(1)}, u32[]{:S(2)}, u32[]{:S(2)}) collective-permute-start(bf16[4,16,128]{2,1,0:T(8,128)(2,1)S(1)} %get-tuple-element.7), channel_id=1, source_target_pairs={{4,0},{8,4},{12,8},{16,12},{20,16},{24,20},{28,24},{5,1},{9,5},{13... | collective-permute-start | bytes 49160 | tf_op jit(solution)/shard_map/ppermute | solution.py:17
  122.7 10.3 %collective-permute-start.2 = (bf16[4,16,128]{2,1,0:T(8,128)(2,1)S(1)}, bf16[4,16,128]{2,1,0:T(8,128)(2,1)S(1)}, u32[]{:S(2)}, u32[]{:S(2)}) collective-permute-start(bf16[4,16,128]{2,1,0:T(8,128)(2,1)S(1)} %get-tuple-element.7), channel_id=1, source_target_pairs={{0,4},{4,8},{8,12},{12,16},{16,20},{20,24},{24,28},{1,5},{5,9},{9,... | collective-permute-start | bytes 49160 | tf_op jit(solution)/shard_map/ppermute | solution.py:14
  128.8 10.9 %all-to-all-start.1 = ((bf16[8,2,4,256]{3,2,1,0:T(4,128)(2,1)}), bf16[8,2,4,256]{3,2,1,0:T(4,128)(2,1)S(1)}, u32[]{:S(2)}, u32[]{:S(2)}) async-start(bf16[8,2,4,256]{3,2,1,0:T(4,128)(2,1)} %bitcast.17), calls=%async_computation.1 | async-start | bytes 65536 | tf_op jit(solution)/shard_map/all_to_all | solution.py:78
where the time goes:
time: 189 us
  blocking collectives  149 us (79%)
  starting transfers between devices  19.3 us (10%)
  local copies, waits for them, and re-layouts  10.3 us (5%)
  waiting for transfers between devices  4.44 us (2%)
  matrix products  2.61 us (1%)
  other arithmetic  2.5 us (1%)
    psum x2, blocking collectives, orthogonalize(): coeffs = lax.psum(stacked, 'box')  39.2 us
    psum x2, blocking collectives, orthogonalize(): height = jnp.sqrt(lax.psum(inner(image, image), 'box'))  35.6 us
    all_gather x1, blocking collectives, per_device(): cached = lax.all_gather(class_ops, 'box', axis=0, tiled=True)  31.2 us
    psum x1, blocking collectives, per_device(): beta = jnp.sqrt(lax.psum(inner(rhs_field, rhs_field), 'box'))  23.1 us
    psum x2, blocking collectives, apply_matrix(): lax.psum(partial_field.astype(jnp.bfloat16), 'level').astype(jnp.float32)  20.2 us
    ppermute x2, starting transfers between devices, extended_2(): lax.ppermute(lax.slice_in_dim(block, block.shape[dim] - width, None, axis...  9.09 us
    all_to_all x2, starting transfers between devices, apply_matrix(): lax.all_to_all(outgoing, 'box', split_axis=0, concat_axis=0, tiled=True)  7.66 us
    all_to_all x2, waiting for transfers between devices, apply_matrix(): lax.all_to_all(outgoing, 'box', split_axis=0, concat_axis=0, tiled=True)  4.43 us
  transfers between devices with their start and end apart: 6, of which 1 were waited for; matrix products, arithmetic and copies ran while one was open for 4% of the time, Pallas kernels for 0%

commit v1 on v0

v1 whole, which is shorter than its diff:
```python
import functools

import jax
import jax.numpy as jnp
from jax import lax
from jax.experimental import pallas as pl
from jax.experimental.pallas import tpu as pltpu
from jax.sharding import Mesh, PartitionSpec as P

SHIFT = 3.0
LANES = 128
HALF = jnp.bfloat16
FULL = jnp.float32
LIMIT = 48 * 1024 * 1024


def each(count, body):
    if count <= 32:
        for number in range(count):
            body(number)
    else:
        lax.fori_loop(0, count, lambda number, state: (body(number), state)[1], 0)


def fold(count, body, state):
    if count <= 32:
        for number in range(count):
            state = body(number, state)
        return state
    return lax.fori_loop(0, count, body, state)


def dot_nt(left, right):
    return lax.dot_general(left, right, (((1,), (1,)), ((), ())), preferred_element_type=FULL)


def dot_nn(left, right):
    return lax.dot_general(left, right, (((1,), (0,)), ((), ())), preferred_element_type=FULL)


def own_rows(values, result, box, boxes):
    row = lax.broadcasted_iota(jnp.int32, result.shape, 0)
    return jnp.where(row % boxes == box, values, result)


def multipoles_of(field, expand_ref):
    boxes, terms, _ = expand_ref.shape
    result = jnp.zeros((field.shape[0], terms), FULL)
    for box in range(boxes):
        result = own_rows(dot_nt(field, expand_ref[box]), result, box, boxes)
    return result


def put_rows(multipoles, send_ref, rows_ref, picked_ref, boxes):
    rows_ref[...] = multipoles
    picked_ref[...] = jnp.zeros(picked_ref.shape, picked_ref.dtype)
    width, cap = multipoles.shape[0] // boxes, send_ref.shape[2]
    parts = multipoles.shape[1] // LANES

    def put(target):
        for turn in range(cap):
            row = send_ref[0, target, turn]
            for rhs in range(width):
                chosen = rows_ref[pl.ds(rhs * boxes + row, 1), :]
                for part in range(parts):
                    place = (part * width + rhs) * cap + turn
                    picked_ref[target, place : place + 1, :] = chosen[:, part * LANES : (part + 1) * LANES]

    each(send_ref.shape[1], put)


def far_of(local, expand_ref, offset):
    boxes, _, panels = expand_ref.shape
    result = jnp.zeros((local.shape[0], panels), FULL)
    for box in range(boxes):
        rows = expand_ref[box, pl.ds(offset, local.shape[1]), :]
        result = own_rows(dot_nn(local, rows), result, box, boxes)
    return result


def near_of(near_ref, source_ref, extended, boxes, width):
    classes = near_ref.shape[0]
    spots = lax.broadcasted_iota(jnp.int32, (boxes, extended.shape[0]), 1)
    chosen = [
        jnp.where(source_ref[:, number : number + 1] == spots, 1.0, 0.0).astype(HALF)
        for number in range(classes)
    ]
    picked = dot_nn(jnp.concatenate(chosen, axis=0), extended).astype(HALF)
    result = jnp.zeros((width * boxes, near_ref.shape[1]), FULL)
    for number in range(classes):
        rows = picked[number * boxes : (number + 1) * boxes]
        stacked = jnp.concatenate(
            [rows[:, rhs * LANES : (rhs + 1) * LANES] for rhs in range(width)], axis=0
        )
        result = result + dot_nt(stacked, near_ref[number])
    return result


def local_of(bands, slot_ref, class_ref, received, width, cap, offset, band):
    boxes = slot_ref.shape[0]
    area = received.shape[0] // bands[0].shape[0]
    slots = slot_ref[...]
    places = (slots // cap) * area + slots % cap
    labels = class_ref[...]
    parts = bands[0].shape[1] * LANES
    halves = 2
    spots = lax.broadcasted_iota(jnp.int32, (boxes, received.shape[0]), 1)

    def add(number, totals):
        place = jnp.max(jnp.where(labels == number, places + 1, 0), axis=1, keepdims=True) - 1
        totals = list(totals)
        for part in range(halves):
            stacked = []
            for rhs in range(width):
                shift = (part * width + rhs) * cap
                chosen = jnp.where((place >= 0) & (place + shift == spots), 1.0, 0.0).astype(HALF)
                stacked.append(dot_nn(chosen, received).astype(HALF))
            source = jnp.concatenate(stacked, axis=0)
            for which, ref in enumerate(bands):
                rows = ref[number, offset + part * band : offset + (part + 1) * band, :]
                totals[which] = totals[which] + dot_nt(source, rows)
        return tuple(totals)

    empty = tuple(jnp.zeros((width * boxes, band), FULL) for _ in bands)
    return fold(bands[0].shape[0], add, empty)


def extended_of(pieces, index, count, boxes):
    low = jnp.where(index > 0, pieces[0], jnp.zeros_like(pieces[0]))
    high = jnp.where(index < count - 1, pieces[2], jnp.zeros_like(pieces[2]))
    width = low.shape[0] // boxes
    columns = [
        jnp.concatenate([piece[rhs * boxes : (rhs + 1) * boxes] for piece in (low, pieces[1], high)], axis=0)
        for rhs in range(width)
    ]
    return jnp.concatenate(columns, axis=1).astype(HALF)


def paired(own, other, core):
    return jnp.where(core == 0, jnp.concatenate([own, other], axis=1), jnp.concatenate([other, own], axis=1))


def first_kernel(width, rhs_ref, expand_ref, class_ref, send_ref, out_ref, rows_ref, picked_ref):
    boxes, panels = expand_ref.shape[0], expand_ref.shape[2]
    core = lax.axis_index("core")
    field = rhs_ref[pl.ds(core * width, width)].reshape(width * boxes, panels).astype(HALF)
    band = class_ref.shape[1]
    put_rows(multipoles_of(field, expand_ref), send_ref, rows_ref, picked_ref, boxes)
    operators = jnp.concatenate([class_ref[0][:, :LANES], class_ref[0][:, LANES:]], axis=0)
    low = 2 * band
    high = low + width * boxes

    def put(target):
        out_ref[target, :low, :] = operators
        out_ref[target, low:high, :] = field
        out_ref[target, high:, :] = picked_ref[target].astype(HALF)

    each(out_ref.shape[0], put)


def second_kernel(
    width,
    own_ref,
    other_ref,
    rhs_ref,
    self_ref,
    expand_ref,
    near_ref,
    source_ref,
    slot_ref,
    class_ref,
    send_ref,
    out_ref,
    rows_ref,
    picked_ref,
):
    boxes, terms, panels = expand_ref.shape
    count = own_ref.shape[0]
    core, side, index = lax.axis_index("core"), lax.axis_index("side"), lax.axis_index("box")
    low = 2 * (terms // 4)
    high = low + width * boxes
    pieces = [
        own_ref[jnp.clip(index + step, 0, count - 1), low:high, :] for step in (-1, 0, 1)
    ]
    extended = extended_of(pieces, index, count, boxes)
    near = near_of(near_ref, source_ref, extended, boxes, width)
    area = own_ref.shape[1] - high
    received = own_ref[:, high:, :].reshape(count * area, LANES)
    own, other = local_of(
        (own_ref, other_ref), slot_ref, class_ref, received, width, send_ref.shape[2], 0, terms // 4
    )
    local = paired(own, other, core).astype(HALF)
    far = far_of(local, expand_ref, side * (terms // 2))
    field = rhs_ref[pl.ds(core * width, width)]
    diagonal = ((self_ref[...] - SHIFT)[None] * field).reshape(width * boxes, panels)
    image = far + jnp.where(side == 0, near + diagonal, 0.0)
    half = image.astype(HALF)
    put_rows(multipoles_of(half, expand_ref), send_ref, rows_ref, picked_ref, boxes)
    rows = width * boxes

    def put(target):
        block = picked_ref[target].astype(HALF)
        for part in range(2):
            out_ref[2 * target + part, :rows, :] = half
            out_ref[2 * target + part, rows:, :] = block

    each(count, put)


def third_kernel(
    width,
    own_ref,
    other_ref,
    parts_ref,
    self_ref,
    expand_ref,
    near_ref,
    source_ref,
    slot_ref,
    class_ref,
    send_ref,
    far_ref,
    rest_ref,
    field_ref,
):
    boxes, terms, panels = expand_ref.shape
    count = own_ref.shape[0]
    core, side, index = lax.axis_index("core"), lax.axis_index("side"), lax.axis_index("box")
    rows = width * boxes

    def joined(place):
        return parts_ref[2 * place, :rows, :].astype(FULL) + parts_ref[2 * place + 1, :rows, :].astype(FULL)

    pieces = [joined(jnp.clip(index + step, 0, count - 1)) for step in (-1, 0, 1)]
    extended = extended_of(pieces, index, count, boxes)
    near = near_of(near_ref, source_ref, extended, boxes, width)
    area = parts_ref.shape[1] - rows
    blocks = parts_ref[:, rows:, :].reshape(count, 2, area, LANES).astype(FULL)
    received = (blocks[:, 0] + blocks[:, 1]).astype(HALF).reshape(count * area, LANES)
    own, other = local_of(
        (own_ref, other_ref), slot_ref, class_ref, received, width, send_ref.shape[2], 0, terms // 4
    )
    local = paired(own, other, core).astype(HALF)
    far_ref[...] = far_of(local, expand_ref, side * (terms // 2))
    field = pieces[1]
    diagonal = ((self_ref[...] - SHIFT)[None] * field.reshape(width, boxes, panels)).reshape(rows, panels)
    rest_ref[...] = near + diagonal
    field_ref[...] = field


def fourth_kernel(width, rest_ref, far_ref, other_ref, field_ref, rhs_ref, out_ref):
    core = lax.axis_index("core")
    rows, panels = field_ref.shape
    boxes = rows // width
    last = rest_ref[...] + (far_ref[...] + other_ref[...])
    field = field_ref[...]
    right = rhs_ref[pl.ds(core * width, width)].reshape(rows, panels)
    spots = lax.broadcasted_iota(jnp.int32, (8, panels), 0)
    lanes = lax.broadcasted_iota(jnp.int32, (8, panels), 1)
    result = jnp.zeros((8, panels), FULL)
    pairs = ((right, right), (right, field), (field, field), (right, last), (field, last), (last, last))
    for number, (one, two) in enumerate(pairs):
        product = one * two
        for rhs in range(width):
            total = jnp.sum(product[rhs * boxes : (rhs + 1) * boxes])
            mine = (spots == number) & (lanes // (panels // width) == rhs)
            result = jnp.where(mine, total, result)

    def put(target):
        out_ref[target] = result

    each(out_ref.shape[0], put)


def last_kernel(width, sums_ref, field_ref, other_ref, rhs_ref, out_ref):
    core = lax.axis_index("core")
    rows, panels = field_ref.shape
    boxes = rows // width
    fields = (field_ref[...], other_ref[...])
    part = panels // width
    lanes = lax.broadcasted_iota(jnp.int32, (1, panels), 1)
    for group in range(2):
        total = fold(
            sums_ref.shape[0] // 2,
            lambda number, state: state + sums_ref[2 * number + group],
            jnp.zeros(sums_ref.shape[1:], FULL),
        )
        rr, ru, uu, rw, uw, ww = (total[number : number + 1] for number in range(6))
        slope = ru / rr
        norm = uu - slope * ru
        first_row = rw - slope * ru
        scale = lax.rsqrt(rr * norm)
        h11 = slope + SHIFT
        h21 = jnp.sqrt(norm / rr)
        h12 = first_row * scale
        h22 = (uw - slope * uu - slope * first_row) / norm
        image = (ww - 2.0 * slope * uw + slope * slope * uu) / norm
        gram_aa = h11 * h11 + h21 * h21
        gram_ab = h11 * h12 + h21 * (h22 + SHIFT)
        gram_bb = image + 2.0 * SHIFT * h22 + SHIFT * SHIFT
        beta = jnp.sqrt(rr)
        right_a, right_b = beta * h11, beta * h12
        determinant = gram_aa * gram_bb - gram_ab * gram_ab
        coef_a = (gram_bb * right_a - gram_ab * right_b) / determinant
        coef_b = (gram_aa * right_b - gram_ab * right_a) / determinant
        weight = coef_b * lax.rsqrt(norm)
        first = coef_a / beta - weight * slope
        chosen = jnp.where(core == group, fields[0], fields[1])
        for rhs in range(width):
            def wide(value):
                inside = jnp.where(lanes // part == rhs, value, 0.0)
                spread = inside
                for step in range(1, width):
                    spread = spread + pltpu.roll(inside, step * part, 1)
                return spread

            place = group * width + rhs
            out_ref[place] = wide(first) * rhs_ref[place] + wide(weight) * chosen[rhs * boxes : (rhs + 1) * boxes]


def call(kernel, outs, *args, scalars=(), scratch=()):
    vmem = pl.BlockSpec(memory_space=pltpu.VMEM)
    smem = pl.BlockSpec(memory_space=pltpu.SMEM)
    many = isinstance(outs, list)
    return pl.pallas_call(
        kernel,
        out_shape=outs,
        in_specs=[smem if number in scalars else vmem for number in range(len(args))],
        out_specs=[vmem] * len(outs) if many else vmem,
        scratch_shapes=list(scratch),
        compiler_params=pltpu.CompilerParams(vmem_limit_bytes=LIMIT),
    )(*args)


def per_device(
    rhs_field, self_coef, expand, near_ops, class_ops, near_src, send_rows, list_slot, list_class
):
    count = lax.axis_size("box")
    boxes, terms, panels = expand.shape
    width = rhs_field.shape[0] // 2
    rows = width * boxes
    band = class_ops.shape[1]
    cap = send_rows.shape[2]
    area = -(-(cap * width * (terms // LANES)) // 16) * 16
    scratch = [pltpu.VMEM((rows, terms), FULL), pltpu.VMEM((count, area, LANES), FULL)]
    swap = [(0, 1), (1, 0)]

    slots = call(
        functools.partial(first_kernel, width),
        jax.ShapeDtypeStruct((count, 2 * band + rows + area, LANES), HALF),
        rhs_field, expand, class_ops, send_rows,
        scalars=(3,), scratch=scratch,
    )
    own = lax.all_to_all(slots, "box", 0, 0, tiled=True)
    other = lax.ppermute(own, "core", swap)
    parts = call(
        functools.partial(second_kernel, width),
        jax.ShapeDtypeStruct((2 * count, rows + area, LANES), HALF),
        own, other, rhs_field, self_coef, expand, near_ops, near_src, list_slot, list_class, send_rows,
        scalars=(9,), scratch=scratch,
    )
    parts = lax.all_to_all(parts, ("box", "side"), 0, 0, tiled=True)
    block = jax.ShapeDtypeStruct((rows, panels), FULL)
    far, rest, field = call(
        functools.partial(third_kernel, width),
        [block, block, block],
        own, other, parts, self_coef, expand, near_ops, near_src, list_slot, list_class, send_rows,
        scalars=(9,),
    )
    far_other = lax.ppermute(far, "side", swap)
    field_other = lax.ppermute(field, "core", swap)
    sums = call(
        functools.partial(fourth_kernel, width),
        jax.ShapeDtypeStruct((2 * count, 8, panels), FULL),
        rest, far, far_other, field, rhs_field,
    )
    sums = lax.all_to_all(sums, ("box", "core"), 0, 0, tiled=True)
    return call(
        functools.partial(last_kernel, width),
        jax.ShapeDtypeStruct(rhs_field.shape, FULL),
        sums, field, field_other, rhs_field,
    )


def solution(mesh):
    count, levels = mesh.devices.shape
    finer = Mesh(mesh.devices.reshape(count, levels // 2, 2), ("box", "side", "core"))
    return jax.shard_map(
        per_device,
        mesh=finer,
        in_specs=(
            P(None, "box", None),
            P("box", None),
            P("box", None, None),
            P(),
            P("box", ("side", "core"), None),
            P("box", None),
            P("box", None, None),
            P("box", None),
            P("box", None),
        ),
        out_specs=P(None, "box", None),
        check_vma=False,
    )
```

time: 189 us -> 61.1 us (0.32)
  blocking collectives: 149 us -> 31.6 us
  starting transfers between devices: 19.3 us -> 4.79 us
  Pallas kernels: 0 us -> 9.6 us
  local copies, waits for them, and re-layouts: 10.3 us -> 3.69 us
  waiting for transfers between devices: 4.44 us -> 10.9 us
  matrix products: 2.61 us -> 0 us
  other arithmetic: 2.5 us -> 0 us
    psum x7 -> x0, blocking collectives: 118 us -> none  [the longest x2 39.2 us: orthogonalize(): coeffs = lax.psum(stacked, 'box')]
    all_to_all x0 -> x2, blocking collectives: none -> 31.6 us  [the longest x1 18.7 us: per_device(): own = lax.all_to_all(slots, 'box', 0, 0, tiled=True)]
    all_gather x1 -> x0, blocking collectives: 31.2 us -> none  [per_device(): cached = lax.all_gather(class_ops, 'box', axis=0, tiled=True)]
    ppermute x4 -> x3, starting transfers between devices: 11.7 us -> 1.3 us  [the longest x1 1.01 us: per_device(): far_other = lax.ppermute(far, 'side', swap)]
    pallas_call x0 -> x5, Pallas kernels: none -> 9.6 us  [call(): pl.pallas_call(kernel, out_shape=outs, in_specs=[smem if number in scalar...]
    gather x6 -> x0, local copies, waits for them, and re-layouts: 8.46 us -> none  [the longest x2 4.39 us: apply_matrix(): neighbours = extended[:, near_src]]
    ppermute x4 -> x3, waiting for transfers between devices: 0.01 us -> 5.25 us  [the longest x1 2.8 us: per_device(): far_other = lax.ppermute(far, 'side', swap)]
    all_to_all x2 -> x1, starting transfers between devices: 7.66 us -> 3.49 us  [per_device(): sums = lax.all_to_all(sums, ('box', 'core'), 0, 0, tiled=True)]
  transfers between devices with their start and end apart: 6 -> 4, of which waited for: 1 -> 4; matrix products, arithmetic and copies ran while one was open for 4% -> 0% of each run, Pallas kernels for 0% -> 0%
where the time goes in v1:
time: 61.1 us; the launch traced here: 60.6 us
  blocking collectives  31.6 us (52%)
  waiting for transfers between devices  10.9 us (18%)
  Pallas kernels  9.6 us (16%)
  starting transfers between devices  4.79 us (8%)
  local copies, waits for them, and re-layouts  3.69 us (6%)
    all_to_all x1, blocking collectives, per_device(): own = lax.all_to_all(slots, 'box', 0, 0, tiled=True)  18.7 us
    all_to_all x1, blocking collectives, per_device(): parts = lax.all_to_all(parts, ('box', 'side'), 0, 0, tiled=True)  12.9 us
    pallas_call x5, Pallas kernels, call(): pl.pallas_call(kernel, out_shape=outs, in_specs=[smem if number in scalar...  9.6 us
    all_to_all x1, waiting for transfers between devices, per_device(): sums = lax.all_to_all(sums, ('box', 'core'), 0, 0, tiled=True)  5.61 us
    unnamed x23, local copies, waits for them, and re-layouts  3.69 us
    all_to_all x1, starting transfers between devices, per_device(): sums = lax.all_to_all(sums, ('box', 'core'), 0, 0, tiled=True)  3.49 us
    ppermute x1, waiting for transfers between devices, per_device(): far_other = lax.ppermute(far, 'side', swap)  2.8 us
    ppermute x1, waiting for transfers between devices, per_device(): other = lax.ppermute(own, 'core', swap)  1.5 us
  transfers between devices with their start and end apart: 4, of which 4 were waited for; matrix products, arithmetic and copies ran while one was open for 0% of the time, Pallas kernels for 0%

profile of v1, /device:TPU:0, one launch (start us, length us, event | category | flops | bytes accessed | tf_op | source)
XLA Modules:
  0.0 60.6 jit_solution(16307771214148729427)
XLA Ops:
  0.0 0.8 %copy.10.send_ref = s32[1,8,2]{2,1,0:T(8,128)S(1)} copy(s32[1,8,2]{1,2,0:T(2,128)} %param.15) | data formatting | bytes 128 | tf_op args[6]
  0.8 1.2 %copy-done = bf16[16,256,128]{2,1,0:T(8,128)(2,1)S(1)} copy-done((bf16[16,256,128]{2,1,0:T(8,128)(2,1)S(1)}, bf16[16,256,128]{2,1,0:T(8,128)(2,1)}, u32[]{:S(2)}) %copy-start) | copy-done | bytes 1048600
  2.0 0.8 %copy-done.3 = f32[4,16,128]{2,1,0:T(8,128)S(1)} copy-done((f32[4,16,128]{2,1,0:T(8,128)S(1)}, f32[4,16,128]{2,1,0:T(8,128)}, u32[]{:S(2)}) %copy-start.3) | copy-done | bytes 32792
  2.7 0.8 %copy-done.7 = bf16[1,64,256]{2,1,0:T(8,128)(2,1)S(1)} copy-done((bf16[1,64,256]{2,1,0:T(8,128)(2,1)S(1)}, bf16[1,64,256]{2,1,0:T(8,128)(2,1)}, u32[]{:S(2)}) %copy-start.7) | copy-done | bytes 32792
  3.5 1.1 %shard_map.91 = bf16[8,176,128]{2,1,0:T(8,128)(2,1)S(1)} custom-call(f32[4,16,128]{2,1,0:T(8,128)S(1)} %copy-done.3, bf16[16,256,128]{2,1,0:T(8,128)(2,1)S(1)} %copy-done, bf16[1,64,256]{2,1,0:T(8,128)(2,1)S(1)} %copy-done.7, s32[1,8,2]{2,1,0:T(8,128)S(1)} %copy.10.send_ref), custom_call_target="tpu_custom_call" | custom-call | tf_op jit(solution)/shard_map/pallas_call | solution.py:325
  4.6 0.0 copy-start.8
  4.6 0.0 copy-start.9
  4.6 0.0 copy-start.4
  4.6 18.7 %all_to_all.15.own_ref = bf16[8,176,128]{2,1,0:T(8,128)(2,1)S(1)} all-to-all(bf16[8,176,128]{2,1,0:T(8,128)(2,1)S(1)} %shard_map.91), channel_id=1, replica_groups=mesh['box'=8,'side'=2,'core'=2] {'box'}, dimensions={0} | all-to-all | bytes 720896 | tf_op jit(solution)/shard_map/all_to_all | solution.py:354
  23.4 0.0 collective-permute-start
  23.4 0.1 copy.11.slot_ref
  23.4 0.1 copy.12.class_ref
  23.5 1.5 %collective-permute-done.other_ref = bf16[8,176,128]{2,1,0:T(8,128)(2,1)S(1)} collective-permute-done((bf16[8,176,128]{2,1,0:T(8,128)(2,1)S(1)}, bf16[8,176,128]{2,1,0:T(8,128)(2,1)S(1)}, u32[]{:S(2)}, u32[]{:S(2)}) %collective-permute-start) | collective-permute-done | bytes 360480 | tf_op jit(solution)/shard_map/ppermute | solution.py:355
  25.1 3.8 %shard_map.92 = bf16[16,48,128]{2,1,0:T(8,128)(2,1)S(1)} custom-call(bf16[8,176,128]{2,1,0:T(8,128)(2,1)S(1)} %all_to_all.15.own_ref, bf16[8,176,128]{2,1,0:T(8,128)(2,1)S(1)} %collective-permute-done.other_ref, f32[4,16,128]{2,1,0:T(8,128)S(1)} %copy-done.4, f32[16,128]{1,0:T(8,128)S(1)} %copy-done.5, bf16[16,256,128]{2,1,0:T(8,128)(2,1)S(1)} %copy-done.1, ...), custom_call_target="tpu_custom_call" | custom-call | tf_op jit(solution)/shard_map/pallas_call | solution.py:325
  28.8 12.9 %all_to_all.16.parts_ref = bf16[16,48,128]{2,1,0:T(8,128)(2,1)S(1)} all-to-all(bf16[16,48,128]{2,1,0:T(8,128)(2,1)S(1)} %shard_map.92), channel_id=1, replica_groups=mesh['box'=8,'side'=2,'core'=2] {'box','side'}, dimensions={0} | all-to-all | bytes 393216 | tf_op jit(solution)/shard_map/all_to_all | solution.py:362
  41.7 3.3 %shard_map.93 = (f32[32,128]{1,0:T(8,128)S(1)}, f32[32,128]{1,0:T(8,128)S(1)}, f32[32,128]{1,0:T(8,128)S(1)}) custom-call(bf16[8,176,128]{2,1,0:T(8,128)(2,1)S(1)} %all_to_all.15.own_ref, bf16[8,176,128]{2,1,0:T(8,128)(2,1)S(1)} %collective-permute-done.other_ref, bf16[16,48,128]{2,1,0:T(8,128)(2,1)S(1)} %all_to_all.16.parts_ref, f32[16,128]{1,0:T(8,128)S(1)} %copy-done.5, ...), custom_call_target="tpu_custom_call" | custom-call | tf_op jit(solution)/shard_map/pallas_call | solution.py:325
  45.0 1.0 %collective-permute-start.1 = (f32[32,128]{1,0:T(8,128)S(1)}, f32[32,128]{1,0:T(8,128)S(1)}, u32[]{:S(2)}, u32[]{:S(2)}) collective-permute-start(f32[32,128]{1,0:T(8,128)S(1)} %get-tuple-element.9.far_ref), channel_id=1, source_target_pairs={{0,2},{2,0},{1,3},{3,1},{4,6},{6,4},{5,7},{7,5},{8,10},{10,8},{9,1... | collective-permute-start | bytes 49160 | tf_op jit(solution)/shard_map/ppermute | solution.py:370
  46.0 2.8 %collective-permute-done.1.other_ref = f32[32,128]{1,0:T(8,128)S(1)} collective-permute-done((f32[32,128]{1,0:T(8,128)S(1)}, f32[32,128]{1,0:T(8,128)S(1)}, u32[]{:S(2)}, u32[]{:S(2)}) %collective-permute-start.1) | collective-permute-done | bytes 16416 | tf_op jit(solution)/shard_map/ppermute | solution.py:370
  48.8 0.8 %shard_map.94 = f32[16,8,128]{2,1,0:T(8,128)} custom-call(f32[32,128]{1,0:T(8,128)S(1)} %get-tuple-element.8.rest_ref, f32[32,128]{1,0:T(8,128)S(1)} %get-tuple-element.9.far_ref, f32[32,128]{1,0:T(8,128)S(1)} %collective-permute-done.1.other_ref, f32[32,128]{1,0:T(8,128)S(1)} %get-tuple-element.10.field_ref, f32[4,16,128]{2,1,0:T(8,128)S(1)} %copy-done.4), custom_call_target="tpu_custom_call" | custom-call | tf_op jit(solution)/shard_map/pallas_call | solution.py:325
  49.5 3.5 %all-to-all-start.2 = ((f32[16,8,128]{2,1,0:T(8,128)}), f32[16,8,128]{2,1,0:T(8,128)S(1)}, u32[]{:S(2)}, u32[]{:S(2)}) async-start(f32[16,8,128]{2,1,0:T(8,128)} %shard_map.94), calls=%async_computation.2 | async-start | bytes 131072 | tf_op jit(solution)/shard_map/all_to_all | solution.py:377
  53.0 0.3 collective-permute-start.2
  53.3 1.0 %collective-permute-done.2.other_ref = f32[32,128]{1,0:T(8,128)S(1)} collective-permute-done((f32[32,128]{1,0:T(8,128)S(1)}, f32[32,128]{1,0:T(8,128)S(1)}, u32[]{:S(2)}, u32[]{:S(2)}) %collective-permute-start.2) | collective-permute-done | bytes 16416 | tf_op jit(solution)/shard_map/ppermute | solution.py:371
  54.3 5.6 %all-to-all-done.2.sums_ref = f32[16,8,128]{2,1,0:T(8,128)S(1)} async-done(((f32[16,8,128]{2,1,0:T(8,128)}), f32[16,8,128]{2,1,0:T(8,128)S(1)}, u32[]{:S(2)}, u32[]{:S(2)}) %all-to-all-start.2) | async-done | bytes 65568 | tf_op jit(solution)/shard_map/all_to_all | solution.py:377
  59.9 0.7 %shard_map.95 = f32[4,16,128]{2,1,0:T(8,128)} custom-call(f32[16,8,128]{2,1,0:T(8,128)S(1)} %all-to-all-done.2.sums_ref, f32[32,128]{1,0:T(8,128)S(1)} %get-tuple-element.10.field_ref, f32[32,128]{1,0:T(8,128)S(1)} %collective-permute-done.2.other_ref, f32[4,16,128]{2,1,0:T(8,128)S(1)} %copy-done.4), custom_call_target="tpu_custom_call" | custom-call | tf_op jit(solution)/shard_map/pallas_call | solution.py:325
  (14 shorter events, 0.0 us)
Async XLA Ops:
  0.8 1.2 %copy-start = (bf16[16,256,128]{2,1,0:T(8,128)(2,1)S(1)}, bf16[16,256,128]{2,1,0:T(8,128)(2,1)}, u32[]{:S(2)}) copy-start(bf16[16,256,128]{2,1,0:T(8,128)(2,1)} %expand_ref.5) | copy-start | bytes 3145732
  2.0 0.8 %copy-start.3 = (f32[4,16,128]{2,1,0:T(8,128)S(1)}, f32[4,16,128]{2,1,0:T(8,128)}, u32[]{:S(2)}) copy-start(f32[4,16,128]{2,1,0:T(8,128)} %rhs_ref.7) | copy-start | bytes 98308
  2.7 0.8 %copy-start.7 = (bf16[1,64,256]{2,1,0:T(8,128)(2,1)S(1)}, bf16[1,64,256]{2,1,0:T(8,128)(2,1)}, u32[]{:S(2)}) copy-start(bf16[1,64,256]{2,1,0:T(8,128)(2,1)} %class_ref.3) | copy-start | bytes 98308
  3.5 21.5 %copy-start.1 = (bf16[16,256,128]{2,1,0:T(8,128)(2,1)S(1)}, bf16[16,256,128]{2,1,0:T(8,128)(2,1)}, u32[]{:S(2)}) copy-start(bf16[16,256,128]{2,1,0:T(8,128)(2,1)} %expand_ref.5) | copy-start | bytes 3145732
  3.5 21.5 %copy-start.2 = (bf16[26,128,128]{2,1,0:T(8,128)(2,1)S(1)}, bf16[26,128,128]{2,1,0:T(8,128)(2,1)}, u32[]{:S(2)}) copy-start(bf16[26,128,128]{2,1,0:T(8,128)(2,1)} %near_ref.3) | copy-start | bytes 2555908
  4.6 18.8 %copy-start.8 = (s32[16,4]{0,1:T(4,128)S(1)}, s32[16,4]{0,1:T(4,128)}, u32[]{:S(2)}) copy-start(s32[16,4]{0,1:T(4,128)} %param.16) | copy-start | bytes 772
  4.6 18.8 %copy-start.9 = (s32[16,4]{0,1:T(4,128)S(1)}, s32[16,4]{0,1:T(4,128)}, u32[]{:S(2)}) copy-start(s32[16,4]{0,1:T(4,128)} %param.17) | copy-start | bytes 772
  4.6 20.4 %copy-start.4 = (f32[4,16,128]{2,1,0:T(8,128)S(1)}, f32[4,16,128]{2,1,0:T(8,128)}, u32[]{:S(2)}) copy-start(f32[4,16,128]{2,1,0:T(8,128)} %rhs_ref.7) | copy-start | bytes 98308
  23.4 1.7 %copy-start.5 = (f32[16,128]{1,0:T(8,128)S(1)}, f32[16,128]{1,0:T(8,128)}, u32[]{:S(2)}) copy-start(f32[16,128]{1,0:T(8,128)} %self_ref.3) | copy-start | bytes 24580
  23.4 1.7 %copy-start.6 = (s32[16,26]{1,0:T(8,128)S(1)}, s32[16,26]{1,0:T(8,128)}, u32[]{:S(2)}) copy-start(s32[16,26]{1,0:T(8,128)} %source_ref.3) | copy-start | bytes 4996
  23.4 1.7 %collective-permute-start = (bf16[8,176,128]{2,1,0:T(8,128)(2,1)S(1)}, bf16[8,176,128]{2,1,0:T(8,128)(2,1)S(1)}, u32[]{:S(2)}, u32[]{:S(2)}) collective-permute-start(bf16[8,176,128]{2,1,0:T(8,128)(2,1)S(1)} %all_to_all.15.own_ref), channel_id=1, source_target_pairs={{0,1},{1,0},{2,3},{3,2},{4,5},{5,4},{6,7},{7,6},{8,9},{9,8},{10,11... | collective-permute-start | bytes 1081352 | tf_op jit(solution)/shard_map/ppermute | solution.py:355
  45.0 3.8 %collective-permute-start.1 = (f32[32,128]{1,0:T(8,128)S(1)}, f32[32,128]{1,0:T(8,128)S(1)}, u32[]{:S(2)}, u32[]{:S(2)}) collective-permute-start(f32[32,128]{1,0:T(8,128)S(1)} %get-tuple-element.9.far_ref), channel_id=1, source_target_pairs={{0,2},{2,0},{1,3},{3,1},{4,6},{6,4},{5,7},{7,5},{8,10},{10,8},{9,1... | collective-permute-start | bytes 49160 | tf_op jit(solution)/shard_map/ppermute | solution.py:370
  49.5 10.4 %all-to-all-start.2 = ((f32[16,8,128]{2,1,0:T(8,128)}), f32[16,8,128]{2,1,0:T(8,128)S(1)}, u32[]{:S(2)}, u32[]{:S(2)}) async-start(f32[16,8,128]{2,1,0:T(8,128)} %shard_map.94), calls=%async_computation.2 | async-start | bytes 131072 | tf_op jit(solution)/shard_map/all_to_all | solution.py:377
  53.0 1.2 %collective-permute-start.2 = (f32[32,128]{1,0:T(8,128)S(1)}, f32[32,128]{1,0:T(8,128)S(1)}, u32[]{:S(2)}, u32[]{:S(2)}) collective-permute-start(f32[32,128]{1,0:T(8,128)S(1)} %get-tuple-element.10.field_ref), channel_id=1, source_target_pairs={{0,1},{1,0},{2,3},{3,2},{4,5},{5,4},{6,7},{7,6},{8,9},{9,8},{10,11... | collective-permute-start | bytes 49160 | tf_op jit(solution)/shard_map/ppermute | solution.py:371

commit v2 on v1

v2 whole, which is shorter than its diff:
```python
import functools

import jax
import jax.numpy as jnp
from jax import lax
from jax.experimental import pallas as pl
from jax.experimental.pallas import tpu as pltpu
from jax.sharding import Mesh, PartitionSpec as P

SHIFT = 3.0
LANES = 128
HALF = jnp.bfloat16
FULL = jnp.float32
SLOT = pltpu.VMEM


def each(count, body):
    if count <= 32:
        for number in range(count):
            body(number)
    else:
        lax.fori_loop(0, count, lambda number, state: (body(number), state)[1], 0)


def fold(count, body, state):
    if count <= 32:
        for number in range(count):
            state = body(number, state)
        return state
    return lax.fori_loop(0, count, body, state)


def dot_nt(left, right):
    return lax.dot_general(left, right, (((1,), (1,)), ((), ())), preferred_element_type=FULL)


def dot_nn(left, right):
    return lax.dot_general(left, right, (((1,), (0,)), ((), ())), preferred_element_type=FULL)


def own_rows(values, result, box, boxes):
    row = lax.broadcasted_iota(jnp.int32, result.shape, 0)
    return jnp.where(row % boxes == box, values, result)


def multipoles_of(field, expand_ref):
    boxes, terms, _ = expand_ref.shape
    result = jnp.zeros((field.shape[0], terms), FULL)
    for box in range(boxes):
        result = own_rows(dot_nt(field, expand_ref[box]), result, box, boxes)
    return result


def send_table(send_ref, out_ref, boxes, width, parts):
    cap, targets = send_ref.shape
    area = out_ref.shape[0] // targets
    row = lax.broadcasted_iota(jnp.int32, (area, out_ref.shape[1]), 0)
    column = lax.broadcasted_iota(jnp.int32, (area, out_ref.shape[1]), 1)
    start = jnp.where(row < cap * width * parts, (row // cap) * boxes, -boxes)

    def put(target):
        place = start
        for turn in range(cap):
            place = jnp.where(row % cap == turn, start + send_ref[turn, target], place)
        begin = target * area if isinstance(target, int) else pl.multiple_of(target * area, area)
        out_ref[pl.ds(begin, area), :] = jnp.where(place == column, 1.0, 0.0)

    each(targets, put)


def sent_of(multipoles, table):
    half = multipoles.astype(HALF)
    parts = half.shape[1] // LANES
    stacked = jnp.concatenate([half[:, part * LANES : (part + 1) * LANES] for part in range(parts)], axis=0)
    return dot_nn(table, stacked)


def far_of(local, expand_ref, offset):
    boxes, _, panels = expand_ref.shape
    result = jnp.zeros((local.shape[0], panels), FULL)
    for box in range(boxes):
        rows = expand_ref[box, pl.ds(offset, local.shape[1]), :]
        result = own_rows(dot_nn(local, rows), result, box, boxes)
    return result


def near_of(near_ref, chosen_ref, extended, boxes, width):
    picked = dot_nn(chosen_ref[...], extended).astype(HALF)
    result = jnp.zeros((width * boxes, near_ref.shape[1]), FULL)
    for number in range(near_ref.shape[0]):
        rows = picked[number * boxes : (number + 1) * boxes]
        stacked = jnp.concatenate(
            [rows[:, rhs * LANES : (rhs + 1) * LANES] for rhs in range(width)], axis=0
        )
        result = result + dot_nt(stacked, near_ref[number])
    return result


def local_of(bands, table_ref, received, width, boxes, band):
    classes = bands[0].shape[0]
    parts = table_ref.shape[0] // width
    group = min(classes, 8)

    def add(number, total):
        begin = number * group * boxes
        if not isinstance(begin, int):
            begin = pl.multiple_of(begin, group * boxes)
        sources = [
            dot_nn(table_ref[place, pl.ds(begin, group * boxes), :], received).astype(HALF)
            for place in range(parts * width)
        ]
        for turn in range(group):
            rows = slice(turn * boxes, (turn + 1) * boxes)
            left = jnp.concatenate(
                [
                    jnp.concatenate([sources[part * width + rhs][rows] for rhs in range(width)], axis=0)
                    for part in range(parts)
                ],
                axis=1,
            )
            right = jnp.concatenate(
                [
                    jnp.concatenate(
                        [ref[number * group + turn, part * band : (part + 1) * band, :] for part in range(parts)],
                        axis=1,
                    )
                    for ref in bands
                ],
                axis=0,
            )
            total = total + dot_nt(left, right)
        return total

    return fold(classes // group, add, jnp.zeros((width * boxes, len(bands) * band), FULL))


def extended_of(pieces, index, count, boxes):
    low = jnp.where(index > 0, pieces[0], jnp.zeros_like(pieces[0]))
    high = jnp.where(index < count - 1, pieces[2], jnp.zeros_like(pieces[2]))
    width = low.shape[0] // boxes
    columns = [
        jnp.concatenate([piece[rhs * boxes : (rhs + 1) * boxes] for piece in (low, pieces[1], high)], axis=0)
        for rhs in range(width)
    ]
    return jnp.concatenate(columns, axis=1).astype(HALF)


def fetch(pairs, signals):
    copies = [
        pltpu.make_async_copy(source, target, signals.at[number])
        for number, (source, target) in enumerate(pairs)
    ]
    for copy in copies:
        copy.start()
    return copies


def near_table(source_ref, chosen_ref):
    boxes, classes = source_ref.shape
    spots = lax.broadcasted_iota(jnp.int32, (boxes, chosen_ref.shape[1]), 1)
    for number in range(classes):
        match = source_ref[:, number : number + 1] == spots
        chosen_ref[number * boxes : (number + 1) * boxes, :] = jnp.where(match, 1.0, 0.0).astype(HALF)


def list_table(cap, slot_ref, label_ref, table_ref):
    boxes = slot_ref.shape[1]
    kinds = table_ref.shape[1] // boxes
    slots, labels = slot_ref[...], label_ref[...]
    area = table_ref.shape[2] // kinds
    places = (slots // cap) * area + slots % cap
    group = min(kinds, 8)

    def put(number):
        rows = [
            jnp.max(jnp.where(labels == number * group + turn, places + 1, 0), axis=0, keepdims=True) - 1
            for turn in range(group)
        ]
        place = jnp.concatenate(rows, axis=1)
        spot = lax.broadcasted_iota(jnp.int32, (table_ref.shape[2], group * boxes), 0)
        begin = number * group * boxes
        if not isinstance(begin, int):
            begin = pl.multiple_of(begin, group * boxes)
        for which in range(table_ref.shape[0]):
            match = (place >= 0) & (place + which * cap == spot)
            table_ref[which, pl.ds(begin, group * boxes), :] = jnp.where(match, 1.0, 0.0).T.astype(HALF)

    each(kinds // group, put)


def first_kernel(
    width,
    rhs_hbm,
    expand_hbm,
    class_hbm,
    send_hbm,
    near_hbm,
    source_hbm,
    slot_hbm,
    label_hbm,
    out_ref,
    picks_ref,
    expand_ref,
    near_ref,
    chosen_ref,
    table_ref,
    rhs_ref,
    class_ref,
    send_ref,
    wide_ref,
    source_ref,
    slot_ref,
    label_ref,
    signals,
):
    boxes, terms, panels = expand_ref.shape
    core = lax.axis_index("core")
    step = boxes // 4
    pairs = [
        (send_hbm, send_ref),
        (rhs_hbm.at[pl.ds(core * width, width)], rhs_ref),
        (class_hbm, class_ref),
        (source_hbm, source_ref),
        (slot_hbm, slot_ref),
        (label_hbm, label_ref),
    ]
    for quarter in range(4):
        part = pl.ds(quarter * step, step)
        pairs.append((expand_hbm.at[part], expand_ref.at[part]))
    pairs.append((near_hbm, near_ref))
    copies = fetch(pairs, signals)
    copies[0].wait()
    send_table(send_ref, wide_ref, boxes, width, terms // LANES)
    picks_ref[...] = wide_ref[...].astype(HALF)
    band = class_ref.shape[1]
    low = (terms // LANES) * band
    high = low + width * boxes
    copies[1].wait()
    copies[2].wait()
    field = rhs_ref[...].reshape(width * boxes, panels).astype(HALF)
    operators = jnp.concatenate(
        [class_ref[0][:, part * LANES : (part + 1) * LANES] for part in range(terms // LANES)], axis=0
    )

    def put(target):
        out_ref[target, :low, :] = operators
        out_ref[target, low:high, :] = field

    each(out_ref.shape[0], put)
    for copy in copies[3:6]:
        copy.wait()
    near_table(source_ref, chosen_ref)
    list_table(send_ref.shape[0], slot_ref, label_ref, table_ref)
    result = jnp.zeros((width * boxes, terms), FULL)
    for box in range(boxes):
        if box % step == 0:
            copies[6 + box // step].wait()
        result = own_rows(dot_nt(field, expand_ref[box]), result, box, boxes)
    sent = sent_of(result, picks_ref[...]).astype(HALF)
    out_ref[:, high:, :] = sent.reshape(out_ref.shape[0], -1, LANES)
    copies[10].wait()


def base_kernel(width, low, own_ref, rhs_ref, self_ref, near_ref, chosen_ref, out_ref):
    boxes, panels = self_ref.shape
    count = own_ref.shape[0]
    core, side, index = lax.axis_index("core"), lax.axis_index("side"), lax.axis_index("box")
    high = low + width * boxes
    pieces = [own_ref[jnp.clip(index + step, 0, count - 1), low:high, :] for step in (-1, 0, 1)]
    near = near_of(near_ref, chosen_ref, extended_of(pieces, index, count, boxes), boxes, width)
    field = rhs_ref[pl.ds(core * width, width)]
    diagonal = ((self_ref[...] - SHIFT)[None] * field).reshape(width * boxes, panels)
    out_ref[...] = jnp.where(side == 0, near + diagonal, 0.0)


def second_kernel(width, band, own_ref, other_ref, base_ref, expand_ref, table_ref, send_ref, out_ref):
    boxes, terms, panels = expand_ref.shape
    count = own_ref.shape[0]
    core, side = lax.axis_index("core"), lax.axis_index("side")
    rows = width * boxes
    high = (terms // LANES) * band + rows
    received = own_ref[:, high:, :].astype(FULL).reshape(-1, LANES).astype(HALF)
    total = local_of((own_ref, other_ref), table_ref, received, width, boxes, band)
    local = jnp.where(core == 0, total, pltpu.roll(total, band, 1)).astype(HALF)
    image = far_of(local, expand_ref, side * (terms // 2)) + base_ref[...]
    half = image.astype(HALF)
    sent = sent_of(multipoles_of(half, expand_ref), send_ref[...]).astype(HALF).reshape(count, -1, LANES)
    for part in range(2):
        out_ref[:, part, rows:, :] = sent

    def put(target):
        for part in range(2):
            out_ref[target, part, :rows, :] = half

    each(count, put)


def rest_kernel(width, parts_ref, self_ref, near_ref, chosen_ref, rest_ref, field_ref):
    boxes, panels = self_ref.shape
    count = parts_ref.shape[0]
    index = lax.axis_index("box")
    rows = width * boxes

    def joined(place):
        return parts_ref[place, 0, :rows, :].astype(FULL) + parts_ref[place, 1, :rows, :].astype(FULL)

    pieces = [joined(jnp.clip(index + step, 0, count - 1)) for step in (-1, 0, 1)]
    near = near_of(near_ref, chosen_ref, extended_of(pieces, index, count, boxes), boxes, width)
    field = pieces[1]
    diagonal = ((self_ref[...] - SHIFT)[None] * field.reshape(width, boxes, panels)).reshape(rows, panels)
    rest_ref[...] = near + diagonal
    field_ref[...] = field


def third_kernel(
    width,
    band,
    own_ref,
    other_ref,
    across_ref,
    corner_ref,
    parts_ref,
    expand_ref,
    table_ref,
    rest_ref,
    field_ref,
    rhs_ref,
    out_ref,
):
    boxes, terms, panels = expand_ref.shape
    core, side = lax.axis_index("core"), lax.axis_index("side")
    rows = width * boxes
    blocks = parts_ref[:, :, rows:, :].astype(FULL)
    received = (blocks[:, 0] + blocks[:, 1]).reshape(-1, LANES).astype(HALF)
    bands = (own_ref, other_ref, across_ref, corner_ref)
    total = local_of(bands, table_ref, received, width, boxes, band)
    halves = [total[:, : 2 * band], total[:, 2 * band :]]
    halves = [jnp.where(core == 0, half, pltpu.roll(half, band, 1)) for half in halves]
    local = jnp.concatenate(
        [jnp.where(side == 0, halves[0], halves[1]), jnp.where(side == 0, halves[1], halves[0])], axis=1
    ).astype(HALF)
    last = rest_ref[...] + far_of(local, expand_ref, 0)
    field = field_ref[...]
    right = rhs_ref[pl.ds(core * width, width)].reshape(rows, panels)
    spots = lax.broadcasted_iota(jnp.int32, (8, panels), 0)
    lanes = lax.broadcasted_iota(jnp.int32, (8, panels), 1)
    result = jnp.zeros((8, panels), FULL)
    pairs = ((right, right), (right, field), (field, field), (right, last), (field, last), (last, last))
    for number, (one, two) in enumerate(pairs):
        product = one * two
        for rhs in range(width):
            total = jnp.sum(product[rhs * boxes : (rhs + 1) * boxes])
            mine = (spots == number) & (lanes // (panels // width) == rhs)
            result = jnp.where(mine, total, result)

    def put(target):
        out_ref[target] = result

    each(out_ref.shape[0], put)


def last_kernel(width, sums_ref, field_ref, other_ref, rhs_ref, out_ref):
    core = lax.axis_index("core")
    rows, panels = field_ref.shape
    boxes = rows // width
    fields = (field_ref[...], other_ref[...])
    part = panels // width
    lanes = lax.broadcasted_iota(jnp.int32, (1, panels), 1)
    for group in range(2):
        total = fold(
            sums_ref.shape[0] // 2,
            lambda number, state: state + sums_ref[2 * number + group],
            jnp.zeros(sums_ref.shape[1:], FULL),
        )
        rr, ru, uu, rw, uw, ww = (total[number : number + 1] for number in range(6))
        slope = ru / rr
        norm = uu - slope * ru
        first_row = rw - slope * ru
        scale = lax.rsqrt(rr * norm)
        h11 = slope + SHIFT
        h21 = jnp.sqrt(norm / rr)
        h12 = first_row * scale
        h22 = (uw - slope * uu - slope * first_row) / norm
        image = (ww - 2.0 * slope * uw + slope * slope * uu) / norm
        gram_aa = h11 * h11 + h21 * h21
        gram_ab = h11 * h12 + h21 * (h22 + SHIFT)
        gram_bb = image + 2.0 * SHIFT * h22 + SHIFT * SHIFT
        beta = jnp.sqrt(rr)
        right_a, right_b = beta * h11, beta * h12
        determinant = gram_aa * gram_bb - gram_ab * gram_ab
        coef_a = (gram_bb * right_a - gram_ab * right_b) / determinant
        coef_b = (gram_aa * right_b - gram_ab * right_a) / determinant
        weight = coef_b * lax.rsqrt(norm)
        first = coef_a / beta - weight * slope
        chosen = jnp.where(core == group, fields[0], fields[1])
        for rhs in range(width):
            def wide(value):
                inside = jnp.where(lanes // part == rhs, value, 0.0)
                spread = inside
                for step in range(1, width):
                    spread = spread + pltpu.roll(inside, step * part, 1)
                return spread

            place = group * width + rhs
            out_ref[place] = wide(first) * rhs_ref[place] + wide(weight) * chosen[rhs * boxes : (rhs + 1) * boxes]


def call(kernel, outs, *args, fixed=0, scratch=(), flops=0, limit=16):
    vmem = pl.BlockSpec(memory_space=pltpu.VMEM)
    many = isinstance(outs, list)
    held = len(args) - fixed
    args = [
        value if number < held else pltpu.with_memory_space_constraint(value, pltpu.HBM)
        for number, value in enumerate(args)
    ]
    return pl.pallas_call(
        kernel,
        out_shape=outs,
        in_specs=[vmem] * held + [pl.BlockSpec(memory_space=pltpu.HBM)] * fixed,
        out_specs=[vmem] * len(outs) if many else vmem,
        scratch_shapes=list(scratch),
        compiler_params=pltpu.CompilerParams(vmem_limit_bytes=limit * 1024 * 1024),
        cost_estimate=pl.CostEstimate(flops=flops, bytes_accessed=0, transcendentals=0) if flops else None,
    )(*args)


def per_device(
    rhs_field, self_coef, expand, near_ops, class_ops, near_src, send_rows, list_slot, list_class
):
    count = lax.axis_size("box")
    boxes, terms, panels = expand.shape
    width = rhs_field.shape[0] // 2
    rows = width * boxes
    band = class_ops.shape[1]
    cap = send_rows.shape[2]
    parts = terms // LANES
    area = -(-(cap * width * parts) // 8) * 8
    low = parts * band
    swap = [(0, 1), (1, 0)]
    shape = jax.ShapeDtypeStruct
    send = jnp.swapaxes(send_rows, 1, 2)[0]
    slot, label = list_slot.T, list_class.T
    block = shape((rows, panels), FULL)
    kernel = functools.partial(call, limit=16 if count <= 16 else 56)

    slots, picks, kept, near, chosen, table = kernel(
        functools.partial(first_kernel, width),
        [
            shape((count, low + rows + area, LANES), HALF),
            shape((count * area, parts * rows), HALF),
            SLOT(expand.shape, HALF),
            SLOT(near_ops.shape, HALF),
            shape((near_ops.shape[0] * boxes, 3 * boxes), HALF),
            shape((width * parts, count * boxes, count * area), HALF),
        ],
        rhs_field, expand, class_ops, send, near_ops, near_src, slot, label,
        fixed=8,
        scratch=[
            pltpu.VMEM((width,) + rhs_field.shape[1:], FULL),
            pltpu.VMEM(class_ops.shape, HALF),
            pltpu.SMEM(send.shape, jnp.int32),
            pltpu.VMEM((count * area, parts * rows), FULL),
            pltpu.VMEM(near_src.shape, jnp.int32),
            pltpu.VMEM(slot.shape, jnp.int32),
            pltpu.VMEM(label.shape, jnp.int32),
            pltpu.SemaphoreType.DMA((11,)),
        ],
    )
    own = lax.all_to_all(slots, "box", 0, 0, tiled=True)
    bands = own[:, :low]
    other = lax.ppermute(bands, "core", swap)
    across = lax.ppermute(bands, "side", swap)
    corner = lax.ppermute(across, "core", swap)
    base = kernel(
        functools.partial(base_kernel, width, low), block,
        own, rhs_field, self_coef, near, chosen,
        flops=1_000_000_000,
    )
    images = kernel(
        functools.partial(second_kernel, width, band),
        shape((count, 2, rows + area, LANES), HALF),
        own, other, base, kept, table, picks,
    )
    images = images.reshape((2 * count,) + images.shape[2:])
    images = lax.all_to_all(images, ("box", "side"), 0, 0, tiled=True)
    images = images.reshape((count, 2) + images.shape[1:])
    rest, field = kernel(
        functools.partial(rest_kernel, width), [block, block],
        images, self_coef, near, chosen,
        flops=1_000_000_000,
    )
    field_other = lax.ppermute(field, "core", swap)
    sums = kernel(
        functools.partial(third_kernel, width, band),
        SLOT((2 * count, 8, panels), FULL),
        bands, other, across, corner, images, kept, table, rest, field, rhs_field,
    )
    sums = lax.all_to_all(sums, ("box", "core"), 0, 0, tiled=True)
    return kernel(
        functools.partial(last_kernel, width),
        shape(rhs_field.shape, FULL),
        sums, field, field_other, rhs_field,
    )


def solution(mesh):
    count, levels = mesh.devices.shape
    finer = Mesh(mesh.devices.reshape(count, levels // 2, 2), ("box", "side", "core"))
    return jax.shard_map(
        per_device,
        mesh=finer,
        in_specs=(
            P(None, "box", None),
            P("box", None),
            P("box", None, None),
            P(),
            P("box", ("side", "core"), None),
            P("box", None),
            P("box", None, None),
            P("box", None),
            P("box", None),
        ),
        out_specs=P(None, "box", None),
        check_vma=False,
    )
```

time: 61.1 us -> 50.9 us (0.83)
  blocking collectives: 31.6 us -> 18.3 us
  starting transfers between devices: 4.79 us -> 8.96 us
  waiting for transfers between devices: 10.9 us -> 14.9 us
  local copies, waits for them, and re-layouts: 3.69 us -> 0.03 us
  Pallas kernels: 9.6 us -> 8.31 us
    all_to_all x1 -> x0, blocking collectives: 12.9 us -> none  [per_device(): parts = lax.all_to_all(parts, ('box', 'side'), 0, 0, tiled=True)]
    all_to_all x0 -> x1, waiting for transfers between devices: none -> 7.69 us  [per_device(): images = lax.all_to_all(images, ('box', 'side'), 0, 0, tiled=True)]
    unnamed x23 -> x4, local copies, waits for them, and re-layouts: 3.69 us -> 0.01 us
    ppermute x2 -> x3, waiting for transfers between devices: 4.29 us -> 0.72 us  [the longest x1 0.72 us: per_device(): across = lax.ppermute(bands, 'side', swap)]
    all_to_all x0 -> x1, starting transfers between devices: none -> 3.52 us  [per_device(): images = lax.all_to_all(images, ('box', 'side'), 0, 0, tiled=True)]
    pallas_call x5 -> x6, Pallas kernels: 9.6 us -> 8.31 us  [call(): pl.pallas_call(kernel, out_shape=outs, in_specs=[vmem] * held + [pl.Block...]
    ppermute x2 -> x3, starting transfers between devices: 1.01 us -> 1.63 us  [the longest x1 1.56 us: per_device(): across = lax.ppermute(bands, 'side', swap)]
  transfers between devices with their start and end apart: 4 -> 6, of which waited for: 4 -> 4; matrix products, arithmetic and copies ran while one was open for 0% -> 0% of each run, Pallas kernels for 0% -> 7%
where the time goes in v2:
time: 50.9 us; the launch traced here: 50.6 us
  blocking collectives  18.3 us (36%)
  waiting for transfers between devices  14.9 us (29%)
  starting transfers between devices  8.96 us (18%)
  Pallas kernels  8.31 us (16%)
    all_to_all x1, blocking collectives, per_device(): own = lax.all_to_all(slots, 'box', 0, 0, tiled=True)  18.3 us
    pallas_call x6, Pallas kernels, call(): pl.pallas_call(kernel, out_shape=outs, in_specs=[vmem] * held + [pl.Block...  8.31 us
    all_to_all x1, waiting for transfers between devices, per_device(): images = lax.all_to_all(images, ('box', 'side'), 0, 0, tiled=True)  7.69 us
    all_to_all x1, waiting for transfers between devices, per_device(): sums = lax.all_to_all(sums, ('box', 'core'), 0, 0, tiled=True)  5.61 us
    all_to_all x1, starting transfers between devices, per_device(): images = lax.all_to_all(images, ('box', 'side'), 0, 0, tiled=True)  3.52 us
    all_to_all x1, starting transfers between devices, per_device(): sums = lax.all_to_all(sums, ('box', 'core'), 0, 0, tiled=True)  3.49 us
    ppermute x1, starting transfers between devices, per_device(): across = lax.ppermute(bands, 'side', swap)  1.56 us
  transfers between devices with their start and end apart: 6, of which 4 were waited for; matrix products, arithmetic and copies ran while one was open for 0% of the time, Pallas kernels for 7%

profile of v2, /device:TPU:0, one launch (start us, length us, event | category | flops | bytes accessed | tf_op | source)
XLA Modules:
  0.0 50.6 jit_solution(16347342551453791170)
XLA Ops:
  0.0 2.1 %shard_map.91 = (bf16[8,168,128]{2,1,0:T(8,128)(2,1)S(1)}, bf16[64,64]{1,0:T(8,128)(2,1)S(1)}, bf16[16,256,128]{2,1,0:T(8,128)(2,1)S(1)}, bf16[26,128,128]{2,1,0...) custom-call(f32[4,16,128]{2,1,0:T(8,128)} %rhs_ref.5, bf16[16,256,128]{2,1,0:T(8,128)(2,1)} %expand_hbm.1, ...), custom_call_target="tpu_custom_call" | custom-call | tf_op jit(solution)/shard_map/pallas_call | solution.py:416
  2.1 18.3 %all_to_all.15.own_ref = bf16[8,168,128]{2,1,0:T(8,128)(2,1)S(1)} all-to-all(bf16[8,168,128]{2,1,0:T(8,128)(2,1)S(1)} %get-tuple-element.13), channel_id=1, replica_groups=mesh['box'=8,'side'=2,'core'=2] {'box'}, dimensions={0} | all-to-all | bytes 688128 | tf_op jit(solution)/shard_map/all_to_all | solution.py:469
  20.4 0.0 copy-start
  20.4 0.0 copy-start.1
  20.4 0.1 collective-permute-start
  20.5 1.6 %collective-permute-start.1 = (bf16[8,128,128]{2,1,0:T(8,128)(2,1)S(1)}, bf16[8,128,128]{2,1,0:T(8,128)(2,1)S(1)}, u32[]{:S(2)}, u32[]{:S(2)}) collective-permute-start(bf16[8,128,128]{2,1,0:T(8,128)(2,1)S(1)} %slice.4.own_ref), channel_id=1, source_target_pairs={{0,2},{2,0},{1,3},{3,1},{4,6},{6,4},{5,7},{7,5},{8,10},{10,8},{9,1... | collective-permute-start | bytes 786440 | tf_op jit(solution)/shard_map/ppermute | solution.py:472
  22.0 0.0 copy-done
  22.0 0.0 copy-done.1
  22.0 0.7 %shard_map.92.base_ref = f32[32,128]{1,0:T(8,128)S(1)} custom-call(bf16[8,168,128]{2,1,0:T(8,128)(2,1)S(1)} %all_to_all.15.own_ref, f32[4,16,128]{2,1,0:T(8,128)S(1)} %copy-done, f32[16,128]{1,0:T(8,128)S(1)} %copy-done.1, bf16[26,128,128]{2,1,0:T(8,128)(2,1)S(1)} %get-tuple-element.14.near_ref, bf16[416,48]{1,0:T(8,128)(2,1)S(1)} %get-tuple-element.15.chosen_ref), custom_call_target="tpu_custom_call" | custom-call | flops 1000000000 | tf_op jit(solution)/shard_map/pallas_call | solution.py:416
  22.8 0.0 collective-permute-done.other_ref
  22.8 2.2 %shard_map.93 = bf16[8,2,40,128]{3,2,1,0:T(8,128)(2,1)} custom-call(bf16[8,168,128]{2,1,0:T(8,128)(2,1)S(1)} %all_to_all.15.own_ref, bf16[8,128,128]{2,1,0:T(8,128)(2,1)S(1)} %collective-permute-done.other_ref, f32[32,128]{1,0:T(8,128)S(1)} %shard_map.92.base_ref, bf16[16,256,128]{2,1,0:T(8,128)(2,1)S(1)} %get-tuple-element.16.expand_ref, ...), custom_call_target="tpu_custom_call" | custom-call | tf_op jit(solution)/shard_map/pallas_call | solution.py:416
  25.0 3.5 %all-to-all-start.1 = ((bf16[16,40,128]{2,1,0:T(8,128)(2,1)}), bf16[16,40,128]{2,1,0:T(8,128)(2,1)S(1)}, u32[]{:S(2)}, u32[]{:S(2)}) async-start(bf16[16,40,128]{2,1,0:T(8,128)(2,1)} %bitcast.4), calls=%async_computation.1 | async-start | bytes 327680 | tf_op jit(solution)/shard_map/all_to_all | solution.py:485
  28.5 0.7 %collective-permute-done.1.across_ref = bf16[8,128,128]{2,1,0:T(8,128)(2,1)S(1)} collective-permute-done((bf16[8,128,128]{2,1,0:T(8,128)(2,1)S(1)}, bf16[8,128,128]{2,1,0:T(8,128)(2,1)S(1)}, u32[]{:S(2)}, u32[]{:S(2)}) %collective-permute-start.1) | collective-permute-done | bytes 262176 | tf_op jit(solution)/shard_map/ppermute | solution.py:472
  29.2 0.0 collective-permute-start.2
  29.2 7.7 %all-to-all-done.1 = bf16[16,40,128]{2,1,0:T(8,128)(2,1)S(1)} async-done(((bf16[16,40,128]{2,1,0:T(8,128)(2,1)}), bf16[16,40,128]{2,1,0:T(8,128)(2,1)S(1)}, u32[]{:S(2)}, u32[]{:S(2)}) %all-to-all-start.1) | async-done | bytes 163872 | tf_op jit(solution)/shard_map/all_to_all | solution.py:485
  36.9 0.7 %shard_map.94 = (f32[32,128]{1,0:T(8,128)S(1)}, f32[32,128]{1,0:T(8,128)S(1)}) custom-call(bf16[8,2,40,128]{3,2,1,0:T(8,128)(2,1)S(1)} %bitcast.7, f32[16,128]{1,0:T(8,128)S(1)} %copy-done.1, bf16[26,128,128]{2,1,0:T(8,128)(2,1)S(1)} %get-tuple-element.14.near_ref, bf16[416,48]{1,0:T(8,128)(2,1)S(1)} %get-tuple-element.15.chosen_ref), custom_call_target="tpu_custom_call" | custom-call | flops 1000000000 | tf_op jit(solution)/shard_map/pallas_call | solution.py:416
  37.6 0.0 collective-permute-done.2.corner_ref
  37.6 1.9 %shard_map.95 = f32[16,8,128]{2,1,0:T(8,128)} custom-call(bf16[8,128,128]{2,1,0:T(8,128)(2,1)S(1)} %slice.4.own_ref, bf16[8,128,128]{2,1,0:T(8,128)(2,1)S(1)} %collective-permute-done.other_ref, bf16[8,128,128]{2,1,0:T(8,128)(2,1)S(1)} %collective-permute-done.1.across_ref, bf16[8,128,128]{2,1,0:T(8,128)(2,1)S(1)} %collective-permute-done.2.corner_ref, ...), custom_call_target="tpu_custom_call" | custom-call | tf_op jit(solution)/shard_map/pallas_call | solution.py:416
  39.5 3.5 %all-to-all-start.2 = ((f32[16,8,128]{2,1,0:T(8,128)}), f32[16,8,128]{2,1,0:T(8,128)S(1)}, u32[]{:S(2)}, u32[]{:S(2)}) async-start(f32[16,8,128]{2,1,0:T(8,128)} %shard_map.95), calls=%async_computation.2 | async-start | bytes 131072 | tf_op jit(solution)/shard_map/all_to_all | solution.py:498
  43.0 0.3 collective-permute-start.3
  43.3 0.9 %collective-permute-done.3.other_ref = f32[32,128]{1,0:T(8,128)S(1)} collective-permute-done((f32[32,128]{1,0:T(8,128)S(1)}, f32[32,128]{1,0:T(8,128)S(1)}, u32[]{:S(2)}, u32[]{:S(2)}) %collective-permute-start.3) | collective-permute-done | bytes 16416 | tf_op jit(solution)/shard_map/ppermute | solution.py:492
  44.2 5.6 %all-to-all-done.2.sums_ref = f32[16,8,128]{2,1,0:T(8,128)S(1)} async-done(((f32[16,8,128]{2,1,0:T(8,128)}), f32[16,8,128]{2,1,0:T(8,128)S(1)}, u32[]{:S(2)}, u32[]{:S(2)}) %all-to-all-start.2) | async-done | bytes 65568 | tf_op jit(solution)/shard_map/all_to_all | solution.py:498
  49.8 0.7 %shard_map.96 = f32[4,16,128]{2,1,0:T(8,128)} custom-call(f32[16,8,128]{2,1,0:T(8,128)S(1)} %all-to-all-done.2.sums_ref, f32[32,128]{1,0:T(8,128)S(1)} %get-tuple-element.20.field_ref, f32[32,128]{1,0:T(8,128)S(1)} %collective-permute-done.3.other_ref, f32[4,16,128]{2,1,0:T(8,128)S(1)} %copy-done), custom_call_target="tpu_custom_call" | custom-call | tf_op jit(solution)/shard_map/pallas_call | solution.py:416
  (1 shorter events, 0.0 us)
Async XLA Ops:
  20.4 1.7 %copy-start = (f32[4,16,128]{2,1,0:T(8,128)S(1)}, f32[4,16,128]{2,1,0:T(8,128)}, u32[]{:S(2)}) copy-start(f32[4,16,128]{2,1,0:T(8,128)} %rhs_ref.5) | copy-start | bytes 98308
  20.4 1.7 %copy-start.1 = (f32[16,128]{1,0:T(8,128)S(1)}, f32[16,128]{1,0:T(8,128)}, u32[]{:S(2)}) copy-start(f32[16,128]{1,0:T(8,128)} %self_ref.3) | copy-start | bytes 24580
  20.4 2.4 %collective-permute-start = (bf16[8,128,128]{2,1,0:T(8,128)(2,1)S(1)}, bf16[8,128,128]{2,1,0:T(8,128)(2,1)S(1)}, u32[]{:S(2)}, u32[]{:S(2)}) collective-permute-start(bf16[8,128,128]{2,1,0:T(8,128)(2,1)S(1)} %slice.4.own_ref), channel_id=1, source_target_pairs={{0,1},{1,0},{2,3},{3,2},{4,5},{5,4},{6,7},{7,6},{8,9},{9,8},{10,11... | collective-permute-start | bytes 786440 | tf_op jit(solution)/shard_map/ppermute | solution.py:471
  20.5 8.7 %collective-permute-start.1 = (bf16[8,128,128]{2,1,0:T(8,128)(2,1)S(1)}, bf16[8,128,128]{2,1,0:T(8,128)(2,1)S(1)}, u32[]{:S(2)}, u32[]{:S(2)}) collective-permute-start(bf16[8,128,128]{2,1,0:T(8,128)(2,1)S(1)} %slice.4.own_ref), channel_id=1, source_target_pairs={{0,2},{2,0},{1,3},{3,1},{4,6},{6,4},{5,7},{7,5},{8,10},{10,8},{9,1... | collective-permute-start | bytes 786440 | tf_op jit(solution)/shard_map/ppermute | solution.py:472
  25.0 11.9 %all-to-all-start.1 = ((bf16[16,40,128]{2,1,0:T(8,128)(2,1)}), bf16[16,40,128]{2,1,0:T(8,128)(2,1)S(1)}, u32[]{:S(2)}, u32[]{:S(2)}) async-start(bf16[16,40,128]{2,1,0:T(8,128)(2,1)} %bitcast.4), calls=%async_computation.1 | async-start | bytes 327680 | tf_op jit(solution)/shard_map/all_to_all | solution.py:485
  29.2 8.4 %collective-permute-start.2 = (bf16[8,128,128]{2,1,0:T(8,128)(2,1)S(1)}, bf16[8,128,128]{2,1,0:T(8,128)(2,1)S(1)}, u32[]{:S(2)}, u32[]{:S(2)}) collective-permute-start(bf16[8,128,128]{2,1,0:T(8,128)(2,1)S(1)} %collective-permute-done.1.across_ref), channel_id=1, source_target_pairs={{0,1},{1,0},{2,3},{3,2},{4,5},{5,4},{6,7},{7,6},{8,9},{9,8},{10,11... | collective-permute-start | bytes 786440 | tf_op jit(solution)/shard_map/ppermute | solution.py:473
  39.5 10.4 %all-to-all-start.2 = ((f32[16,8,128]{2,1,0:T(8,128)}), f32[16,8,128]{2,1,0:T(8,128)S(1)}, u32[]{:S(2)}, u32[]{:S(2)}) async-start(f32[16,8,128]{2,1,0:T(8,128)} %shard_map.95), calls=%async_computation.2 | async-start | bytes 131072 | tf_op jit(solution)/shard_map/all_to_all | solution.py:498
  43.0 1.2 %collective-permute-start.3 = (f32[32,128]{1,0:T(8,128)S(1)}, f32[32,128]{1,0:T(8,128)S(1)}, u32[]{:S(2)}, u32[]{:S(2)}) collective-permute-start(f32[32,128]{1,0:T(8,128)S(1)} %get-tuple-element.20.field_ref), channel_id=1, source_target_pairs={{0,1},{1,0},{2,3},{3,2},{4,5},{5,4},{6,7},{7,6},{8,9},{9,8},{10,11... | collective-permute-start | bytes 49160 | tf_op jit(solution)/shard_map/ppermute | solution.py:492

commit v3 on v2

--- a/solution.py
+++ b/solution.py
@@ -76,62 +76,69 @@
 
 
 def far_of(local, expand_ref, offset):
-    boxes, _, panels = expand_ref.shape
-    result = jnp.zeros((local.shape[0], panels), FULL)
-    for box in range(boxes):
-        rows = expand_ref[box, pl.ds(offset, local.shape[1]), :]
-        result = own_rows(dot_nn(local, rows), result, box, boxes)
-    return result
+    boxes = expand_ref.shape[0]
+    row = lax.broadcasted_iota(jnp.int32, local.shape, 0)
+    left = [jnp.where(row % boxes == box, local, jnp.zeros_like(local)) for box in range(boxes)]
+    right = [expand_ref[box, pl.ds(offset, local.shape[1]), :] for box in range(boxes)]
+    return dot_nn(jnp.concatenate(left, axis=1), jnp.concatenate(right, axis=0))
 
 
 def near_of(near_ref, chosen_ref, extended, boxes, width):
     picked = dot_nn(chosen_ref[...], extended).astype(HALF)
+    classes = near_ref.shape[0]
     result = jnp.zeros((width * boxes, near_ref.shape[1]), FULL)
-    for number in range(near_ref.shape[0]):
-        rows = picked[number * boxes : (number + 1) * boxes]
-        stacked = jnp.concatenate(
-            [rows[:, rhs * LANES : (rhs + 1) * LANES] for rhs in range(width)], axis=0
-        )
-        result = result + dot_nt(stacked, near_ref[number])
-    return result
-
-
-def local_of(bands, table_ref, received, width, boxes, band):
-    classes = bands[0].shape[0]
-    parts = table_ref.shape[0] // width
-    group = min(classes, 8)
-
-    def add(number, total):
-        begin = number * group * boxes
-        if not isinstance(begin, int):
-            begin = pl.multiple_of(begin, group * boxes)
-        sources = [
-            dot_nn(table_ref[place, pl.ds(begin, group * boxes), :], received).astype(HALF)
-            for place in range(parts * width)
-        ]
-        for turn in range(group):
-            rows = slice(turn * boxes, (turn + 1) * boxes)
-            left = jnp.concatenate(
+    for first in range(0, classes, 2):
+        group = range(first, min(first + 2, classes))
+        left = [
+            jnp.concatenate(
                 [
-                    jnp.concatenate([sources[part * width + rhs][rows] for rhs in range(width)], axis=0)
-                    for part in range(parts)
+                    picked[number * boxes : (number + 1) * boxes, rhs * LANES : (rhs + 1) * LANES]
+                    for number in group
                 ],
                 axis=1,
             )
-            right = jnp.concatenate(
-                [
-                    jnp.concatenate(
-                        [ref[number * group + turn, part * band : (part + 1) * band, :] for part in range(parts)],
-                        axis=1,
-                    )
-                    for ref in bands
-                ],
-                axis=0,
-            )
-            total = total + dot_nt(left, right)
-        return total
-
-    return fold(classes // group, add, jnp.zeros((width * boxes, len(bands) * band), FULL))
+            for rhs in range(width)
+        ]
+        right = [near_ref[number] for number in group]
+        result = result + dot_nt(jnp.concatenate(left, axis=0), jnp.concatenate(right, axis=1))
+    return result
+
+
+def sources_of(blocks):
+    count, area, panels = blocks.shape
+    half = area // 2
+    pairs = blocks.reshape(count // 2, 2, area, panels)
+    low, high = pairs[:, 0], pairs[:, 1]
+    row = lax.broadcasted_iota(jnp.int32, low.shape, 1)
+    moved_low, moved_high = pltpu.roll(low, half, 1), pltpu.roll(high, half, 1)
+    first = jnp.where(row < half, low, moved_high).reshape(-1, panels)
+    second = jnp.where(row < half, moved_low, high).reshape(-1, panels)
+    return jnp.concatenate([first, second], axis=1).astype(HALF)
+
+
+def local_of(bands, table_ref, sources, band):
+    classes = bands[0].shape[0]
+    group = classes // table_ref.shape[0]
+    parts = sources.shape[1] // LANES
+
+    def add(number, total):
+        images = []
+        for turn in range(group):
+            right = [
+                jnp.concatenate(
+                    [ref[number * group + turn, part * band : (part + 1) * band, :] for part in range(parts)],
+                    axis=1,
+                )
+                for ref in bands
+            ]
+            images.append(dot_nt(sources, jnp.concatenate(right, axis=0)))
+        images = jnp.concatenate(images, axis=0)
+        upper = images.astype(HALF)
+        lower = (images - upper.astype(FULL)).astype(HALF)
+        table = table_ref[number]
+        return total + (dot_nn(table, upper) + dot_nn(table, lower))
+
+    return fold(table_ref.shape[0], add, jnp.zeros((table_ref.shape[1], len(bands) * band), FULL))
 
 
 def extended_of(pieces, index, count, boxes):
@@ -163,29 +170,24 @@
         chosen_ref[number * boxes : (number + 1) * boxes, :] = jnp.where(match, 1.0, 0.0).astype(HALF)
 
 
-def list_table(cap, slot_ref, label_ref, table_ref):
+def list_table(cap, width, kinds, slot_ref, label_ref, table_ref):
     boxes = slot_ref.shape[1]
-    kinds = table_ref.shape[1] // boxes
+    groups, rows, columns = table_ref.shape
     slots, labels = slot_ref[...], label_ref[...]
-    area = table_ref.shape[2] // kinds
-    places = (slots // cap) * area + slots % cap
-    group = min(kinds, 8)
+    places = (slots // cap) * (cap * width) + slots % cap
+    group = kinds // groups
+    received = columns // group
 
     def put(number):
-        rows = [
-            jnp.max(jnp.where(labels == number * group + turn, places + 1, 0), axis=0, keepdims=True) - 1
-            for turn in range(group)
-        ]
-        place = jnp.concatenate(rows, axis=1)
-        spot = lax.broadcasted_iota(jnp.int32, (table_ref.shape[2], group * boxes), 0)
-        begin = number * group * boxes
-        if not isinstance(begin, int):
-            begin = pl.multiple_of(begin, group * boxes)
-        for which in range(table_ref.shape[0]):
-            match = (place >= 0) & (place + which * cap == spot)
-            table_ref[which, pl.ds(begin, group * boxes), :] = jnp.where(match, 1.0, 0.0).T.astype(HALF)
-
-    each(kinds // group, put)
+        blocks = []
+        for turn in range(group):
+            place = jnp.max(jnp.where(labels == number * group + turn, places + 1, 0), axis=0, keepdims=True) - 1
+            place = jnp.concatenate([jnp.where(place >= 0, place + rhs * cap, -1) for rhs in range(width)], axis=1)
+            spot = lax.broadcasted_iota(jnp.int32, (received, rows), 0)
+            blocks.append(jnp.where(place == spot, 1.0, 0.0))
+        table_ref[number] = jnp.concatenate(blocks, axis=0).T.astype(HALF)
+
+    each(groups, put)
 
 
 def first_kernel(
@@ -214,7 +216,7 @@
     signals,
 ):
     boxes, terms, panels = expand_ref.shape
-    core = lax.axis_index("core")
+    core, side = lax.axis_index("core"), lax.axis_index("side")
     step = boxes // 4
     pairs = [
         (send_hbm, send_ref),
@@ -234,9 +236,10 @@
     picks_ref[...] = wide_ref[...].astype(HALF)
     band = class_ref.shape[1]
     low = (terms // LANES) * band
-    high = low + width * boxes
+    high = low + width * (boxes // 2)
     copies[1].wait()
     copies[2].wait()
+    shown = rhs_ref[:, pl.ds(side * (boxes // 2), boxes // 2), :].reshape(high - low, panels).astype(HALF)
     field = rhs_ref[...].reshape(width * boxes, panels).astype(HALF)
     operators = jnp.concatenate(
         [class_ref[0][:, part * LANES : (part + 1) * LANES] for part in range(terms // LANES)], axis=0
@@ -244,13 +247,13 @@
 
     def put(target):
         out_ref[target, :low, :] = operators
-        out_ref[target, low:high, :] = field
+        out_ref[target, low:high, :] = shown
 
     each(out_ref.shape[0], put)
     for copy in copies[3:6]:
         copy.wait()
     near_table(source_ref, chosen_ref)
-    list_table(send_ref.shape[0], slot_ref, label_ref, table_ref)
+    list_table(send_ref.shape[0], width, out_ref.shape[0], slot_ref, label_ref, table_ref)
     result = jnp.zeros((width * boxes, terms), FULL)
     for box in range(boxes):
         if box % step == 0:
@@ -265,12 +268,20 @@
     boxes, panels = self_ref.shape
     count = own_ref.shape[0]
     core, side, index = lax.axis_index("core"), lax.axis_index("side"), lax.axis_index("box")
-    high = low + width * boxes
-    pieces = [own_ref[jnp.clip(index + step, 0, count - 1), low:high, :] for step in (-1, 0, 1)]
+    half = boxes // 2
+    empty = jnp.zeros((half, panels), FULL)
+    pieces = []
+    for step in (-1, 0, 1):
+        shown = own_ref[jnp.clip(index + step, 0, count - 1), low : low + width * half, :].astype(FULL)
+        rows = []
+        for rhs in range(width):
+            part = shown[rhs * half : (rhs + 1) * half]
+            rows += [jnp.where(side == 0, part, empty), jnp.where(side == 0, empty, part)]
+        pieces.append(jnp.concatenate(rows, axis=0))
     near = near_of(near_ref, chosen_ref, extended_of(pieces, index, count, boxes), boxes, width)
     field = rhs_ref[pl.ds(core * width, width)]
     diagonal = ((self_ref[...] - SHIFT)[None] * field).reshape(width * boxes, panels)
-    out_ref[...] = jnp.where(side == 0, near + diagonal, 0.0)
+    out_ref[...] = near + jnp.where(side == 0, diagonal, 0.0)
 
 
 def second_kernel(width, band, own_ref, other_ref, base_ref, expand_ref, table_ref, send_ref, out_ref):
@@ -278,9 +289,9 @@
     count = own_ref.shape[0]
     core, side = lax.axis_index("core"), lax.axis_index("side")
     rows = width * boxes
-    high = (terms // LANES) * band + rows
-    received = own_ref[:, high:, :].astype(FULL).reshape(-1, LANES).astype(HALF)
-    total = local_of((own_ref, other_ref), table_ref, received, width, boxes, band)
+    high = (terms // LANES) * band + rows // 2
+    sources = sources_of(own_ref[:, high:, :].astype(FULL))
+    total = local_of((own_ref, other_ref), table_ref, sources, band)
     local = jnp.where(core == 0, total, pltpu.roll(total, band, 1)).astype(HALF)
     image = far_of(local, expand_ref, side * (terms // 2)) + base_ref[...]
     half = image.astype(HALF)
@@ -331,9 +342,9 @@
     core, side = lax.axis_index("core"), lax.axis_index("side")
     rows = width * boxes
     blocks = parts_ref[:, :, rows:, :].astype(FULL)
-    received = (blocks[:, 0] + blocks[:, 1]).reshape(-1, LANES).astype(HALF)
+    sources = sources_of(blocks[:, 0] + blocks[:, 1])
     bands = (own_ref, other_ref, across_ref, corner_ref)
-    total = local_of(bands, table_ref, received, width, boxes, band)
+    total = local_of(bands, table_ref, sources, band)
     halves = [total[:, : 2 * band], total[:, 2 * band :]]
     halves = [jnp.where(core == 0, half, pltpu.roll(half, band, 1)) for half in halves]
     local = jnp.concatenate(
@@ -446,12 +457,12 @@
     slots, picks, kept, near, chosen, table = kernel(
         functools.partial(first_kernel, width),
         [
-            shape((count, low + rows + area, LANES), HALF),
+            shape((count, low + rows // 2 + area, LANES), HALF),
             shape((count * area, parts * rows), HALF),
             SLOT(expand.shape, HALF),
             SLOT(near_ops.shape, HALF),
             shape((near_ops.shape[0] * boxes, 3 * boxes), HALF),
-            shape((width * parts, count * boxes, count * area), HALF),
+            shape((-(-count // 8), rows, min(count, 8) * count * cap * width), HALF),
         ],
         rhs_field, expand, class_ops, send, near_ops, near_src, slot, label,
         fixed=8,
@@ -495,6 +506,7 @@
         SLOT((2 * count, 8, panels), FULL),
         bands, other, across, corner, images, kept, table, rest, field, rhs_field,
     )
+    sums, field_other = lax.optimization_barrier((sums, field_other))
     sums = lax.all_to_all(sums, ("box", "core"), 0, 0, tiled=True)
     return kernel(
         functools.partial(last_kernel, width),

time: 50.9 us -> 48.7 us (0.957)
  blocking collectives: 18.3 us -> 27.9 us
  waiting for transfers between devices: 14.9 us -> 8.49 us
  starting transfers between devices: 8.96 us -> 5.21 us
  Pallas kernels: 8.31 us -> 6.74 us
    all_to_all x0 -> x1, blocking collectives: none -> 10.1 us  [per_device(): sums = lax.all_to_all(sums, ('box', 'core'), 0, 0, tiled=True)]
    all_to_all x1 -> x0, waiting for transfers between devices: 5.61 us -> none  [per_device(): sums = lax.all_to_all(sums, ('box', 'core'), 0, 0, tiled=True)]
    all_to_all x1 -> x0, starting transfers between devices: 3.49 us -> none  [per_device(): sums = lax.all_to_all(sums, ('box', 'core'), 0, 0, tiled=True)]
    pallas_call x6, Pallas kernels: 8.31 us -> 6.74 us  [call(): pl.pallas_call(kernel, out_shape=outs, in_specs=[vmem] * held + [pl.Block...]
    ppermute x1, waiting for transfers between devices: 0.92 us -> 0.08 us  [per_device(): field_other = lax.ppermute(field, 'core', swap)]
    all_to_all x1, blocking collectives: 18.3 us -> 17.7 us  [per_device(): own = lax.all_to_all(slots, 'box', 0, 0, tiled=True)]
    all_to_all x1, waiting for transfers between devices: 7.69 us -> 7.16 us  [per_device(): images = lax.all_to_all(images, ('box', 'side'), 0, 0, tiled=True)]
    ppermute x1, waiting for transfers between devices: 0.72 us -> 1.25 us  [per_device(): across = lax.ppermute(bands, 'side', swap)]
  transfers between devices with their start and end apart: 6 -> 5, of which waited for: 4 -> 3; matrix products, arithmetic and copies ran while one was open for 0% -> 0% of each run, Pallas kernels for 7% -> 8%
where the time goes in v3:
time: 48.7 us; the launch traced here: 48.4 us
  blocking collectives  27.9 us (57%)
  waiting for transfers between devices  8.49 us (17%)
  Pallas kernels  6.74 us (14%)
  starting transfers between devices  5.21 us (11%)
    all_to_all x1, blocking collectives, per_device(): own = lax.all_to_all(slots, 'box', 0, 0, tiled=True)  17.7 us
    all_to_all x1, blocking collectives, per_device(): sums = lax.all_to_all(sums, ('box', 'core'), 0, 0, tiled=True)  10.1 us
    all_to_all x1, waiting for transfers between devices, per_device(): images = lax.all_to_all(images, ('box', 'side'), 0, 0, tiled=True)  7.16 us
    pallas_call x6, Pallas kernels, call(): pl.pallas_call(kernel, out_shape=outs, in_specs=[vmem] * held + [pl.Block...  6.74 us
    all_to_all x1, starting transfers between devices, per_device(): images = lax.all_to_all(images, ('box', 'side'), 0, 0, tiled=True)  3.52 us
    ppermute x1, starting transfers between devices, per_device(): across = lax.ppermute(bands, 'side', swap)  1.55 us
    ppermute x1, waiting for transfers between devices, per_device(): across = lax.ppermute(bands, 'side', swap)  1.25 us
  transfers between devices with their start and end apart: 5, of which 3 were waited for; matrix products, arithmetic and copies ran while one was open for 0% of the time, Pallas kernels for 8%

profile of v3, /device:TPU:0, one launch (start us, length us, event | category | flops | bytes accessed | tf_op | source)
XLA Modules:
  0.0 48.4 jit_solution(9693146492839855412)
XLA Ops:
  0.0 2.1 %shard_map.91 = (bf16[8,152,128]{2,1,0:T(8,128)(2,1)S(1)}, bf16[64,64]{1,0:T(8,128)(2,1)S(1)}, bf16[16,256,128]{2,1,0:T(8,128)(2,1)S(1)}, bf16[26,128,128]{2,1,0...) custom-call(f32[4,16,128]{2,1,0:T(8,128)} %rhs_ref.5, bf16[16,256,128]{2,1,0:T(8,128)(2,1)} %expand_hbm.1, ...), custom_call_target="tpu_custom_call" | custom-call | tf_op jit(solution)/shard_map/pallas_call | solution.py:427
  2.1 17.7 %all_to_all.15.own_ref = bf16[8,152,128]{2,1,0:T(8,128)(2,1)S(1)} all-to-all(bf16[8,152,128]{2,1,0:T(8,128)(2,1)S(1)} %get-tuple-element.15), channel_id=1, replica_groups=mesh['box'=8,'side'=2,'core'=2] {'box'}, dimensions={0} | all-to-all | bytes 622592 | tf_op jit(solution)/shard_map/all_to_all | solution.py:480
  19.8 0.0 copy-start
  19.8 0.0 copy-start.1
  19.8 0.1 collective-permute-start
  19.9 1.6 %collective-permute-start.1 = (bf16[8,128,128]{2,1,0:T(8,128)(2,1)S(1)}, bf16[8,128,128]{2,1,0:T(8,128)(2,1)S(1)}, u32[]{:S(2)}, u32[]{:S(2)}) collective-permute-start(bf16[8,128,128]{2,1,0:T(8,128)(2,1)S(1)} %slice.4.own_ref), channel_id=1, source_target_pairs={{0,2},{2,0},{1,3},{3,1},{4,6},{6,4},{5,7},{7,5},{8,10},{10,8},{9,1... | collective-permute-start | bytes 786440 | tf_op jit(solution)/shard_map/ppermute | solution.py:483
  21.4 0.0 copy-done
  21.4 0.0 copy-done.1
  21.4 0.5 %shard_map.92.base_ref = f32[32,128]{1,0:T(8,128)S(1)} custom-call(bf16[8,152,128]{2,1,0:T(8,128)(2,1)S(1)} %all_to_all.15.own_ref, f32[4,16,128]{2,1,0:T(8,128)S(1)} %copy-done, f32[16,128]{1,0:T(8,128)S(1)} %copy-done.1, bf16[26,128,128]{2,1,0:T(8,128)(2,1)S(1)} %get-tuple-element.16.near_ref, bf16[416,48]{1,0:T(8,128)(2,1)S(1)} %get-tuple-element.17.chosen_ref), custom_call_target="tpu_custom_call" | custom-call | flops 1000000000 | tf_op jit(solution)/shard_map/pallas_call | solution.py:427
  21.9 0.0 collective-permute-done.other_ref
  21.9 1.9 %shard_map.93 = bf16[8,2,40,128]{3,2,1,0:T(8,128)(2,1)} custom-call(bf16[8,152,128]{2,1,0:T(8,128)(2,1)S(1)} %all_to_all.15.own_ref, bf16[8,128,128]{2,1,0:T(8,128)(2,1)S(1)} %collective-permute-done.other_ref, f32[32,128]{1,0:T(8,128)S(1)} %shard_map.92.base_ref, bf16[16,256,128]{2,1,0:T(8,128)(2,1)S(1)} %get-tuple-element.18.expand_ref, ...), custom_call_target="tpu_custom_call" | custom-call | tf_op jit(solution)/shard_map/pallas_call | solution.py:427
  23.8 3.5 %all-to-all-start.1 = ((bf16[16,40,128]{2,1,0:T(8,128)(2,1)}), bf16[16,40,128]{2,1,0:T(8,128)(2,1)S(1)}, u32[]{:S(2)}, u32[]{:S(2)}) async-start(bf16[16,40,128]{2,1,0:T(8,128)(2,1)} %bitcast.4), calls=%async_computation.1 | async-start | bytes 327680 | tf_op jit(solution)/shard_map/all_to_all | solution.py:496
  27.3 1.2 %collective-permute-done.1.across_ref = bf16[8,128,128]{2,1,0:T(8,128)(2,1)S(1)} collective-permute-done((bf16[8,128,128]{2,1,0:T(8,128)(2,1)S(1)}, bf16[8,128,128]{2,1,0:T(8,128)(2,1)S(1)}, u32[]{:S(2)}, u32[]{:S(2)}) %collective-permute-start.1) | collective-permute-done | bytes 262176 | tf_op jit(solution)/shard_map/ppermute | solution.py:483
  28.6 0.0 collective-permute-start.2
  28.6 7.2 %all-to-all-done.1 = bf16[16,40,128]{2,1,0:T(8,128)(2,1)S(1)} async-done(((bf16[16,40,128]{2,1,0:T(8,128)(2,1)}), bf16[16,40,128]{2,1,0:T(8,128)(2,1)S(1)}, u32[]{:S(2)}, u32[]{:S(2)}) %all-to-all-start.1) | async-done | bytes 163872 | tf_op jit(solution)/shard_map/all_to_all | solution.py:496
  35.8 0.5 %shard_map.94 = (f32[32,128]{1,0:T(8,128)S(1)}, f32[32,128]{1,0:T(8,128)S(1)}) custom-call(bf16[8,2,40,128]{3,2,1,0:T(8,128)(2,1)S(1)} %bitcast.7, f32[16,128]{1,0:T(8,128)S(1)} %copy-done.1, bf16[26,128,128]{2,1,0:T(8,128)(2,1)S(1)} %get-tuple-element.16.near_ref, bf16[416,48]{1,0:T(8,128)(2,1)S(1)} %get-tuple-element.17.chosen_ref), custom_call_target="tpu_custom_call" | custom-call | flops 1000000000 | tf_op jit(solution)/shard_map/pallas_call | solution.py:427
  36.2 0.1 collective-permute-start.3
  36.3 0.0 collective-permute-done.2.corner_ref
  36.3 1.1 %shard_map.95 = f32[16,8,128]{2,1,0:T(8,128)S(1)} custom-call(bf16[8,128,128]{2,1,0:T(8,128)(2,1)S(1)} %slice.4.own_ref, bf16[8,128,128]{2,1,0:T(8,128)(2,1)S(1)} %collective-permute-done.other_ref, bf16[8,128,128]{2,1,0:T(8,128)(2,1)S(1)} %collective-permute-done.1.across_ref, bf16[8,128,128]{2,1,0:T(8,128)(2,1)S(1)} %collective-permute-done.2.corner_ref, ...), custom_call_target="tpu_custom_call" | custom-call | tf_op jit(solution)/shard_map/pallas_call | solution.py:427
  37.4 0.1 collective-permute-done.3.other_ref
  37.5 10.1 %all_to_all.16.sums_ref = f32[16,8,128]{2,1,0:T(8,128)S(1)} all-to-all(f32[16,8,128]{2,1,0:T(8,128)S(1)} %shard_map.95), channel_id=1, replica_groups=mesh['box'=8,'side'=2,'core'=2] {'box','core'}, dimensions={0} | all-to-all | bytes 131072 | tf_op jit(solution)/shard_map/all_to_all | solution.py:510
  47.6 0.7 %shard_map.96 = f32[4,16,128]{2,1,0:T(8,128)} custom-call(f32[16,8,128]{2,1,0:T(8,128)S(1)} %all_to_all.16.sums_ref, f32[32,128]{1,0:T(8,128)S(1)} %get-tuple-element.22.field_ref, f32[32,128]{1,0:T(8,128)S(1)} %collective-permute-done.3.other_ref, f32[4,16,128]{2,1,0:T(8,128)S(1)} %copy-done), custom_call_target="tpu_custom_call" | custom-call | tf_op jit(solution)/shard_map/pallas_call | solution.py:427
  (1 shorter events, 0.0 us)
Async XLA Ops:
  19.8 1.7 %copy-start = (f32[4,16,128]{2,1,0:T(8,128)S(1)}, f32[4,16,128]{2,1,0:T(8,128)}, u32[]{:S(2)}) copy-start(f32[4,16,128]{2,1,0:T(8,128)} %rhs_ref.5) | copy-start | bytes 98308
  19.8 1.7 %copy-start.1 = (f32[16,128]{1,0:T(8,128)S(1)}, f32[16,128]{1,0:T(8,128)}, u32[]{:S(2)}) copy-start(f32[16,128]{1,0:T(8,128)} %self_ref.3) | copy-start | bytes 24580
  19.8 2.1 %collective-permute-start = (bf16[8,128,128]{2,1,0:T(8,128)(2,1)S(1)}, bf16[8,128,128]{2,1,0:T(8,128)(2,1)S(1)}, u32[]{:S(2)}, u32[]{:S(2)}) collective-permute-start(bf16[8,128,128]{2,1,0:T(8,128)(2,1)S(1)} %slice.4.own_ref), channel_id=1, source_target_pairs={{0,1},{1,0},{2,3},{3,2},{4,5},{5,4},{6,7},{7,6},{8,9},{9,8},{10,11... | collective-permute-start | bytes 786440 | tf_op jit(solution)/shard_map/ppermute | solution.py:482
  19.9 8.7 %collective-permute-start.1 = (bf16[8,128,128]{2,1,0:T(8,128)(2,1)S(1)}, bf16[8,128,128]{2,1,0:T(8,128)(2,1)S(1)}, u32[]{:S(2)}, u32[]{:S(2)}) collective-permute-start(bf16[8,128,128]{2,1,0:T(8,128)(2,1)S(1)} %slice.4.own_ref), channel_id=1, source_target_pairs={{0,2},{2,0},{1,3},{3,1},{4,6},{6,4},{5,7},{7,5},{8,10},{10,8},{9,1... | collective-permute-start | bytes 786440 | tf_op jit(solution)/shard_map/ppermute | solution.py:483
  23.8 11.9 %all-to-all-start.1 = ((bf16[16,40,128]{2,1,0:T(8,128)(2,1)}), bf16[16,40,128]{2,1,0:T(8,128)(2,1)S(1)}, u32[]{:S(2)}, u32[]{:S(2)}) async-start(bf16[16,40,128]{2,1,0:T(8,128)(2,1)} %bitcast.4), calls=%async_computation.1 | async-start | bytes 327680 | tf_op jit(solution)/shard_map/all_to_all | solution.py:496
  28.6 7.7 %collective-permute-start.2 = (bf16[8,128,128]{2,1,0:T(8,128)(2,1)S(1)}, bf16[8,128,128]{2,1,0:T(8,128)(2,1)S(1)}, u32[]{:S(2)}, u32[]{:S(2)}) collective-permute-start(bf16[8,128,128]{2,1,0:T(8,128)(2,1)S(1)} %collective-permute-done.1.across_ref), channel_id=1, source_target_pairs={{0,1},{1,0},{2,3},{3,2},{4,5},{5,4},{6,7},{7,6},{8,9},{9,8},{10,11... | collective-permute-start | bytes 786440 | tf_op jit(solution)/shard_map/ppermute | solution.py:484
  36.2 1.2 %collective-permute-start.3 = (f32[32,128]{1,0:T(8,128)S(1)}, f32[32,128]{1,0:T(8,128)S(1)}, u32[]{:S(2)}, u32[]{:S(2)}) collective-permute-start(f32[32,128]{1,0:T(8,128)S(1)} %get-tuple-element.22.field_ref), channel_id=1, source_target_pairs={{0,1},{1,0},{2,3},{3,2},{4,5},{5,4},{6,7},{7,6},{8,9},{9,8},{10,11... | collective-permute-start | bytes 49160 | tf_op jit(solution)/shard_map/ppermute | solution.py:503

commit v4 on v3

--- a/solution.py
+++ b/solution.py
@@ -12,6 +12,25 @@
 HALF = jnp.bfloat16
 FULL = jnp.float32
 SLOT = pltpu.VMEM
+FIRST = {8: (2, 4, 6, 0, 5, 1, 7, 3)}
+SECOND = {16: (10, 3, 8, 6, 15, 4, 13, 14, 12, 11, 9, 7, 2, 1, 0, 5)}
+THIRD = {16: (7, 9, 3, 14, 4, 12, 13, 10, 1, 8, 11, 2, 15, 6, 5, 0)}
+
+
+def spot(order, member):
+    if order is None:
+        return member
+    if isinstance(member, int):
+        return order.index(member)
+    result = jnp.zeros_like(member)
+    for number, value in enumerate(order):
+        result = jnp.where(member == value, number, result)
+    return result
+
+
+def exchange(value, axes, order):
+    groups = None if order is None else [list(order)]
+    return lax.all_to_all(value, axes, 0, 0, tiled=True, axis_index_groups=groups)
 
 
 def each(count, body):
@@ -51,7 +70,7 @@
     return result
 
 
-def send_table(send_ref, out_ref, boxes, width, parts):
+def send_table(order, send_ref, out_ref, boxes, width, parts):
     cap, targets = send_ref.shape
     area = out_ref.shape[0] // targets
     row = lax.broadcasted_iota(jnp.int32, (area, out_ref.shape[1]), 0)
@@ -62,7 +81,9 @@
         place = start
         for turn in range(cap):
             place = jnp.where(row % cap == turn, start + send_ref[turn, target], place)
-        begin = target * area if isinstance(target, int) else pl.multiple_of(target * area, area)
+        begin = spot(order, target) * area
+        if not isinstance(target, int):
+            begin = pl.multiple_of(begin, area)
         out_ref[pl.ds(begin, area), :] = jnp.where(place == column, 1.0, 0.0)
 
     each(targets, put)
@@ -116,7 +137,7 @@
     return jnp.concatenate([first, second], axis=1).astype(HALF)
 
 
-def local_of(bands, table_ref, sources, band):
+def local_of(order, bands, table_ref, sources, band):
     classes = bands[0].shape[0]
     group = classes // table_ref.shape[0]
     parts = sources.shape[1] // LANES
@@ -126,7 +147,10 @@
         for turn in range(group):
             right = [
                 jnp.concatenate(
-                    [ref[number * group + turn, part * band : (part + 1) * band, :] for part in range(parts)],
+                    [
+                        ref[spot(order, number * group + turn), part * band : (part + 1) * band, :]
+                        for part in range(parts)
+                    ],
                     axis=1,
                 )
                 for ref in bands
@@ -170,11 +194,11 @@
         chosen_ref[number * boxes : (number + 1) * boxes, :] = jnp.where(match, 1.0, 0.0).astype(HALF)
 
 
-def list_table(cap, width, kinds, slot_ref, label_ref, table_ref):
+def list_table(order, cap, width, kinds, slot_ref, label_ref, table_ref):
     boxes = slot_ref.shape[1]
     groups, rows, columns = table_ref.shape
     slots, labels = slot_ref[...], label_ref[...]
-    places = (slots // cap) * (cap * width) + slots % cap
+    places = spot(order, slots // cap) * (cap * width) + slots % cap
     group = kinds // groups
     received = columns // group
 
@@ -191,6 +215,7 @@
 
 
 def first_kernel(
+    order,
     width,
     rhs_hbm,
     expand_hbm,
@@ -232,7 +257,7 @@
     pairs.append((near_hbm, near_ref))
     copies = fetch(pairs, signals)
     copies[0].wait()
-    send_table(send_ref, wide_ref, boxes, width, terms // LANES)
+    send_table(order, send_ref, wide_ref, boxes, width, terms // LANES)
     picks_ref[...] = wide_ref[...].astype(HALF)
     band = class_ref.shape[1]
     low = (terms // LANES) * band
@@ -246,14 +271,15 @@
     )
 
     def put(target):
-        out_ref[target, :low, :] = operators
-        out_ref[target, low:high, :] = shown
+        place = spot(order, target)
+        out_ref[place, :low, :] = operators
+        out_ref[place, low:high, :] = shown
 
     each(out_ref.shape[0], put)
     for copy in copies[3:6]:
         copy.wait()
     near_table(source_ref, chosen_ref)
-    list_table(send_ref.shape[0], width, out_ref.shape[0], slot_ref, label_ref, table_ref)
+    list_table(order, send_ref.shape[0], width, out_ref.shape[0], slot_ref, label_ref, table_ref)
     result = jnp.zeros((width * boxes, terms), FULL)
     for box in range(boxes):
         if box % step == 0:
@@ -264,7 +290,7 @@
     copies[10].wait()
 
 
-def base_kernel(width, low, own_ref, rhs_ref, self_ref, near_ref, chosen_ref, out_ref):
+def base_of(order, width, low, own_ref, rhs_ref, self_ref, near_ref, chosen_ref):
     boxes, panels = self_ref.shape
     count = own_ref.shape[0]
     core, side, index = lax.axis_index("core"), lax.axis_index("side"), lax.axis_index("box")
@@ -272,7 +298,7 @@
     empty = jnp.zeros((half, panels), FULL)
     pieces = []
     for step in (-1, 0, 1):
-        shown = own_ref[jnp.clip(index + step, 0, count - 1), low : low + width * half, :].astype(FULL)
+        shown = own_ref[spot(order, jnp.clip(index + step, 0, count - 1)), low : low + width * half, :].astype(FULL)
         rows = []
         for rhs in range(width):
             part = shown[rhs * half : (rhs + 1) * half]
@@ -281,49 +307,76 @@
     near = near_of(near_ref, chosen_ref, extended_of(pieces, index, count, boxes), boxes, width)
     field = rhs_ref[pl.ds(core * width, width)]
     diagonal = ((self_ref[...] - SHIFT)[None] * field).reshape(width * boxes, panels)
-    out_ref[...] = near + jnp.where(side == 0, diagonal, 0.0)
-
-
-def second_kernel(width, band, own_ref, other_ref, base_ref, expand_ref, table_ref, send_ref, out_ref):
+    return near + jnp.where(side == 0, diagonal, 0.0)
+
+
+def second_kernel(
+    first,
+    second,
+    width,
+    band,
+    own_ref,
+    other_ref,
+    rhs_ref,
+    self_ref,
+    near_ref,
+    chosen_ref,
+    expand_ref,
+    table_ref,
+    send_ref,
+    out_ref,
+):
     boxes, terms, panels = expand_ref.shape
     count = own_ref.shape[0]
     core, side = lax.axis_index("core"), lax.axis_index("side")
     rows = width * boxes
     high = (terms // LANES) * band + rows // 2
     sources = sources_of(own_ref[:, high:, :].astype(FULL))
-    total = local_of((own_ref, other_ref), table_ref, sources, band)
+    total = local_of(first, (own_ref, other_ref), table_ref, sources, band)
     local = jnp.where(core == 0, total, pltpu.roll(total, band, 1)).astype(HALF)
-    image = far_of(local, expand_ref, side * (terms // 2)) + base_ref[...]
+    base = base_of(first, width, (terms // LANES) * band, own_ref, rhs_ref, self_ref, near_ref, chosen_ref)
+    image = far_of(local, expand_ref, side * (terms // 2)) + base
     half = image.astype(HALF)
     sent = sent_of(multipoles_of(half, expand_ref), send_ref[...]).astype(HALF).reshape(count, -1, LANES)
-    for part in range(2):
-        out_ref[:, part, rows:, :] = sent
 
     def put(target):
         for part in range(2):
-            out_ref[target, part, :rows, :] = half
-
-    each(count, put)
-
-
-def rest_kernel(width, parts_ref, self_ref, near_ref, chosen_ref, rest_ref, field_ref):
+            place = spot(second, 2 * target + part)
+            out_ref[place, :rows, :] = half
+            out_ref[place, rows:, :] = sent[spot(first, target)]
+
+    if second is None:
+        out_ref[...] = jnp.concatenate(
+            [jnp.broadcast_to(half[None, None], (count, 2, rows, LANES)), jnp.stack([sent, sent], axis=1)], axis=2
+        ).reshape(out_ref.shape)
+    else:
+        each(count, put)
+
+
+def joined(order, parts_ref, place):
+    first, second = spot(order, 2 * place), spot(order, 2 * place + 1)
+    return parts_ref[first].astype(FULL) + parts_ref[second].astype(FULL)
+
+
+def field_kernel(order, parts_ref, out_ref):
+    out_ref[...] = joined(order, parts_ref, lax.axis_index("box"))[: out_ref.shape[0]]
+
+
+def rest_of(order, width, parts_ref, self_ref, near_ref, chosen_ref):
     boxes, panels = self_ref.shape
-    count = parts_ref.shape[0]
+    count = parts_ref.shape[0] // 2
     index = lax.axis_index("box")
     rows = width * boxes
-
-    def joined(place):
-        return parts_ref[place, 0, :rows, :].astype(FULL) + parts_ref[place, 1, :rows, :].astype(FULL)
-
-    pieces = [joined(jnp.clip(index + step, 0, count - 1)) for step in (-1, 0, 1)]
+    pieces = [joined(order, parts_ref, jnp.clip(index + step, 0, count - 1))[:rows] for step in (-1, 0, 1)]
     near = near_of(near_ref, chosen_ref, extended_of(pieces, index, count, boxes), boxes, width)
     field = pieces[1]
     diagonal = ((self_ref[...] - SHIFT)[None] * field.reshape(width, boxes, panels)).reshape(rows, panels)
-    rest_ref[...] = near + diagonal
-    field_ref[...] = field
+    return near + diagonal
 
 
 def third_kernel(
+    first,
+    second,
     width,
     band,
     own_ref,
@@ -333,7 +386,9 @@
     parts_ref,
     expand_ref,
     table_ref,
-    rest_ref,
+    self_ref,
+    near_ref,
+    chosen_ref,
     field_ref,
     rhs_ref,
     out_ref,
@@ -341,16 +396,21 @@
     boxes, terms, panels = expand_ref.shape
     core, side = lax.axis_index("core"), lax.axis_index("side")
     rows = width * boxes
-    blocks = parts_ref[:, :, rows:, :].astype(FULL)
-    sources = sources_of(blocks[:, 0] + blocks[:, 1])
+    count = parts_ref.shape[0] // 2
+    if second is None:
+        blocks = parts_ref[:, rows:, :].astype(FULL).reshape(count, 2, -1, LANES)
+        blocks = blocks[:, 0] + blocks[:, 1]
+    else:
+        blocks = jnp.stack([joined(second, parts_ref, place)[rows:] for place in first])
+    sources = sources_of(blocks)
     bands = (own_ref, other_ref, across_ref, corner_ref)
-    total = local_of(bands, table_ref, sources, band)
+    total = local_of(first, bands, table_ref, sources, band)
     halves = [total[:, : 2 * band], total[:, 2 * band :]]
     halves = [jnp.where(core == 0, half, pltpu.roll(half, band, 1)) for half in halves]
     local = jnp.concatenate(
         [jnp.where(side == 0, halves[0], halves[1]), jnp.where(side == 0, halves[1], halves[0])], axis=1
     ).astype(HALF)
-    last = rest_ref[...] + far_of(local, expand_ref, 0)
+    last = rest_of(second, width, parts_ref, self_ref, near_ref, chosen_ref) + far_of(local, expand_ref, 0)
     field = field_ref[...]
     right = rhs_ref[pl.ds(core * width, width)].reshape(rows, panels)
     spots = lax.broadcasted_iota(jnp.int32, (8, panels), 0)
@@ -370,7 +430,7 @@
     each(out_ref.shape[0], put)
 
 
-def last_kernel(width, sums_ref, field_ref, other_ref, rhs_ref, out_ref):
+def last_kernel(order, width, sums_ref, field_ref, other_ref, rhs_ref, out_ref):
     core = lax.axis_index("core")
     rows, panels = field_ref.shape
     boxes = rows // width
@@ -380,7 +440,7 @@
     for group in range(2):
         total = fold(
             sums_ref.shape[0] // 2,
-            lambda number, state: state + sums_ref[2 * number + group],
+            lambda number, state: state + sums_ref[spot(order, 2 * number + group)],
             jnp.zeros(sums_ref.shape[1:], FULL),
         )
         rr, ru, uu, rw, uw, ww = (total[number : number + 1] for number in range(6))
@@ -448,6 +508,7 @@
     area = -(-(cap * width * parts) // 8) * 8
     low = parts * band
     swap = [(0, 1), (1, 0)]
+    first, second, third = FIRST.get(count), SECOND.get(2 * count), THIRD.get(2 * count)
     shape = jax.ShapeDtypeStruct
     send = jnp.swapaxes(send_rows, 1, 2)[0]
     slot, label = list_slot.T, list_class.T
@@ -455,7 +516,7 @@
     kernel = functools.partial(call, limit=16 if count <= 16 else 56)
 
     slots, picks, kept, near, chosen, table = kernel(
-        functools.partial(first_kernel, width),
+        functools.partial(first_kernel, first, width),
         [
             shape((count, low + rows // 2 + area, LANES), HALF),
             shape((count * area, parts * rows), HALF),
@@ -477,39 +538,28 @@
             pltpu.SemaphoreType.DMA((11,)),
         ],
     )
-    own = lax.all_to_all(slots, "box", 0, 0, tiled=True)
+    own = exchange(slots, "box", first)
     bands = own[:, :low]
     other = lax.ppermute(bands, "core", swap)
     across = lax.ppermute(bands, "side", swap)
     corner = lax.ppermute(across, "core", swap)
-    base = kernel(
-        functools.partial(base_kernel, width, low), block,
-        own, rhs_field, self_coef, near, chosen,
-        flops=1_000_000_000,
+    images = kernel(
+        functools.partial(second_kernel, first, second, width, band),
+        shape((2 * count, rows + area, LANES), HALF),
+        own, other, rhs_field, self_coef, near, chosen, kept, table, picks,
     )
-    images = kernel(
-        functools.partial(second_kernel, width, band),
-        shape((count, 2, rows + area, LANES), HALF),
-        own, other, base, kept, table, picks,
-    )
-    images = images.reshape((2 * count,) + images.shape[2:])
-    images = lax.all_to_all(images, ("box", "side"), 0, 0, tiled=True)
-    images = images.reshape((count, 2) + images.shape[1:])
-    rest, field = kernel(
-        functools.partial(rest_kernel, width), [block, block],
-        images, self_coef, near, chosen,
-        flops=1_000_000_000,
-    )
+    images = exchange(images, ("box", "side"), second)
+    field = kernel(functools.partial(field_kernel, second), block, images)
     field_other = lax.ppermute(field, "core", swap)
     sums = kernel(
-        functools.partial(third_kernel, width, band),
+        functools.partial(third_kernel, first, second, width, band),
         SLOT((2 * count, 8, panels), FULL),
-        bands, other, across, corner, images, kept, table, rest, field, rhs_field,
+        bands, other, across, corner, images, kept, table, self_coef, near, chosen, field, rhs_field,
     )
     sums, field_other = lax.optimization_barrier((sums, field_other))
-    sums = lax.all_to_all(sums, ("box", "core"), 0, 0, tiled=True)
+    sums = exchange(sums, ("box", "core"), third)
     return kernel(
-        functools.partial(last_kernel, width),
+        functools.partial(last_kernel, third, width),
         shape(rhs_field.shape, FULL),
         sums, field, field_other, rhs_field,
     )

time: 48.7 us -> 45.6 us (0.936)
  waiting for transfers between devices: 8.49 us -> 5 us
  starting transfers between devices: 5.21 us -> 7.71 us
  blocking collectives: 27.9 us -> 26.5 us
  Pallas kernels: 6.74 us -> 5.98 us
    all_to_all x1, starting transfers between devices: 3.52 us -> 6.01 us  [exchange(): lax.all_to_all(value, axes, 0, 0, tiled=True, axis_index_groups=groups)]
    all_to_all x1, waiting for transfers between devices: 7.16 us -> 4.98 us  [exchange(): lax.all_to_all(value, axes, 0, 0, tiled=True, axis_index_groups=groups)]
    all_to_all x2, blocking collectives: 27.9 us -> 26.5 us  [exchange(): lax.all_to_all(value, axes, 0, 0, tiled=True, axis_index_groups=groups)]
    ppermute x1, waiting for transfers between devices: 1.25 us -> 0.01 us  [per_device(): across = lax.ppermute(bands, 'side', swap)]
    pallas_call x6 -> x5, Pallas kernels: 6.74 us -> 5.98 us  [call(): pl.pallas_call(kernel, out_shape=outs, in_specs=[vmem] * held + [pl.Block...]
  transfers between devices with their start and end apart: 5 -> 5, of which waited for: 3 -> 1; matrix products, arithmetic and copies ran while one was open for 0% -> 0% of each run, Pallas kernels for 8% -> 7%
where the time goes in v4:
time: 45.6 us; the launch traced here: 45.3 us
  blocking collectives  26.5 us (58%)
  starting transfers between devices  7.71 us (17%)
  Pallas kernels  5.98 us (13%)
  waiting for transfers between devices  5 us (11%)
    all_to_all x2, blocking collectives, exchange(): lax.all_to_all(value, axes, 0, 0, tiled=True, axis_index_groups=groups)  26.5 us
    all_to_all x1, starting transfers between devices, exchange(): lax.all_to_all(value, axes, 0, 0, tiled=True, axis_index_groups=groups)  6.01 us
    pallas_call x5, Pallas kernels, call(): pl.pallas_call(kernel, out_shape=outs, in_specs=[vmem] * held + [pl.Block...  5.98 us
    all_to_all x1, waiting for transfers between devices, exchange(): lax.all_to_all(value, axes, 0, 0, tiled=True, axis_index_groups=groups)  4.98 us
    ppermute x1, starting transfers between devices, per_device(): across = lax.ppermute(bands, 'side', swap)  1.55 us
  transfers between devices with their start and end apart: 5, of which 1 were waited for; matrix products, arithmetic and copies ran while one was open for 0% of the time, Pallas kernels for 7%

profile of v4, /device:TPU:0, one launch (start us, length us, event | category | flops | bytes accessed | tf_op | source)
XLA Modules:
  0.0 45.3 jit_solution(6371392218755809151)
XLA Ops:
  0.0 2.1 %shard_map.91 = (bf16[8,152,128]{2,1,0:T(8,128)(2,1)S(1)}, bf16[64,64]{1,0:T(8,128)(2,1)S(1)}, bf16[16,256,128]{2,1,0:T(8,128)(2,1)S(1)}, bf16[26,128,128]{2,1,0...) custom-call(f32[4,16,128]{2,1,0:T(8,128)} %rhs_ref.5, bf16[16,256,128]{2,1,0:T(8,128)(2,1)} %expand_hbm.1, ...), custom_call_target="tpu_custom_call" | custom-call | tf_op jit(solution)/shard_map/pallas_call | solution.py:487
  2.1 16.8 %all_to_all.15.own_ref = bf16[8,152,128]{2,1,0:T(8,128)(2,1)S(1)} all-to-all(bf16[8,152,128]{2,1,0:T(8,128)(2,1)S(1)} %get-tuple-element.13), channel_id=1, replica_groups={{8,16,24,0,20,4,28,12},{9,17,25,1,21,5,29,13},{10,18,26,2,22,6,30,14},{..., dimensions={0} | all-to-all | bytes 622592 | tf_op jit(solution)/shard_map/all_to_all | solution.py:33
  18.9 0.0 copy-start
  18.9 0.0 copy-start.1
  18.9 0.1 collective-permute-start
  19.0 1.6 %collective-permute-start.1 = (bf16[8,128,128]{2,1,0:T(8,128)(2,1)S(1)}, bf16[8,128,128]{2,1,0:T(8,128)(2,1)S(1)}, u32[]{:S(2)}, u32[]{:S(2)}) collective-permute-start(bf16[8,128,128]{2,1,0:T(8,128)(2,1)S(1)} %slice.4.own_ref), channel_id=1, source_target_pairs={{0,2},{2,0},{1,3},{3,1},{4,6},{6,4},{5,7},{7,5},{8,10},{10,8},{9,1... | collective-permute-start | bytes 786440 | tf_op jit(solution)/shard_map/ppermute | solution.py:544
  20.5 0.0 collective-permute-done.other_ref
  20.5 0.0 copy-done
  20.5 0.0 copy-done.1
  20.5 2.0 %shard_map.92 = bf16[16,40,128]{2,1,0:T(8,128)(2,1)} custom-call(bf16[8,152,128]{2,1,0:T(8,128)(2,1)S(1)} %all_to_all.15.own_ref, bf16[8,128,128]{2,1,0:T(8,128)(2,1)S(1)} %collective-permute-done.other_ref, f32[4,16,128]{2,1,0:T(8,128)S(1)} %copy-done, f32[16,128]{1,0:T(8,128)S(1)} %copy-done.1, bf16[26,128,128]{2,1,0:T(8,128)(2,1)S(1)} %get-tuple-element.14.near_ref, ...), custom_call_target="tpu_custom_call" | custom-call | tf_op jit(solution)/shard_map/pallas_call | solution.py:487
  22.6 6.0 %all-to-all-start.1 = ((bf16[16,40,128]{2,1,0:T(8,128)(2,1)}), bf16[16,40,128]{2,1,0:T(8,128)(2,1)S(1)}, u32[]{:S(2)}, u32[]{:S(2)}) async-start(bf16[16,40,128]{2,1,0:T(8,128)(2,1)} %shard_map.92), calls=%async_computation.1 | async-start | bytes 327680 | tf_op jit(solution)/shard_map/all_to_all | solution.py:33
  28.6 0.0 collective-permute-done.1.across_ref
  28.6 0.1 collective-permute-start.2
  28.7 5.0 %all-to-all-done.1.parts_ref = bf16[16,40,128]{2,1,0:T(8,128)(2,1)S(1)} async-done(((bf16[16,40,128]{2,1,0:T(8,128)(2,1)}), bf16[16,40,128]{2,1,0:T(8,128)(2,1)S(1)}, u32[]{:S(2)}, u32[]{:S(2)}) %all-to-all-start.1) | async-done | bytes 163872 | tf_op jit(solution)/shard_map/all_to_all | solution.py:33
  33.7 0.0 collective-permute-start.3
  33.7 0.0 collective-permute-done.2.corner_ref
  33.7 1.1 %shard_map.94 = f32[16,8,128]{2,1,0:T(8,128)S(1)} custom-call(bf16[8,128,128]{2,1,0:T(8,128)(2,1)S(1)} %slice.4.own_ref, bf16[8,128,128]{2,1,0:T(8,128)(2,1)S(1)} %collective-permute-done.other_ref, bf16[8,128,128]{2,1,0:T(8,128)(2,1)S(1)} %collective-permute-done.1.across_ref, bf16[8,128,128]{2,1,0:T(8,128)(2,1)S(1)} %collective-permute-done.2.corner_ref, ...), custom_call_target="tpu_custom_call" | custom-call | tf_op jit(solution)/shard_map/pallas_call | solution.py:487
  34.8 0.0 collective-permute-done.3.other_ref
  34.8 9.7 %all_to_all.16.sums_ref = f32[16,8,128]{2,1,0:T(8,128)S(1)} all-to-all(f32[16,8,128]{2,1,0:T(8,128)S(1)} %shard_map.94), channel_id=1, replica_groups={{13,17,5,28,8,24,25,20,1,16,21,4,29,12,9,0},{15,19,7,30,10,26,27,22,3,1..., dimensions={0} | all-to-all | bytes 131072 | tf_op jit(solution)/shard_map/all_to_all | solution.py:33
  44.6 0.7 %shard_map.95 = f32[4,16,128]{2,1,0:T(8,128)} custom-call(f32[16,8,128]{2,1,0:T(8,128)S(1)} %all_to_all.16.sums_ref, f32[32,128]{1,0:T(8,128)S(1)} %shard_map.93.field_ref, f32[32,128]{1,0:T(8,128)S(1)} %collective-permute-done.3.other_ref, f32[4,16,128]{2,1,0:T(8,128)S(1)} %copy-done), custom_call_target="tpu_custom_call" | custom-call | tf_op jit(solution)/shard_map/pallas_call | solution.py:487
  (2 shorter events, 0.0 us)
Async XLA Ops:
  18.9 1.7 %copy-start = (f32[4,16,128]{2,1,0:T(8,128)S(1)}, f32[4,16,128]{2,1,0:T(8,128)}, u32[]{:S(2)}) copy-start(f32[4,16,128]{2,1,0:T(8,128)} %rhs_ref.5) | copy-start | bytes 98308
  18.9 1.7 %copy-start.1 = (f32[16,128]{1,0:T(8,128)S(1)}, f32[16,128]{1,0:T(8,128)}, u32[]{:S(2)}) copy-start(f32[16,128]{1,0:T(8,128)} %self_ref.3) | copy-start | bytes 24580
  18.9 1.6 %collective-permute-start = (bf16[8,128,128]{2,1,0:T(8,128)(2,1)S(1)}, bf16[8,128,128]{2,1,0:T(8,128)(2,1)S(1)}, u32[]{:S(2)}, u32[]{:S(2)}) collective-permute-start(bf16[8,128,128]{2,1,0:T(8,128)(2,1)S(1)} %slice.4.own_ref), channel_id=1, source_target_pairs={{0,1},{1,0},{2,3},{3,2},{4,5},{5,4},{6,7},{7,6},{8,9},{9,8},{10,11... | collective-permute-start | bytes 786440 | tf_op jit(solution)/shard_map/ppermute | solution.py:543
  19.0 9.6 %collective-permute-start.1 = (bf16[8,128,128]{2,1,0:T(8,128)(2,1)S(1)}, bf16[8,128,128]{2,1,0:T(8,128)(2,1)S(1)}, u32[]{:S(2)}, u32[]{:S(2)}) collective-permute-start(bf16[8,128,128]{2,1,0:T(8,128)(2,1)S(1)} %slice.4.own_ref), channel_id=1, source_target_pairs={{0,2},{2,0},{1,3},{3,1},{4,6},{6,4},{5,7},{7,5},{8,10},{10,8},{9,1... | collective-permute-start | bytes 786440 | tf_op jit(solution)/shard_map/ppermute | solution.py:544
  22.6 11.1 %all-to-all-start.1 = ((bf16[16,40,128]{2,1,0:T(8,128)(2,1)}), bf16[16,40,128]{2,1,0:T(8,128)(2,1)S(1)}, u32[]{:S(2)}, u32[]{:S(2)}) async-start(bf16[16,40,128]{2,1,0:T(8,128)(2,1)} %shard_map.92), calls=%async_computation.1 | async-start | bytes 327680 | tf_op jit(solution)/shard_map/all_to_all | solution.py:33
  28.6 5.1 %collective-permute-start.2 = (bf16[8,128,128]{2,1,0:T(8,128)(2,1)S(1)}, bf16[8,128,128]{2,1,0:T(8,128)(2,1)S(1)}, u32[]{:S(2)}, u32[]{:S(2)}) collective-permute-start(bf16[8,128,128]{2,1,0:T(8,128)(2,1)S(1)} %collective-permute-done.1.across_ref), channel_id=1, source_target_pairs={{0,1},{1,0},{2,3},{3,2},{4,5},{5,4},{6,7},{7,6},{8,9},{9,8},{10,11... | collective-permute-start | bytes 786440 | tf_op jit(solution)/shard_map/ppermute | solution.py:545
  33.7 1.2 %collective-permute-start.3 = (f32[32,128]{1,0:T(8,128)S(1)}, f32[32,128]{1,0:T(8,128)S(1)}, u32[]{:S(2)}, u32[]{:S(2)}) collective-permute-start(f32[32,128]{1,0:T(8,128)S(1)} %shard_map.93.field_ref), channel_id=1, source_target_pairs={{0,1},{1,0},{2,3},{3,2},{4,5},{5,4},{6,7},{7,6},{8,9},{9,8},{10,11... | collective-permute-start | bytes 49160 | tf_op jit(solution)/shard_map/ppermute | solution.py:553

commit v5 on v4

--- a/solution.py
+++ b/solution.py
@@ -12,9 +12,9 @@
 HALF = jnp.bfloat16
 FULL = jnp.float32
 SLOT = pltpu.VMEM
-FIRST = {8: (2, 4, 6, 0, 5, 1, 7, 3)}
-SECOND = {16: (10, 3, 8, 6, 15, 4, 13, 14, 12, 11, 9, 7, 2, 1, 0, 5)}
-THIRD = {16: (7, 9, 3, 14, 4, 12, 13, 10, 1, 8, 11, 2, 15, 6, 5, 0)}
+FIRST = {8: (5, 7, 0, 4, 6, 3, 1, 2)}
+SECOND = {16: (6, 0, 2, 1, 15, 3, 8, 7, 4, 11, 14, 9, 10, 13, 5, 12)}
+THIRD = {16: (11, 9, 13, 8, 14, 5, 7, 4, 12, 1, 15, 3, 0, 6, 2, 10)}
 
 
 def spot(order, member):
@@ -242,7 +242,7 @@
 ):
     boxes, terms, panels = expand_ref.shape
     core, side = lax.axis_index("core"), lax.axis_index("side")
-    step = boxes // 4
+    step = boxes // 2
     pairs = [
         (send_hbm, send_ref),
         (rhs_hbm.at[pl.ds(core * width, width)], rhs_ref),
@@ -251,8 +251,8 @@
         (slot_hbm, slot_ref),
         (label_hbm, label_ref),
     ]
-    for quarter in range(4):
-        part = pl.ds(quarter * step, step)
+    for chunk in range(2):
+        part = pl.ds(chunk * step, step)
         pairs.append((expand_hbm.at[part], expand_ref.at[part]))
     pairs.append((near_hbm, near_ref))
     copies = fetch(pairs, signals)
@@ -287,7 +287,7 @@
         result = own_rows(dot_nt(field, expand_ref[box]), result, box, boxes)
     sent = sent_of(result, picks_ref[...]).astype(HALF)
     out_ref[:, high:, :] = sent.reshape(out_ref.shape[0], -1, LANES)
-    copies[10].wait()
+    copies[8].wait()
 
 
 def base_of(order, width, low, own_ref, rhs_ref, self_ref, near_ref, chosen_ref):
@@ -535,7 +535,7 @@
             pltpu.VMEM(near_src.shape, jnp.int32),
             pltpu.VMEM(slot.shape, jnp.int32),
             pltpu.VMEM(label.shape, jnp.int32),
-            pltpu.SemaphoreType.DMA((11,)),
+            pltpu.SemaphoreType.DMA((9,)),
         ],
     )
     own = exchange(slots, "box", first)

time: 45.6 us -> 43.2 us (0.947)
  blocking collectives: 26.5 us -> 23 us
  waiting for transfers between devices: 5 us -> 6.24 us
    all_to_all x2, blocking collectives: 26.5 us -> 23 us  [exchange(): lax.all_to_all(value, axes, 0, 0, tiled=True, axis_index_groups=groups)]
    all_to_all x1, waiting for transfers between devices: 4.98 us -> 6.22 us  [exchange(): lax.all_to_all(value, axes, 0, 0, tiled=True, axis_index_groups=groups)]
where the time goes in v5:
time: 43.2 us; the launch traced here: 43 us
  blocking collectives  23 us (53%)
  starting transfers between devices  7.78 us (18%)
  waiting for transfers between devices  6.24 us (14%)
  Pallas kernels  5.83 us (13%)
    all_to_all x2, blocking collectives, exchange(): lax.all_to_all(value, axes, 0, 0, tiled=True, axis_index_groups=groups)  23 us
    all_to_all x1, waiting for transfers between devices, exchange(): lax.all_to_all(value, axes, 0, 0, tiled=True, axis_index_groups=groups)  6.22 us
    all_to_all x1, starting transfers between devices, exchange(): lax.all_to_all(value, axes, 0, 0, tiled=True, axis_index_groups=groups)  6.08 us
    pallas_call x5, Pallas kernels, call(): pl.pallas_call(kernel, out_shape=outs, in_specs=[vmem] * held + [pl.Block...  5.83 us
    ppermute x1, starting transfers between devices, per_device(): across = lax.ppermute(bands, 'side', swap)  1.56 us
  transfers between devices with their start and end apart: 5, of which 1 were waited for; matrix products, arithmetic and copies ran while one was open for 0% of the time, Pallas kernels for 7%

profile of v5, /device:TPU:0, one launch (start us, length us, event | category | flops | bytes accessed | tf_op | source)
XLA Modules:
  0.0 43.0 jit_solution(7057613399443795243)
XLA Ops:
  0.0 1.9 %shard_map.91 = (bf16[8,152,128]{2,1,0:T(8,128)(2,1)S(1)}, bf16[64,64]{1,0:T(8,128)(2,1)S(1)}, bf16[16,256,128]{2,1,0:T(8,128)(2,1)S(1)}, bf16[26,128,128]{2,1,0...) custom-call(f32[4,16,128]{2,1,0:T(8,128)} %rhs_ref.5, bf16[16,256,128]{2,1,0:T(8,128)(2,1)} %expand_hbm.1, ...), custom_call_target="tpu_custom_call" | custom-call | tf_op jit(solution)/shard_map/pallas_call | solution.py:487
  1.9 15.0 %all_to_all.15.own_ref = bf16[8,152,128]{2,1,0:T(8,128)(2,1)S(1)} all-to-all(bf16[8,152,128]{2,1,0:T(8,128)(2,1)S(1)} %get-tuple-element.13), channel_id=1, replica_groups={{20,28,0,16,24,12,4,8},{21,29,1,17,25,13,5,9},{22,30,2,18,26,14,6,10},{..., dimensions={0} | all-to-all | bytes 622592 | tf_op jit(solution)/shard_map/all_to_all | solution.py:33
  16.9 0.0 copy-start
  16.9 0.0 copy-start.1
  16.9 0.1 collective-permute-start
  17.0 1.6 %collective-permute-start.1 = (bf16[8,128,128]{2,1,0:T(8,128)(2,1)S(1)}, bf16[8,128,128]{2,1,0:T(8,128)(2,1)S(1)}, u32[]{:S(2)}, u32[]{:S(2)}) collective-permute-start(bf16[8,128,128]{2,1,0:T(8,128)(2,1)S(1)} %slice.4.own_ref), channel_id=1, source_target_pairs={{0,2},{2,0},{1,3},{3,1},{4,6},{6,4},{5,7},{7,5},{8,10},{10,8},{9,1... | collective-permute-start | bytes 786440 | tf_op jit(solution)/shard_map/ppermute | solution.py:544
  18.6 0.0 collective-permute-done.other_ref
  18.6 0.0 copy-done
  18.6 0.0 copy-done.1
  18.6 2.0 %shard_map.92 = bf16[16,40,128]{2,1,0:T(8,128)(2,1)} custom-call(bf16[8,152,128]{2,1,0:T(8,128)(2,1)S(1)} %all_to_all.15.own_ref, bf16[8,128,128]{2,1,0:T(8,128)(2,1)S(1)} %collective-permute-done.other_ref, f32[4,16,128]{2,1,0:T(8,128)S(1)} %copy-done, f32[16,128]{1,0:T(8,128)S(1)} %copy-done.1, bf16[26,128,128]{2,1,0:T(8,128)(2,1)S(1)} %get-tuple-element.14.near_ref, ...), custom_call_target="tpu_custom_call" | custom-call | tf_op jit(solution)/shard_map/pallas_call | solution.py:487
  20.6 6.1 %all-to-all-start.1 = ((bf16[16,40,128]{2,1,0:T(8,128)(2,1)}), bf16[16,40,128]{2,1,0:T(8,128)(2,1)S(1)}, u32[]{:S(2)}, u32[]{:S(2)}) async-start(bf16[16,40,128]{2,1,0:T(8,128)(2,1)} %shard_map.92), calls=%async_computation.1 | async-start | bytes 327680 | tf_op jit(solution)/shard_map/all_to_all | solution.py:33
  26.7 0.0 collective-permute-done.1.across_ref
  26.7 0.1 collective-permute-start.2
  26.8 6.2 %all-to-all-done.1.parts_ref = bf16[16,40,128]{2,1,0:T(8,128)(2,1)S(1)} async-done(((bf16[16,40,128]{2,1,0:T(8,128)(2,1)}), bf16[16,40,128]{2,1,0:T(8,128)(2,1)S(1)}, u32[]{:S(2)}, u32[]{:S(2)}) %all-to-all-start.1) | async-done | bytes 163872 | tf_op jit(solution)/shard_map/all_to_all | solution.py:33
  33.0 0.0 collective-permute-start.3
  33.0 0.0 collective-permute-done.2.corner_ref
  33.0 1.2 %shard_map.94 = f32[16,8,128]{2,1,0:T(8,128)S(1)} custom-call(bf16[8,128,128]{2,1,0:T(8,128)(2,1)S(1)} %slice.4.own_ref, bf16[8,128,128]{2,1,0:T(8,128)(2,1)S(1)} %collective-permute-done.other_ref, bf16[8,128,128]{2,1,0:T(8,128)(2,1)S(1)} %collective-permute-done.1.across_ref, bf16[8,128,128]{2,1,0:T(8,128)(2,1)S(1)} %collective-permute-done.2.corner_ref, ...), custom_call_target="tpu_custom_call" | custom-call | tf_op jit(solution)/shard_map/pallas_call | solution.py:487
  34.2 0.0 collective-permute-done.3.other_ref
  34.2 8.0 %all_to_all.16.sums_ref = f32[16,8,128]{2,1,0:T(8,128)S(1)} all-to-all(f32[16,8,128]{2,1,0:T(8,128)S(1)} %shard_map.94), channel_id=1, replica_groups={{21,17,25,16,28,9,13,8,24,1,29,5,0,12,4,20},{23,19,27,18,30,11,15,10,26..., dimensions={0} | all-to-all | bytes 131072 | tf_op jit(solution)/shard_map/all_to_all | solution.py:33
  42.2 0.7 %shard_map.95 = f32[4,16,128]{2,1,0:T(8,128)} custom-call(f32[16,8,128]{2,1,0:T(8,128)S(1)} %all_to_all.16.sums_ref, f32[32,128]{1,0:T(8,128)S(1)} %shard_map.93.field_ref, f32[32,128]{1,0:T(8,128)S(1)} %collective-permute-done.3.other_ref, f32[4,16,128]{2,1,0:T(8,128)S(1)} %copy-done), custom_call_target="tpu_custom_call" | custom-call | tf_op jit(solution)/shard_map/pallas_call | solution.py:487
  (2 shorter events, 0.0 us)
Async XLA Ops:
  16.9 1.7 %copy-start = (f32[4,16,128]{2,1,0:T(8,128)S(1)}, f32[4,16,128]{2,1,0:T(8,128)}, u32[]{:S(2)}) copy-start(f32[4,16,128]{2,1,0:T(8,128)} %rhs_ref.5) | copy-start | bytes 98308
  16.9 1.7 %copy-start.1 = (f32[16,128]{1,0:T(8,128)S(1)}, f32[16,128]{1,0:T(8,128)}, u32[]{:S(2)}) copy-start(f32[16,128]{1,0:T(8,128)} %self_ref.3) | copy-start | bytes 24580
  16.9 1.6 %collective-permute-start = (bf16[8,128,128]{2,1,0:T(8,128)(2,1)S(1)}, bf16[8,128,128]{2,1,0:T(8,128)(2,1)S(1)}, u32[]{:S(2)}, u32[]{:S(2)}) collective-permute-start(bf16[8,128,128]{2,1,0:T(8,128)(2,1)S(1)} %slice.4.own_ref), channel_id=1, source_target_pairs={{0,1},{1,0},{2,3},{3,2},{4,5},{5,4},{6,7},{7,6},{8,9},{9,8},{10,11... | collective-permute-start | bytes 786440 | tf_op jit(solution)/shard_map/ppermute | solution.py:543
  17.0 9.7 %collective-permute-start.1 = (bf16[8,128,128]{2,1,0:T(8,128)(2,1)S(1)}, bf16[8,128,128]{2,1,0:T(8,128)(2,1)S(1)}, u32[]{:S(2)}, u32[]{:S(2)}) collective-permute-start(bf16[8,128,128]{2,1,0:T(8,128)(2,1)S(1)} %slice.4.own_ref), channel_id=1, source_target_pairs={{0,2},{2,0},{1,3},{3,1},{4,6},{6,4},{5,7},{7,5},{8,10},{10,8},{9,1... | collective-permute-start | bytes 786440 | tf_op jit(solution)/shard_map/ppermute | solution.py:544
  20.6 12.4 %all-to-all-start.1 = ((bf16[16,40,128]{2,1,0:T(8,128)(2,1)}), bf16[16,40,128]{2,1,0:T(8,128)(2,1)S(1)}, u32[]{:S(2)}, u32[]{:S(2)}) async-start(bf16[16,40,128]{2,1,0:T(8,128)(2,1)} %shard_map.92), calls=%async_computation.1 | async-start | bytes 327680 | tf_op jit(solution)/shard_map/all_to_all | solution.py:33
  26.7 6.3 %collective-permute-start.2 = (bf16[8,128,128]{2,1,0:T(8,128)(2,1)S(1)}, bf16[8,128,128]{2,1,0:T(8,128)(2,1)S(1)}, u32[]{:S(2)}, u32[]{:S(2)}) collective-permute-start(bf16[8,128,128]{2,1,0:T(8,128)(2,1)S(1)} %collective-permute-done.1.across_ref), channel_id=1, source_target_pairs={{0,1},{1,0},{2,3},{3,2},{4,5},{5,4},{6,7},{7,6},{8,9},{9,8},{10,11... | collective-permute-start | bytes 786440 | tf_op jit(solution)/shard_map/ppermute | solution.py:545
  33.0 1.2 %collective-permute-start.3 = (f32[32,128]{1,0:T(8,128)S(1)}, f32[32,128]{1,0:T(8,128)S(1)}, u32[]{:S(2)}, u32[]{:S(2)}) collective-permute-start(f32[32,128]{1,0:T(8,128)S(1)} %shard_map.93.field_ref), channel_id=1, source_target_pairs={{0,1},{1,0},{2,3},{3,2},{4,5},{5,4},{6,7},{7,6},{8,9},{9,8},{10,11... | collective-permute-start | bytes 49160 | tf_op jit(solution)/shard_map/ppermute | solution.py:553

commit v6 on v5

--- a/solution.py
+++ b/solution.py
@@ -13,7 +13,7 @@
 FULL = jnp.float32
 SLOT = pltpu.VMEM
 FIRST = {8: (5, 7, 0, 4, 6, 3, 1, 2)}
-SECOND = {16: (6, 0, 2, 1, 15, 3, 8, 7, 4, 11, 14, 9, 10, 13, 5, 12)}
+SECOND = {16: (10, 8, 3, 7, 2, 14, 5, 1, 11, 9, 15, 13, 12, 6, 4, 0)}
 THIRD = {16: (11, 9, 13, 8, 14, 5, 7, 4, 12, 1, 15, 3, 0, 6, 2, 10)}
 
 

time: 43.2 us -> 42.6 us (0.986)
  waiting for transfers between devices: 6.24 us -> 5.24 us
    all_to_all x1, waiting for transfers between devices: 6.22 us -> 5.22 us  [exchange(): lax.all_to_all(value, axes, 0, 0, tiled=True, axis_index_groups=groups)]
  transfers between devices with their start and end apart: 5 -> 5, of which waited for: 1 -> 1; matrix products, arithmetic and copies ran while one was open for 0% -> 0% of each run, Pallas kernels for 7% -> 8%
where the time goes in v6:
time: 42.6 us; the launch traced here: 42.3 us
  blocking collectives  23.3 us (55%)
  starting transfers between devices  7.78 us (18%)
  Pallas kernels  5.83 us (14%)
  waiting for transfers between devices  5.24 us (12%)
    all_to_all x2, blocking collectives, exchange(): lax.all_to_all(value, axes, 0, 0, tiled=True, axis_index_groups=groups)  23.3 us
    all_to_all x1, starting transfers between devices, exchange(): lax.all_to_all(value, axes, 0, 0, tiled=True, axis_index_groups=groups)  6.08 us
    pallas_call x5, Pallas kernels, call(): pl.pallas_call(kernel, out_shape=outs, in_specs=[vmem] * held + [pl.Block...  5.83 us
    all_to_all x1, waiting for transfers between devices, exchange(): lax.all_to_all(value, axes, 0, 0, tiled=True, axis_index_groups=groups)  5.22 us
    ppermute x1, starting transfers between devices, per_device(): across = lax.ppermute(bands, 'side', swap)  1.56 us
  transfers between devices with their start and end apart: 5, of which 1 were waited for; matrix products, arithmetic and copies ran while one was open for 0% of the time, Pallas kernels for 8%

profile of v6, /device:TPU:0, one launch (start us, length us, event | category | flops | bytes accessed | tf_op | source)
XLA Modules:
  0.0 42.3 jit_solution(17817752108343767699)
XLA Ops:
  0.0 1.9 %shard_map.91 = (bf16[8,152,128]{2,1,0:T(8,128)(2,1)S(1)}, bf16[64,64]{1,0:T(8,128)(2,1)S(1)}, bf16[16,256,128]{2,1,0:T(8,128)(2,1)S(1)}, bf16[26,128,128]{2,1,0...) custom-call(f32[4,16,128]{2,1,0:T(8,128)} %rhs_ref.5, bf16[16,256,128]{2,1,0:T(8,128)(2,1)} %expand_hbm.1, ...), custom_call_target="tpu_custom_call" | custom-call | tf_op jit(solution)/shard_map/pallas_call | solution.py:487
  1.9 15.0 %all_to_all.15.own_ref = bf16[8,152,128]{2,1,0:T(8,128)(2,1)S(1)} all-to-all(bf16[8,152,128]{2,1,0:T(8,128)(2,1)S(1)} %get-tuple-element.13), channel_id=1, replica_groups={{20,28,0,16,24,12,4,8},{21,29,1,17,25,13,5,9},{22,30,2,18,26,14,6,10},{..., dimensions={0} | all-to-all | bytes 622592 | tf_op jit(solution)/shard_map/all_to_all | solution.py:33
  16.9 0.0 copy-start
  16.9 0.0 copy-start.1
  16.9 0.1 collective-permute-start
  17.0 1.6 %collective-permute-start.1 = (bf16[8,128,128]{2,1,0:T(8,128)(2,1)S(1)}, bf16[8,128,128]{2,1,0:T(8,128)(2,1)S(1)}, u32[]{:S(2)}, u32[]{:S(2)}) collective-permute-start(bf16[8,128,128]{2,1,0:T(8,128)(2,1)S(1)} %slice.4.own_ref), channel_id=1, source_target_pairs={{0,2},{2,0},{1,3},{3,1},{4,6},{6,4},{5,7},{7,5},{8,10},{10,8},{9,1... | collective-permute-start | bytes 786440 | tf_op jit(solution)/shard_map/ppermute | solution.py:544
  18.6 0.0 collective-permute-done.other_ref
  18.6 0.0 copy-done
  18.6 0.0 copy-done.1
  18.6 2.0 %shard_map.92 = bf16[16,40,128]{2,1,0:T(8,128)(2,1)} custom-call(bf16[8,152,128]{2,1,0:T(8,128)(2,1)S(1)} %all_to_all.15.own_ref, bf16[8,128,128]{2,1,0:T(8,128)(2,1)S(1)} %collective-permute-done.other_ref, f32[4,16,128]{2,1,0:T(8,128)S(1)} %copy-done, f32[16,128]{1,0:T(8,128)S(1)} %copy-done.1, bf16[26,128,128]{2,1,0:T(8,128)(2,1)S(1)} %get-tuple-element.14.near_ref, ...), custom_call_target="tpu_custom_call" | custom-call | tf_op jit(solution)/shard_map/pallas_call | solution.py:487
  20.6 6.1 %all-to-all-start.1 = ((bf16[16,40,128]{2,1,0:T(8,128)(2,1)}), bf16[16,40,128]{2,1,0:T(8,128)(2,1)S(1)}, u32[]{:S(2)}, u32[]{:S(2)}) async-start(bf16[16,40,128]{2,1,0:T(8,128)(2,1)} %shard_map.92), calls=%async_computation.1 | async-start | bytes 327680 | tf_op jit(solution)/shard_map/all_to_all | solution.py:33
  26.7 0.0 collective-permute-done.1.across_ref
  26.7 0.1 collective-permute-start.2
  26.8 5.2 %all-to-all-done.1.parts_ref = bf16[16,40,128]{2,1,0:T(8,128)(2,1)S(1)} async-done(((bf16[16,40,128]{2,1,0:T(8,128)(2,1)}), bf16[16,40,128]{2,1,0:T(8,128)(2,1)S(1)}, u32[]{:S(2)}, u32[]{:S(2)}) %all-to-all-start.1) | async-done | bytes 163872 | tf_op jit(solution)/shard_map/all_to_all | solution.py:33
  32.0 0.0 collective-permute-start.3
  32.0 0.0 collective-permute-done.2.corner_ref
  32.0 1.2 %shard_map.94 = f32[16,8,128]{2,1,0:T(8,128)S(1)} custom-call(bf16[8,128,128]{2,1,0:T(8,128)(2,1)S(1)} %slice.4.own_ref, bf16[8,128,128]{2,1,0:T(8,128)(2,1)S(1)} %collective-permute-done.other_ref, bf16[8,128,128]{2,1,0:T(8,128)(2,1)S(1)} %collective-permute-done.1.across_ref, bf16[8,128,128]{2,1,0:T(8,128)(2,1)S(1)} %collective-permute-done.2.corner_ref, ...), custom_call_target="tpu_custom_call" | custom-call | tf_op jit(solution)/shard_map/pallas_call | solution.py:487
  33.2 0.0 collective-permute-done.3.other_ref
  33.2 8.3 %all_to_all.16.sums_ref = f32[16,8,128]{2,1,0:T(8,128)S(1)} all-to-all(f32[16,8,128]{2,1,0:T(8,128)S(1)} %shard_map.94), channel_id=1, replica_groups={{21,17,25,16,28,9,13,8,24,1,29,5,0,12,4,20},{23,19,27,18,30,11,15,10,26..., dimensions={0} | all-to-all | bytes 131072 | tf_op jit(solution)/shard_map/all_to_all | solution.py:33
  41.5 0.7 %shard_map.95 = f32[4,16,128]{2,1,0:T(8,128)} custom-call(f32[16,8,128]{2,1,0:T(8,128)S(1)} %all_to_all.16.sums_ref, f32[32,128]{1,0:T(8,128)S(1)} %shard_map.93.field_ref, f32[32,128]{1,0:T(8,128)S(1)} %collective-permute-done.3.other_ref, f32[4,16,128]{2,1,0:T(8,128)S(1)} %copy-done), custom_call_target="tpu_custom_call" | custom-call | tf_op jit(solution)/shard_map/pallas_call | solution.py:487
  (2 shorter events, 0.0 us)
Async XLA Ops:
  16.9 1.7 %copy-start = (f32[4,16,128]{2,1,0:T(8,128)S(1)}, f32[4,16,128]{2,1,0:T(8,128)}, u32[]{:S(2)}) copy-start(f32[4,16,128]{2,1,0:T(8,128)} %rhs_ref.5) | copy-start | bytes 98308
  16.9 1.7 %copy-start.1 = (f32[16,128]{1,0:T(8,128)S(1)}, f32[16,128]{1,0:T(8,128)}, u32[]{:S(2)}) copy-start(f32[16,128]{1,0:T(8,128)} %self_ref.3) | copy-start | bytes 24580
  16.9 1.6 %collective-permute-start = (bf16[8,128,128]{2,1,0:T(8,128)(2,1)S(1)}, bf16[8,128,128]{2,1,0:T(8,128)(2,1)S(1)}, u32[]{:S(2)}, u32[]{:S(2)}) collective-permute-start(bf16[8,128,128]{2,1,0:T(8,128)(2,1)S(1)} %slice.4.own_ref), channel_id=1, source_target_pairs={{0,1},{1,0},{2,3},{3,2},{4,5},{5,4},{6,7},{7,6},{8,9},{9,8},{10,11... | collective-permute-start | bytes 786440 | tf_op jit(solution)/shard_map/ppermute | solution.py:543
  17.0 9.7 %collective-permute-start.1 = (bf16[8,128,128]{2,1,0:T(8,128)(2,1)S(1)}, bf16[8,128,128]{2,1,0:T(8,128)(2,1)S(1)}, u32[]{:S(2)}, u32[]{:S(2)}) collective-permute-start(bf16[8,128,128]{2,1,0:T(8,128)(2,1)S(1)} %slice.4.own_ref), channel_id=1, source_target_pairs={{0,2},{2,0},{1,3},{3,1},{4,6},{6,4},{5,7},{7,5},{8,10},{10,8},{9,1... | collective-permute-start | bytes 786440 | tf_op jit(solution)/shard_map/ppermute | solution.py:544
  20.6 11.4 %all-to-all-start.1 = ((bf16[16,40,128]{2,1,0:T(8,128)(2,1)}), bf16[16,40,128]{2,1,0:T(8,128)(2,1)S(1)}, u32[]{:S(2)}, u32[]{:S(2)}) async-start(bf16[16,40,128]{2,1,0:T(8,128)(2,1)} %shard_map.92), calls=%async_computation.1 | async-start | bytes 327680 | tf_op jit(solution)/shard_map/all_to_all | solution.py:33
  26.7 5.3 %collective-permute-start.2 = (bf16[8,128,128]{2,1,0:T(8,128)(2,1)S(1)}, bf16[8,128,128]{2,1,0:T(8,128)(2,1)S(1)}, u32[]{:S(2)}, u32[]{:S(2)}) collective-permute-start(bf16[8,128,128]{2,1,0:T(8,128)(2,1)S(1)} %collective-permute-done.1.across_ref), channel_id=1, source_target_pairs={{0,1},{1,0},{2,3},{3,2},{4,5},{5,4},{6,7},{7,6},{8,9},{9,8},{10,11... | collective-permute-start | bytes 786440 | tf_op jit(solution)/shard_map/ppermute | solution.py:545
  32.0 1.2 %collective-permute-start.3 = (f32[32,128]{1,0:T(8,128)S(1)}, f32[32,128]{1,0:T(8,128)S(1)}, u32[]{:S(2)}, u32[]{:S(2)}) collective-permute-start(f32[32,128]{1,0:T(8,128)S(1)} %shard_map.93.field_ref), channel_id=1, source_target_pairs={{0,1},{1,0},{2,3},{3,2},{4,5},{5,4},{6,7},{7,6},{8,9},{9,8},{10,11... | collective-permute-start | bytes 49160 | tf_op jit(solution)/shard_map/ppermute | solution.py:553

commit v7 on v6

--- a/solution.py
+++ b/solution.py
@@ -447,7 +447,7 @@
         slope = ru / rr
         norm = uu - slope * ru
         first_row = rw - slope * ru
-        scale = lax.rsqrt(rr * norm)
+        scale = lax.rsqrt(rr) * lax.rsqrt(norm)
         h11 = slope + SHIFT
         h21 = jnp.sqrt(norm / rr)
         h12 = first_row * scale

time: 42.6 us -> 42.6 us (level)
  no operation moved by 1% of the time
where the time goes in v7:
time: 42.6 us; the launch traced here: 42.3 us
  blocking collectives  23.3 us (55%)
  starting transfers between devices  7.78 us (18%)
  Pallas kernels  5.82 us (14%)
  waiting for transfers between devices  5.24 us (12%)
    all_to_all x2, blocking collectives, exchange(): lax.all_to_all(value, axes, 0, 0, tiled=True, axis_index_groups=groups)  23.3 us
    all_to_all x1, starting transfers between devices, exchange(): lax.all_to_all(value, axes, 0, 0, tiled=True, axis_index_groups=groups)  6.08 us
    pallas_call x5, Pallas kernels, call(): pl.pallas_call(kernel, out_shape=outs, in_specs=[vmem] * held + [pl.Block...  5.82 us
    all_to_all x1, waiting for transfers between devices, exchange(): lax.all_to_all(value, axes, 0, 0, tiled=True, axis_index_groups=groups)  5.22 us
    ppermute x1, starting transfers between devices, per_device(): across = lax.ppermute(bands, 'side', swap)  1.56 us
  transfers between devices with their start and end apart: 5, of which 1 were waited for; matrix products, arithmetic and copies ran while one was open for 0% of the time, Pallas kernels for 8%

profile of v7, /device:TPU:0, one launch (start us, length us, event | category | flops | bytes accessed | tf_op | source)
XLA Modules:
  0.0 42.3 jit_solution(14747169717383710919)
XLA Ops:
  0.0 1.9 %shard_map.91 = (bf16[8,152,128]{2,1,0:T(8,128)(2,1)S(1)}, bf16[64,64]{1,0:T(8,128)(2,1)S(1)}, bf16[16,256,128]{2,1,0:T(8,128)(2,1)S(1)}, bf16[26,128,128]{2,1,0...) custom-call(f32[4,16,128]{2,1,0:T(8,128)} %rhs_ref.5, bf16[16,256,128]{2,1,0:T(8,128)(2,1)} %expand_hbm.1, ...), custom_call_target="tpu_custom_call" | custom-call | tf_op jit(solution)/shard_map/pallas_call | solution.py:487
  1.9 15.0 %all_to_all.15.own_ref = bf16[8,152,128]{2,1,0:T(8,128)(2,1)S(1)} all-to-all(bf16[8,152,128]{2,1,0:T(8,128)(2,1)S(1)} %get-tuple-element.13), channel_id=1, replica_groups={{20,28,0,16,24,12,4,8},{21,29,1,17,25,13,5,9},{22,30,2,18,26,14,6,10},{..., dimensions={0} | all-to-all | bytes 622592 | tf_op jit(solution)/shard_map/all_to_all | solution.py:33
  16.9 0.0 copy-start
  16.9 0.0 copy-start.1
  16.9 0.1 collective-permute-start
  17.0 1.6 %collective-permute-start.1 = (bf16[8,128,128]{2,1,0:T(8,128)(2,1)S(1)}, bf16[8,128,128]{2,1,0:T(8,128)(2,1)S(1)}, u32[]{:S(2)}, u32[]{:S(2)}) collective-permute-start(bf16[8,128,128]{2,1,0:T(8,128)(2,1)S(1)} %slice.4.own_ref), channel_id=1, source_target_pairs={{0,2},{2,0},{1,3},{3,1},{4,6},{6,4},{5,7},{7,5},{8,10},{10,8},{9,1... | collective-permute-start | bytes 786440 | tf_op jit(solution)/shard_map/ppermute | solution.py:544
  18.6 0.0 collective-permute-done.other_ref
  18.6 0.0 copy-done
  18.6 0.0 copy-done.1
  18.6 2.0 %shard_map.92 = bf16[16,40,128]{2,1,0:T(8,128)(2,1)} custom-call(bf16[8,152,128]{2,1,0:T(8,128)(2,1)S(1)} %all_to_all.15.own_ref, bf16[8,128,128]{2,1,0:T(8,128)(2,1)S(1)} %collective-permute-done.other_ref, f32[4,16,128]{2,1,0:T(8,128)S(1)} %copy-done, f32[16,128]{1,0:T(8,128)S(1)} %copy-done.1, bf16[26,128,128]{2,1,0:T(8,128)(2,1)S(1)} %get-tuple-element.14.near_ref, ...), custom_call_target="tpu_custom_call" | custom-call | tf_op jit(solution)/shard_map/pallas_call | solution.py:487
  20.6 6.1 %all-to-all-start.1 = ((bf16[16,40,128]{2,1,0:T(8,128)(2,1)}), bf16[16,40,128]{2,1,0:T(8,128)(2,1)S(1)}, u32[]{:S(2)}, u32[]{:S(2)}) async-start(bf16[16,40,128]{2,1,0:T(8,128)(2,1)} %shard_map.92), calls=%async_computation.1 | async-start | bytes 327680 | tf_op jit(solution)/shard_map/all_to_all | solution.py:33
  26.7 0.0 collective-permute-done.1.across_ref
  26.7 0.1 collective-permute-start.2
  26.8 5.2 %all-to-all-done.1.parts_ref = bf16[16,40,128]{2,1,0:T(8,128)(2,1)S(1)} async-done(((bf16[16,40,128]{2,1,0:T(8,128)(2,1)}), bf16[16,40,128]{2,1,0:T(8,128)(2,1)S(1)}, u32[]{:S(2)}, u32[]{:S(2)}) %all-to-all-start.1) | async-done | bytes 163872 | tf_op jit(solution)/shard_map/all_to_all | solution.py:33
  32.0 0.0 collective-permute-start.3
  32.0 0.0 collective-permute-done.2.corner_ref
  32.0 1.2 %shard_map.94 = f32[16,8,128]{2,1,0:T(8,128)S(1)} custom-call(bf16[8,128,128]{2,1,0:T(8,128)(2,1)S(1)} %slice.4.own_ref, bf16[8,128,128]{2,1,0:T(8,128)(2,1)S(1)} %collective-permute-done.other_ref, bf16[8,128,128]{2,1,0:T(8,128)(2,1)S(1)} %collective-permute-done.1.across_ref, bf16[8,128,128]{2,1,0:T(8,128)(2,1)S(1)} %collective-permute-done.2.corner_ref, ...), custom_call_target="tpu_custom_call" | custom-call | tf_op jit(solution)/shard_map/pallas_call | solution.py:487
  33.2 0.0 collective-permute-done.3.other_ref
  33.2 8.3 %all_to_all.16.sums_ref = f32[16,8,128]{2,1,0:T(8,128)S(1)} all-to-all(f32[16,8,128]{2,1,0:T(8,128)S(1)} %shard_map.94), channel_id=1, replica_groups={{21,17,25,16,28,9,13,8,24,1,29,5,0,12,4,20},{23,19,27,18,30,11,15,10,26..., dimensions={0} | all-to-all | bytes 131072 | tf_op jit(solution)/shard_map/all_to_all | solution.py:33
  41.5 0.7 %shard_map.95 = f32[4,16,128]{2,1,0:T(8,128)} custom-call(f32[16,8,128]{2,1,0:T(8,128)S(1)} %all_to_all.16.sums_ref, f32[32,128]{1,0:T(8,128)S(1)} %shard_map.93.field_ref, f32[32,128]{1,0:T(8,128)S(1)} %collective-permute-done.3.other_ref, f32[4,16,128]{2,1,0:T(8,128)S(1)} %copy-done), custom_call_target="tpu_custom_call" | custom-call | tf_op jit(solution)/shard_map/pallas_call | solution.py:487
  (2 shorter events, 0.0 us)
Async XLA Ops:
  16.9 1.7 %copy-start = (f32[4,16,128]{2,1,0:T(8,128)S(1)}, f32[4,16,128]{2,1,0:T(8,128)}, u32[]{:S(2)}) copy-start(f32[4,16,128]{2,1,0:T(8,128)} %rhs_ref.5) | copy-start | bytes 98308
  16.9 1.7 %copy-start.1 = (f32[16,128]{1,0:T(8,128)S(1)}, f32[16,128]{1,0:T(8,128)}, u32[]{:S(2)}) copy-start(f32[16,128]{1,0:T(8,128)} %self_ref.3) | copy-start | bytes 24580
  16.9 1.6 %collective-permute-start = (bf16[8,128,128]{2,1,0:T(8,128)(2,1)S(1)}, bf16[8,128,128]{2,1,0:T(8,128)(2,1)S(1)}, u32[]{:S(2)}, u32[]{:S(2)}) collective-permute-start(bf16[8,128,128]{2,1,0:T(8,128)(2,1)S(1)} %slice.4.own_ref), channel_id=1, source_target_pairs={{0,1},{1,0},{2,3},{3,2},{4,5},{5,4},{6,7},{7,6},{8,9},{9,8},{10,11... | collective-permute-start | bytes 786440 | tf_op jit(solution)/shard_map/ppermute | solution.py:543
  17.0 9.7 %collective-permute-start.1 = (bf16[8,128,128]{2,1,0:T(8,128)(2,1)S(1)}, bf16[8,128,128]{2,1,0:T(8,128)(2,1)S(1)}, u32[]{:S(2)}, u32[]{:S(2)}) collective-permute-start(bf16[8,128,128]{2,1,0:T(8,128)(2,1)S(1)} %slice.4.own_ref), channel_id=1, source_target_pairs={{0,2},{2,0},{1,3},{3,1},{4,6},{6,4},{5,7},{7,5},{8,10},{10,8},{9,1... | collective-permute-start | bytes 786440 | tf_op jit(solution)/shard_map/ppermute | solution.py:544
  20.6 11.4 %all-to-all-start.1 = ((bf16[16,40,128]{2,1,0:T(8,128)(2,1)}), bf16[16,40,128]{2,1,0:T(8,128)(2,1)S(1)}, u32[]{:S(2)}, u32[]{:S(2)}) async-start(bf16[16,40,128]{2,1,0:T(8,128)(2,1)} %shard_map.92), calls=%async_computation.1 | async-start | bytes 327680 | tf_op jit(solution)/shard_map/all_to_all | solution.py:33
  26.7 5.3 %collective-permute-start.2 = (bf16[8,128,128]{2,1,0:T(8,128)(2,1)S(1)}, bf16[8,128,128]{2,1,0:T(8,128)(2,1)S(1)}, u32[]{:S(2)}, u32[]{:S(2)}) collective-permute-start(bf16[8,128,128]{2,1,0:T(8,128)(2,1)S(1)} %collective-permute-done.1.across_ref), channel_id=1, source_target_pairs={{0,1},{1,0},{2,3},{3,2},{4,5},{5,4},{6,7},{7,6},{8,9},{9,8},{10,11... | collective-permute-start | bytes 786440 | tf_op jit(solution)/shard_map/ppermute | solution.py:545
  32.0 1.2 %collective-permute-start.3 = (f32[32,128]{1,0:T(8,128)S(1)}, f32[32,128]{1,0:T(8,128)S(1)}, u32[]{:S(2)}, u32[]{:S(2)}) collective-permute-start(f32[32,128]{1,0:T(8,128)S(1)} %shard_map.93.field_ref), channel_id=1, source_target_pairs={{0,1},{1,0},{2,3},{3,2},{4,5},{5,4},{6,7},{7,6},{8,9},{9,8},{10,11... | collective-permute-start | bytes 49160 | tf_op jit(solution)/shard_map/ppermute | solution.py:553

commit v8 on v7

--- a/solution.py
+++ b/solution.py
@@ -13,7 +13,7 @@
 FULL = jnp.float32
 SLOT = pltpu.VMEM
 FIRST = {8: (5, 7, 0, 4, 6, 3, 1, 2)}
-SECOND = {16: (10, 8, 3, 7, 2, 14, 5, 1, 11, 9, 15, 13, 12, 6, 4, 0)}
+SECOND = {16: (10, 8, 3, 1, 2, 14, 5, 7, 11, 9, 15, 13, 12, 6, 4, 0)}
 THIRD = {16: (11, 9, 13, 8, 14, 5, 7, 4, 12, 1, 15, 3, 0, 6, 2, 10)}
 
 
@@ -156,11 +156,8 @@
                 for ref in bands
             ]
             images.append(dot_nt(sources, jnp.concatenate(right, axis=0)))
-        images = jnp.concatenate(images, axis=0)
-        upper = images.astype(HALF)
-        lower = (images - upper.astype(FULL)).astype(HALF)
-        table = table_ref[number]
-        return total + (dot_nn(table, upper) + dot_nn(table, lower))
+        images = jnp.concatenate(images, axis=0).astype(HALF)
+        return total + dot_nn(table_ref[number], images)
 
     return fold(table_ref.shape[0], add, jnp.zeros((table_ref.shape[1], len(bands) * band), FULL))
 

time: 42.6 us -> 42.5 us (level)
  transfers between devices with their start and end apart: 5 -> 5, of which waited for: 1 -> 2; matrix products, arithmetic and copies ran while one was open for 0% -> 0% of each run, Pallas kernels for 8% -> 7%
where the time goes in v8:
time: 42.5 us; the launch traced here: 42.2 us
  blocking collectives  23.4 us (55%)
  starting transfers between devices  7.78 us (18%)
  Pallas kernels  5.68 us (13%)
  waiting for transfers between devices  5.29 us (12%)
    all_to_all x2, blocking collectives, exchange(): lax.all_to_all(value, axes, 0, 0, tiled=True, axis_index_groups=groups)  23.4 us
    all_to_all x1, starting transfers between devices, exchange(): lax.all_to_all(value, axes, 0, 0, tiled=True, axis_index_groups=groups)  6.08 us
    pallas_call x5, Pallas kernels, call(): pl.pallas_call(kernel, out_shape=outs, in_specs=[vmem] * held + [pl.Block...  5.68 us
    all_to_all x1, waiting for transfers between devices, exchange(): lax.all_to_all(value, axes, 0, 0, tiled=True, axis_index_groups=groups)  5.2 us
    ppermute x1, starting transfers between devices, per_device(): across = lax.ppermute(bands, 'side', swap)  1.56 us
  transfers between devices with their start and end apart: 5, of which 2 were waited for; matrix products, arithmetic and copies ran while one was open for 0% of the time, Pallas kernels for 7%

profile of v8, /device:TPU:0, one launch (start us, length us, event | category | flops | bytes accessed | tf_op | source)
XLA Modules:
  0.0 42.2 jit_solution(1003946835204808814)
XLA Ops:
  0.0 1.9 %shard_map.91 = (bf16[8,152,128]{2,1,0:T(8,128)(2,1)S(1)}, bf16[64,64]{1,0:T(8,128)(2,1)S(1)}, bf16[16,256,128]{2,1,0:T(8,128)(2,1)S(1)}, bf16[26,128,128]{2,1,0...) custom-call(f32[4,16,128]{2,1,0:T(8,128)} %rhs_ref.5, bf16[16,256,128]{2,1,0:T(8,128)(2,1)} %expand_hbm.1, ...), custom_call_target="tpu_custom_call" | custom-call | tf_op jit(solution)/shard_map/pallas_call | solution.py:484
  1.9 15.0 %all_to_all.15.own_ref = bf16[8,152,128]{2,1,0:T(8,128)(2,1)S(1)} all-to-all(bf16[8,152,128]{2,1,0:T(8,128)(2,1)S(1)} %get-tuple-element.13), channel_id=1, replica_groups={{20,28,0,16,24,12,4,8},{21,29,1,17,25,13,5,9},{22,30,2,18,26,14,6,10},{..., dimensions={0} | all-to-all | bytes 622592 | tf_op jit(solution)/shard_map/all_to_all | solution.py:33
  16.9 0.0 copy-start
  16.9 0.0 copy-start.1
  16.9 0.1 collective-permute-start
  17.0 1.6 %collective-permute-start.1 = (bf16[8,128,128]{2,1,0:T(8,128)(2,1)S(1)}, bf16[8,128,128]{2,1,0:T(8,128)(2,1)S(1)}, u32[]{:S(2)}, u32[]{:S(2)}) collective-permute-start(bf16[8,128,128]{2,1,0:T(8,128)(2,1)S(1)} %slice.4.own_ref), channel_id=1, source_target_pairs={{0,2},{2,0},{1,3},{3,1},{4,6},{6,4},{5,7},{7,5},{8,10},{10,8},{9,1... | collective-permute-start | bytes 786440 | tf_op jit(solution)/shard_map/ppermute | solution.py:541
  18.6 0.0 collective-permute-done.other_ref
  18.6 0.0 copy-done
  18.6 0.0 copy-done.1
  18.6 2.0 %shard_map.92 = bf16[16,40,128]{2,1,0:T(8,128)(2,1)} custom-call(bf16[8,152,128]{2,1,0:T(8,128)(2,1)S(1)} %all_to_all.15.own_ref, bf16[8,128,128]{2,1,0:T(8,128)(2,1)S(1)} %collective-permute-done.other_ref, f32[4,16,128]{2,1,0:T(8,128)S(1)} %copy-done, f32[16,128]{1,0:T(8,128)S(1)} %copy-done.1, bf16[26,128,128]{2,1,0:T(8,128)(2,1)S(1)} %get-tuple-element.14.near_ref, ...), custom_call_target="tpu_custom_call" | custom-call | tf_op jit(solution)/shard_map/pallas_call | solution.py:484
  20.5 6.1 %all-to-all-start.1 = ((bf16[16,40,128]{2,1,0:T(8,128)(2,1)}), bf16[16,40,128]{2,1,0:T(8,128)(2,1)S(1)}, u32[]{:S(2)}, u32[]{:S(2)}) async-start(bf16[16,40,128]{2,1,0:T(8,128)(2,1)} %shard_map.92), calls=%async_computation.1 | async-start | bytes 327680 | tf_op jit(solution)/shard_map/all_to_all | solution.py:33
  26.6 0.0 collective-permute-done.1.across_ref
  26.6 0.1 collective-permute-start.2
  26.7 5.2 %all-to-all-done.1.parts_ref = bf16[16,40,128]{2,1,0:T(8,128)(2,1)S(1)} async-done(((bf16[16,40,128]{2,1,0:T(8,128)(2,1)}), bf16[16,40,128]{2,1,0:T(8,128)(2,1)S(1)}, u32[]{:S(2)}, u32[]{:S(2)}) %all-to-all-start.1) | async-done | bytes 163872 | tf_op jit(solution)/shard_map/all_to_all | solution.py:33
  31.9 0.0 collective-permute-start.3
  31.9 0.0 collective-permute-done.2.corner_ref
  31.9 1.1 %shard_map.94 = f32[16,8,128]{2,1,0:T(8,128)S(1)} custom-call(bf16[8,128,128]{2,1,0:T(8,128)(2,1)S(1)} %slice.4.own_ref, bf16[8,128,128]{2,1,0:T(8,128)(2,1)S(1)} %collective-permute-done.other_ref, bf16[8,128,128]{2,1,0:T(8,128)(2,1)S(1)} %collective-permute-done.1.across_ref, bf16[8,128,128]{2,1,0:T(8,128)(2,1)S(1)} %collective-permute-done.2.corner_ref, ...), custom_call_target="tpu_custom_call" | custom-call | tf_op jit(solution)/shard_map/pallas_call | solution.py:484
  33.0 0.1 collective-permute-done.3.other_ref
  33.1 8.4 %all_to_all.16.sums_ref = f32[16,8,128]{2,1,0:T(8,128)S(1)} all-to-all(f32[16,8,128]{2,1,0:T(8,128)S(1)} %shard_map.94), channel_id=1, replica_groups={{21,17,25,16,28,9,13,8,24,1,29,5,0,12,4,20},{23,19,27,18,30,11,15,10,26..., dimensions={0} | all-to-all | bytes 131072 | tf_op jit(solution)/shard_map/all_to_all | solution.py:33
  41.5 0.7 %shard_map.95 = f32[4,16,128]{2,1,0:T(8,128)} custom-call(f32[16,8,128]{2,1,0:T(8,128)S(1)} %all_to_all.16.sums_ref, f32[32,128]{1,0:T(8,128)S(1)} %shard_map.93.field_ref, f32[32,128]{1,0:T(8,128)S(1)} %collective-permute-done.3.other_ref, f32[4,16,128]{2,1,0:T(8,128)S(1)} %copy-done), custom_call_target="tpu_custom_call" | custom-call | tf_op jit(solution)/shard_map/pallas_call | solution.py:484
  (2 shorter events, 0.0 us)
Async XLA Ops:
  16.9 1.7 %copy-start = (f32[4,16,128]{2,1,0:T(8,128)S(1)}, f32[4,16,128]{2,1,0:T(8,128)}, u32[]{:S(2)}) copy-start(f32[4,16,128]{2,1,0:T(8,128)} %rhs_ref.5) | copy-start | bytes 98308
  16.9 1.7 %copy-start.1 = (f32[16,128]{1,0:T(8,128)S(1)}, f32[16,128]{1,0:T(8,128)}, u32[]{:S(2)}) copy-start(f32[16,128]{1,0:T(8,128)} %self_ref.3) | copy-start | bytes 24580
  16.9 1.6 %collective-permute-start = (bf16[8,128,128]{2,1,0:T(8,128)(2,1)S(1)}, bf16[8,128,128]{2,1,0:T(8,128)(2,1)S(1)}, u32[]{:S(2)}, u32[]{:S(2)}) collective-permute-start(bf16[8,128,128]{2,1,0:T(8,128)(2,1)S(1)} %slice.4.own_ref), channel_id=1, source_target_pairs={{0,1},{1,0},{2,3},{3,2},{4,5},{5,4},{6,7},{7,6},{8,9},{9,8},{10,11... | collective-permute-start | bytes 786440 | tf_op jit(solution)/shard_map/ppermute | solution.py:540
  17.0 9.6 %collective-permute-start.1 = (bf16[8,128,128]{2,1,0:T(8,128)(2,1)S(1)}, bf16[8,128,128]{2,1,0:T(8,128)(2,1)S(1)}, u32[]{:S(2)}, u32[]{:S(2)}) collective-permute-start(bf16[8,128,128]{2,1,0:T(8,128)(2,1)S(1)} %slice.4.own_ref), channel_id=1, source_target_pairs={{0,2},{2,0},{1,3},{3,1},{4,6},{6,4},{5,7},{7,5},{8,10},{10,8},{9,1... | collective-permute-start | bytes 786440 | tf_op jit(solution)/shard_map/ppermute | solution.py:541
  20.5 11.4 %all-to-all-start.1 = ((bf16[16,40,128]{2,1,0:T(8,128)(2,1)}), bf16[16,40,128]{2,1,0:T(8,128)(2,1)S(1)}, u32[]{:S(2)}, u32[]{:S(2)}) async-start(bf16[16,40,128]{2,1,0:T(8,128)(2,1)} %shard_map.92), calls=%async_computation.1 | async-start | bytes 327680 | tf_op jit(solution)/shard_map/all_to_all | solution.py:33
  26.6 5.3 %collective-permute-start.2 = (bf16[8,128,128]{2,1,0:T(8,128)(2,1)S(1)}, bf16[8,128,128]{2,1,0:T(8,128)(2,1)S(1)}, u32[]{:S(2)}, u32[]{:S(2)}) collective-permute-start(bf16[8,128,128]{2,1,0:T(8,128)(2,1)S(1)} %collective-permute-done.1.across_ref), channel_id=1, source_target_pairs={{0,1},{1,0},{2,3},{3,2},{4,5},{5,4},{6,7},{7,6},{8,9},{9,8},{10,11... | collective-permute-start | bytes 786440 | tf_op jit(solution)/shard_map/ppermute | solution.py:542
  31.9 1.2 %collective-permute-start.3 = (f32[32,128]{1,0:T(8,128)S(1)}, f32[32,128]{1,0:T(8,128)S(1)}, u32[]{:S(2)}, u32[]{:S(2)}) collective-permute-start(f32[32,128]{1,0:T(8,128)S(1)} %shard_map.93.field_ref), channel_id=1, source_target_pairs={{0,1},{1,0},{2,3},{3,2},{4,5},{5,4},{6,7},{7,6},{8,9},{9,8},{10,11... | collective-permute-start | bytes 49160 | tf_op jit(solution)/shard_map/ppermute | solution.py:550

commit v9 on v7

--- a/solution.py
+++ b/solution.py
@@ -415,14 +415,17 @@
     right = rhs_ref[pl.ds(core * width, width)].reshape(rows, panels)
     spots = lax.broadcasted_iota(jnp.int32, (8, panels), 0)
     lanes = lax.broadcasted_iota(jnp.int32, (8, panels), 1)
-    result = jnp.zeros((8, panels), FULL)
+    rows_of = [jnp.zeros((8, panels), FULL) for _ in range(width)]
     pairs = ((right, right), (right, field), (field, field), (right, last), (field, last), (last, last))
     for number, (one, two) in enumerate(pairs):
         product = one * two
         for rhs in range(width):
-            total = jnp.sum(product[rhs * boxes : (rhs + 1) * boxes])
-            mine = (spots == number) & (lanes // (panels // width) == rhs)
-            result = jnp.where(mine, total, result)
+            row = jnp.sum(product[rhs * boxes : (rhs + 1) * boxes], axis=0, keepdims=True)
+            rows_of[rhs] = jnp.where(spots == number, row, rows_of[rhs])
+    result = jnp.zeros((8, panels), FULL)
+    for rhs in range(width):
+        total = jnp.sum(rows_of[rhs], axis=1, keepdims=True)
+        result = jnp.where(lanes // (panels // width) == rhs, total, result)
 
     def put(target):
         out_ref[target] = result

time: 42.6 us -> 42.5 us (level)
  transfers between devices with their start and end apart: 5 -> 5, of which waited for: 1 -> 2; matrix products, arithmetic and copies ran while one was open for 0% -> 0% of each run, Pallas kernels for 8% -> 7%
where the time goes in v9:
time: 42.5 us; the launch traced here: 42.2 us
  blocking collectives  23.3 us (55%)
  starting transfers between devices  7.78 us (18%)
  Pallas kernels  5.77 us (14%)
  waiting for transfers between devices  5.3 us (12%)
    all_to_all x2, blocking collectives, exchange(): lax.all_to_all(value, axes, 0, 0, tiled=True, axis_index_groups=groups)  23.3 us
    all_to_all x1, starting transfers between devices, exchange(): lax.all_to_all(value, axes, 0, 0, tiled=True, axis_index_groups=groups)  6.08 us
    pallas_call x5, Pallas kernels, call(): pl.pallas_call(kernel, out_shape=outs, in_specs=[vmem] * held + [pl.Block...  5.77 us
    all_to_all x1, waiting for transfers between devices, exchange(): lax.all_to_all(value, axes, 0, 0, tiled=True, axis_index_groups=groups)  5.22 us
    ppermute x1, starting transfers between devices, per_device(): across = lax.ppermute(bands, 'side', swap)  1.56 us
  transfers between devices with their start and end apart: 5, of which 2 were waited for; matrix products, arithmetic and copies ran while one was open for 0% of the time, Pallas kernels for 7%

profile of v9, /device:TPU:0, one launch (start us, length us, event | category | flops | bytes accessed | tf_op | source)
XLA Modules:
  0.0 42.2 jit_solution(6333813690433127176)
XLA Ops:
  0.0 1.9 %shard_map.91 = (bf16[8,152,128]{2,1,0:T(8,128)(2,1)S(1)}, bf16[64,64]{1,0:T(8,128)(2,1)S(1)}, bf16[16,256,128]{2,1,0:T(8,128)(2,1)S(1)}, bf16[26,128,128]{2,1,0...) custom-call(f32[4,16,128]{2,1,0:T(8,128)} %rhs_ref.5, bf16[16,256,128]{2,1,0:T(8,128)(2,1)} %expand_hbm.1, ...), custom_call_target="tpu_custom_call" | custom-call | tf_op jit(solution)/shard_map/pallas_call | solution.py:490
  1.9 15.0 %all_to_all.15.own_ref = bf16[8,152,128]{2,1,0:T(8,128)(2,1)S(1)} all-to-all(bf16[8,152,128]{2,1,0:T(8,128)(2,1)S(1)} %get-tuple-element.13), channel_id=1, replica_groups={{20,28,0,16,24,12,4,8},{21,29,1,17,25,13,5,9},{22,30,2,18,26,14,6,10},{..., dimensions={0} | all-to-all | bytes 622592 | tf_op jit(solution)/shard_map/all_to_all | solution.py:33
  16.9 0.0 copy-start
  16.9 0.0 copy-start.1
  16.9 0.1 collective-permute-start
  17.0 1.6 %collective-permute-start.1 = (bf16[8,128,128]{2,1,0:T(8,128)(2,1)S(1)}, bf16[8,128,128]{2,1,0:T(8,128)(2,1)S(1)}, u32[]{:S(2)}, u32[]{:S(2)}) collective-permute-start(bf16[8,128,128]{2,1,0:T(8,128)(2,1)S(1)} %slice.4.own_ref), channel_id=1, source_target_pairs={{0,2},{2,0},{1,3},{3,1},{4,6},{6,4},{5,7},{7,5},{8,10},{10,8},{9,1... | collective-permute-start | bytes 786440 | tf_op jit(solution)/shard_map/ppermute | solution.py:547
  18.6 0.0 collective-permute-done.other_ref
  18.6 0.0 copy-done
  18.6 0.0 copy-done.1
  18.6 2.0 %shard_map.92 = bf16[16,40,128]{2,1,0:T(8,128)(2,1)} custom-call(bf16[8,152,128]{2,1,0:T(8,128)(2,1)S(1)} %all_to_all.15.own_ref, bf16[8,128,128]{2,1,0:T(8,128)(2,1)S(1)} %collective-permute-done.other_ref, f32[4,16,128]{2,1,0:T(8,128)S(1)} %copy-done, f32[16,128]{1,0:T(8,128)S(1)} %copy-done.1, bf16[26,128,128]{2,1,0:T(8,128)(2,1)S(1)} %get-tuple-element.14.near_ref, ...), custom_call_target="tpu_custom_call" | custom-call | tf_op jit(solution)/shard_map/pallas_call | solution.py:490
  20.6 6.1 %all-to-all-start.1 = ((bf16[16,40,128]{2,1,0:T(8,128)(2,1)}), bf16[16,40,128]{2,1,0:T(8,128)(2,1)S(1)}, u32[]{:S(2)}, u32[]{:S(2)}) async-start(bf16[16,40,128]{2,1,0:T(8,128)(2,1)} %shard_map.92), calls=%async_computation.1 | async-start | bytes 327680 | tf_op jit(solution)/shard_map/all_to_all | solution.py:33
  26.7 0.0 collective-permute-done.1.across_ref
  26.7 0.1 collective-permute-start.2
  26.8 5.2 %all-to-all-done.1.parts_ref = bf16[16,40,128]{2,1,0:T(8,128)(2,1)S(1)} async-done(((bf16[16,40,128]{2,1,0:T(8,128)(2,1)}), bf16[16,40,128]{2,1,0:T(8,128)(2,1)S(1)}, u32[]{:S(2)}, u32[]{:S(2)}) %all-to-all-start.1) | async-done | bytes 163872 | tf_op jit(solution)/shard_map/all_to_all | solution.py:33
  32.0 0.0 collective-permute-start.3
  32.0 0.0 collective-permute-done.2.corner_ref
  32.0 1.1 %shard_map.94 = f32[16,8,128]{2,1,0:T(8,128)S(1)} custom-call(bf16[8,128,128]{2,1,0:T(8,128)(2,1)S(1)} %slice.4.own_ref, bf16[8,128,128]{2,1,0:T(8,128)(2,1)S(1)} %collective-permute-done.other_ref, bf16[8,128,128]{2,1,0:T(8,128)(2,1)S(1)} %collective-permute-done.1.across_ref, bf16[8,128,128]{2,1,0:T(8,128)(2,1)S(1)} %collective-permute-done.2.corner_ref, ...), custom_call_target="tpu_custom_call" | custom-call | tf_op jit(solution)/shard_map/pallas_call | solution.py:490
  33.1 0.1 collective-permute-done.3.other_ref
  33.2 8.3 %all_to_all.16.sums_ref = f32[16,8,128]{2,1,0:T(8,128)S(1)} all-to-all(f32[16,8,128]{2,1,0:T(8,128)S(1)} %shard_map.94), channel_id=1, replica_groups={{21,17,25,16,28,9,13,8,24,1,29,5,0,12,4,20},{23,19,27,18,30,11,15,10,26..., dimensions={0} | all-to-all | bytes 131072 | tf_op jit(solution)/shard_map/all_to_all | solution.py:33
  41.5 0.7 %shard_map.95 = f32[4,16,128]{2,1,0:T(8,128)} custom-call(f32[16,8,128]{2,1,0:T(8,128)S(1)} %all_to_all.16.sums_ref, f32[32,128]{1,0:T(8,128)S(1)} %shard_map.93.field_ref, f32[32,128]{1,0:T(8,128)S(1)} %collective-permute-done.3.other_ref, f32[4,16,128]{2,1,0:T(8,128)S(1)} %copy-done), custom_call_target="tpu_custom_call" | custom-call | tf_op jit(solution)/shard_map/pallas_call | solution.py:490
  (2 shorter events, 0.0 us)
Async XLA Ops:
  16.9 1.7 %copy-start = (f32[4,16,128]{2,1,0:T(8,128)S(1)}, f32[4,16,128]{2,1,0:T(8,128)}, u32[]{:S(2)}) copy-start(f32[4,16,128]{2,1,0:T(8,128)} %rhs_ref.5) | copy-start | bytes 98308
  16.9 1.7 %copy-start.1 = (f32[16,128]{1,0:T(8,128)S(1)}, f32[16,128]{1,0:T(8,128)}, u32[]{:S(2)}) copy-start(f32[16,128]{1,0:T(8,128)} %self_ref.3) | copy-start | bytes 24580
  16.9 1.6 %collective-permute-start = (bf16[8,128,128]{2,1,0:T(8,128)(2,1)S(1)}, bf16[8,128,128]{2,1,0:T(8,128)(2,1)S(1)}, u32[]{:S(2)}, u32[]{:S(2)}) collective-permute-start(bf16[8,128,128]{2,1,0:T(8,128)(2,1)S(1)} %slice.4.own_ref), channel_id=1, source_target_pairs={{0,1},{1,0},{2,3},{3,2},{4,5},{5,4},{6,7},{7,6},{8,9},{9,8},{10,11... | collective-permute-start | bytes 786440 | tf_op jit(solution)/shard_map/ppermute | solution.py:546
  17.0 9.7 %collective-permute-start.1 = (bf16[8,128,128]{2,1,0:T(8,128)(2,1)S(1)}, bf16[8,128,128]{2,1,0:T(8,128)(2,1)S(1)}, u32[]{:S(2)}, u32[]{:S(2)}) collective-permute-start(bf16[8,128,128]{2,1,0:T(8,128)(2,1)S(1)} %slice.4.own_ref), channel_id=1, source_target_pairs={{0,2},{2,0},{1,3},{3,1},{4,6},{6,4},{5,7},{7,5},{8,10},{10,8},{9,1... | collective-permute-start | bytes 786440 | tf_op jit(solution)/shard_map/ppermute | solution.py:547
  20.6 11.4 %all-to-all-start.1 = ((bf16[16,40,128]{2,1,0:T(8,128)(2,1)}), bf16[16,40,128]{2,1,0:T(8,128)(2,1)S(1)}, u32[]{:S(2)}, u32[]{:S(2)}) async-start(bf16[16,40,128]{2,1,0:T(8,128)(2,1)} %shard_map.92), calls=%async_computation.1 | async-start | bytes 327680 | tf_op jit(solution)/shard_map/all_to_all | solution.py:33
  26.7 5.3 %collective-permute-start.2 = (bf16[8,128,128]{2,1,0:T(8,128)(2,1)S(1)}, bf16[8,128,128]{2,1,0:T(8,128)(2,1)S(1)}, u32[]{:S(2)}, u32[]{:S(2)}) collective-permute-start(bf16[8,128,128]{2,1,0:T(8,128)(2,1)S(1)} %collective-permute-done.1.across_ref), channel_id=1, source_target_pairs={{0,1},{1,0},{2,3},{3,2},{4,5},{5,4},{6,7},{7,6},{8,9},{9,8},{10,11... | collective-permute-start | bytes 786440 | tf_op jit(solution)/shard_map/ppermute | solution.py:548
  32.0 1.2 %collective-permute-start.3 = (f32[32,128]{1,0:T(8,128)S(1)}, f32[32,128]{1,0:T(8,128)S(1)}, u32[]{:S(2)}, u32[]{:S(2)}) collective-permute-start(f32[32,128]{1,0:T(8,128)S(1)} %shard_map.93.field_ref), channel_id=1, source_target_pairs={{0,1},{1,0},{2,3},{3,2},{4,5},{5,4},{6,7},{7,6},{8,9},{9,8},{10,11... | collective-permute-start | bytes 49160 | tf_op jit(solution)/shard_map/ppermute | solution.py:556
